TPU v7x, 32 devices: a whole 2x2x4 slice. The times are simulated.
32 devices in a mesh: ctx: 8 (over y, x, core), wt: 4 (over z).
Axes of the slice: x: 2, y: 2, z: 4, core: 2. Of those that a mesh axis runs over, the one named last changes fastest.
Arguments:
- hidden_in: bfloat16 [4, 1280, 896], P('wt', 'ctx'), may hold values from -6 to 6
- positions: int32 [4, 1280], P('wt', 'ctx'), may hold values from 0 to 1279, as said below
- cotangent: bfloat16 [4, 1280, 896], P('wt', 'ctx'), may hold values from -6 to 6
- attn_gain: bfloat16 [2, 896], P(None, ('ctx', 'wt')), may hold values from 0.5 to 1.5
- qkv_weight: bfloat16 [2, 896, 1152], P(None, ('ctx', 'wt')), may hold values from -0.25 to 0.25
- qkv_bias: bfloat16 [2, 1152], P(None, ('ctx', 'wt')), may hold values from -3 to 3
- out_weight: bfloat16 [2, 896, 896], P(None, ('ctx', 'wt')), may hold values from -1 to 1
- mlp_gain: bfloat16 [2, 896], P(None, ('ctx', 'wt')), may hold values from 0.5 to 1.5
- in_weight: bfloat16 [2, 896, 9728], P(None, ('ctx', 'wt')), may hold values from -0.1875 to 0.1875
- down_weight: bfloat16 [2, 4864, 896], P(None, ('ctx', 'wt')), may hold values from -0.15625 to 0.15625
Outputs:
- hidden_out: float32 [4, 1280, 896], P('wt', 'ctx')
- input_grad: float32 [4, 1280, 896], P('wt', 'ctx')
- attn_gain_grad: float32 [2, 896], P(None, ('ctx', 'wt'))
- qkv_weight_grad: float32 [2, 896, 1152], P(None, ('ctx', 'wt'))
- qkv_bias_grad: float32 [2, 1152], P(None, ('ctx', 'wt'))
- out_weight_grad: float32 [2, 896, 896], P(None, ('ctx', 'wt'))
- mlp_gain_grad: float32 [2, 896], P(None, ('ctx', 'wt'))
- in_weight_grad: float32 [2, 896, 9728], P(None, ('ctx', 'wt'))
- down_weight_grad: float32 [2, 4864, 896], P(None, ('ctx', 'wt'))
Inputs may be any that keep to these rules, and one draw needn't show every extreme that they name: Each row of positions holds every value of 0 to 1279 once, as 16 runs of 80 consecutive ascending values, each run starting at a multiple of 80 and at a column that is a multiple of 80; the order of the runs differs from row to row.
All inputs are finite; a program needn't handle non-finite values.
Results may differ from a plain program's by a relative error of at most 0.025.
Values may be sent and summed in bfloat16 or wider, within the bound.
No kernel may reach another device: no remote copies, remote signals or barrier semaphores. Data moves between devices by JAX's collectives and lax.ppermute only.
A program may use at most 448 MiB of HBM per device.

v0:
```python
import math

import jax
import jax.numpy as jnp
from jax import lax
from jax.sharding import PartitionSpec as P

HEADS = 14
KV_HEADS = 2
HEAD = 64
FF = 4864
LAYERS = 2
QW = 896


EPSILON = 1e-06
ROPE_BASE = 1000000.0
NEGATIVE = -1e30


def norm_rows(hidden, norm_gain):
    return (
        hidden * lax.rsqrt(jnp.mean(hidden * hidden, axis=-1, keepdims=True) + EPSILON) * norm_gain
    )


def rope_tables(own_positions):
    half_head = HEAD // 2
    frequency = jnp.exp(
        jnp.arange(half_head, dtype=jnp.float32) * (-2.0 * math.log(ROPE_BASE) / HEAD)
    )
    angles = own_positions.astype(jnp.float32)[:, None] * frequency[None, :]
    cos_half = jnp.cos(angles)
    sin_half = jnp.sin(angles)
    return (
        jnp.concatenate([cos_half, cos_half], axis=-1),
        jnp.concatenate([sin_half, sin_half], axis=-1),
    )


def rotate(tensor, cos_table, sin_table):
    half_head = HEAD // 2
    turned = jnp.concatenate([-tensor[..., half_head:], tensor[..., :half_head]], axis=-1)
    return tensor * cos_table[:, None, :] + turned * sin_table[:, None, :]


def contract_rows(left, right):
    return lax.dot_general(
        left, right, (((0,), (0,)), ((), ())), preferred_element_type=jnp.float32
    )


def contract_cols(left, right):
    return lax.dot_general(
        left, right, (((1,), (1,)), ((), ())), preferred_element_type=jnp.float32
    )


def gated_unit(gate_up):
    return jax.nn.silu(gate_up[:, :FF]) * gate_up[:, FF:]


def refetch_layer(
    layer_idx, attn_gain, qkv_weight, qkv_bias, out_weight, mlp_gain, in_weight, down_weight
):
    gathered = (
        lax.all_gather(attn_gain[layer_idx], ("ctx", "wt"), axis=0, tiled=True),
        lax.all_gather(qkv_weight[layer_idx], ("ctx", "wt"), axis=0, tiled=True),
        lax.all_gather(qkv_bias[layer_idx], ("ctx", "wt"), axis=0, tiled=True),
        lax.all_gather(out_weight[layer_idx], ("ctx", "wt"), axis=0, tiled=True),
        lax.all_gather(mlp_gain[layer_idx], ("ctx", "wt"), axis=0, tiled=True),
        lax.all_gather(in_weight[layer_idx], ("ctx", "wt"), axis=0, tiled=True),
        lax.all_gather(down_weight[layer_idx], ("ctx", "wt"), axis=0, tiled=True),
    )
    return (tuple(gathered[:4]), tuple(gathered[4:]))


def grouped_scores(queries, all_keys, own_positions, all_positions):
    row_count = queries.shape[0]
    grouped = queries.reshape(row_count, KV_HEADS, HEADS // KV_HEADS, HEAD)
    scores = jnp.einsum(
        "tkgd,skd->tkgs", grouped, all_keys, preferred_element_type=jnp.float32
    ) * HEAD ** (-0.5)
    allowed = all_positions[None, :] <= own_positions[:, None]
    return (grouped, jnp.where(allowed[:, None, None, :], scores, NEGATIVE))


def attention_forward(hidden, params, cos_table, sin_table, own_positions, all_positions):
    norm_gain, joint_proj, joint_bias, out_proj = params
    row_count = hidden.shape[0]
    kv_cols = KV_HEADS * HEAD
    normed = norm_rows(hidden, norm_gain.astype(jnp.float32)).astype(jnp.bfloat16)
    packed = jnp.dot(normed, joint_proj, preferred_element_type=jnp.float32) + joint_bias.astype(
        jnp.float32
    )
    queries = rotate(packed[:, :QW].reshape(row_count, HEADS, HEAD), cos_table, sin_table).astype(
        jnp.bfloat16
    )
    own_keys = rotate(
        packed[:, QW : QW + kv_cols].reshape(row_count, KV_HEADS, HEAD), cos_table, sin_table
    ).astype(jnp.bfloat16)
    own_values = packed[:, QW + kv_cols :].reshape(row_count, KV_HEADS, HEAD).astype(jnp.bfloat16)
    all_keys, all_values = (
        lax.all_gather(own_keys, "ctx", axis=0, tiled=True),
        lax.all_gather(own_values, "ctx", axis=0, tiled=True),
    )
    grouped, scores = grouped_scores(queries, all_keys, own_positions, all_positions)
    row_max = jnp.max(scores, axis=-1, keepdims=True)
    exponent = jnp.exp(scores - row_max)
    row_sum = jnp.sum(exponent, axis=-1, keepdims=True)
    attn_probs = (exponent / row_sum).astype(jnp.bfloat16)
    head_mix = jnp.einsum(
        "tkgs,skd->tkgd", attn_probs, all_values, preferred_element_type=jnp.float32
    )
    heads_out = head_mix.reshape(row_count, QW).astype(jnp.bfloat16)
    middle = hidden + jnp.dot(heads_out, out_proj, preferred_element_type=jnp.float32)
    stored = (
        normed,
        queries,
        own_keys,
        own_values,
        all_keys,
        all_values,
        row_max,
        row_sum,
        heads_out,
    )
    return (middle, stored)


def mlp_forward(middle, params):
    norm_gain, in_proj, down_proj = params
    normed2 = norm_rows(middle, norm_gain.astype(jnp.float32)).astype(jnp.bfloat16)
    gate_up = jnp.dot(normed2, in_proj, preferred_element_type=jnp.float32)
    activated = gated_unit(gate_up).astype(jnp.bfloat16)
    after = middle + jnp.dot(activated, down_proj, preferred_element_type=jnp.float32)
    return (after, (normed2, gate_up, activated))


def mlp_weight_sums(normed2, gate_up_grad, activated, grad_low):
    in_part = lax.psum_scatter(
        contract_rows(normed2, gate_up_grad), ("ctx", "wt"), scatter_dimension=0, tiled=True
    )
    down_part = lax.psum_scatter(
        contract_rows(activated, grad_low), ("ctx", "wt"), scatter_dimension=0, tiled=True
    )
    return (in_part, down_part)


def mlp_backward(gradient, middle, stored, params):
    norm_gain, in_proj, down_proj = params
    normed2, gate_up, activated = stored
    grad_low = gradient.astype(jnp.bfloat16)
    act_grad = contract_cols(grad_low, down_proj)
    unused, unit_back = jax.vjp(gated_unit, gate_up)
    gate_up_grad = unit_back(act_grad)[0].astype(jnp.bfloat16)
    normed_grad = contract_cols(gate_up_grad, in_proj)
    unused, norm_back = jax.vjp(norm_rows, middle, norm_gain.astype(jnp.float32))
    middle_part, gain_grad = norm_back(normed_grad)
    weight_parts = mlp_weight_sums(normed2, gate_up_grad, activated, grad_low)
    return (gradient + middle_part, gain_grad, weight_parts)


def attention_backward(
    gradient,
    hidden,
    stored,
    params,
    all_keys,
    all_values,
    cos_table,
    sin_table,
    own_positions,
    all_positions,
    mlp_gain_term,
):
    norm_gain, joint_proj, joint_bias, out_proj = params
    normed, queries, own_keys, own_values, kept_keys, kept_values, row_max, row_sum, heads_out = (
        stored
    )
    row_count = gradient.shape[0]
    score_scale = HEAD ** (-0.5)
    grad_low = gradient.astype(jnp.bfloat16)
    out_grad = contract_rows(heads_out, grad_low)
    heads_grad = contract_cols(grad_low, out_proj).astype(jnp.bfloat16)
    heads_grad = heads_grad.reshape(row_count, KV_HEADS, HEADS // KV_HEADS, HEAD)
    grouped, scores = grouped_scores(queries, all_keys, own_positions, all_positions)
    attn_probs = jnp.exp(scores - row_max) / row_sum
    prob_grad = jnp.einsum(
        "tkgd,skd->tkgs", heads_grad, all_values, preferred_element_type=jnp.float32
    )
    row_inner = jnp.sum(attn_probs * prob_grad, axis=-1, keepdims=True)
    score_grad = (attn_probs * (prob_grad - row_inner)).astype(jnp.bfloat16)
    query_grad = jnp.einsum(
        "tkgs,skd->tkgd", score_grad, all_keys, preferred_element_type=jnp.float32
    )
    query_grad = query_grad.reshape(row_count, HEADS, HEAD) * score_scale
    key_terms = (
        jnp.einsum("tkgs,tkgd->skd", score_grad, grouped, preferred_element_type=jnp.float32)
        * score_scale
    )
    value_terms = jnp.einsum(
        "tkgs,tkgd->skd",
        attn_probs.astype(jnp.bfloat16),
        heads_grad,
        preferred_element_type=jnp.float32,
    )
    key_grad, value_grad = (
        lax.psum_scatter(
            key_terms.astype(jnp.bfloat16), "ctx", scatter_dimension=0, tiled=True
        ).astype(jnp.float32),
        lax.psum_scatter(
            value_terms.astype(jnp.bfloat16), "ctx", scatter_dimension=0, tiled=True
        ).astype(jnp.float32),
    )

    def turn(tensor):
        return rotate(tensor, cos_table, sin_table)

    unused, query_back = jax.vjp(turn, query_grad)
    unused, key_back = jax.vjp(turn, key_grad)
    packed_grad = jnp.concatenate(
        [
            query_back(query_grad)[0].reshape(row_count, QW),
            key_back(key_grad)[0].reshape(row_count, KV_HEADS * HEAD),
            value_grad.reshape(row_count, KV_HEADS * HEAD),
        ],
        axis=1,
    ).astype(jnp.bfloat16)
    bias_grad = jnp.sum(packed_grad, axis=0, dtype=jnp.float32)
    joint_grad = contract_rows(normed, packed_grad)
    normed_grad = contract_cols(packed_grad, joint_proj)
    unused, norm_back = jax.vjp(norm_rows, hidden, norm_gain.astype(jnp.float32))
    hidden_part, gain_grad = norm_back(normed_grad)
    summed = (
        lax.psum_scatter(gain_grad, ("ctx", "wt"), scatter_dimension=0, tiled=True),
        lax.psum_scatter(joint_grad, ("ctx", "wt"), scatter_dimension=0, tiled=True),
        lax.psum_scatter(bias_grad, ("ctx", "wt"), scatter_dimension=0, tiled=True),
        lax.psum_scatter(out_grad, ("ctx", "wt"), scatter_dimension=0, tiled=True),
        lax.psum_scatter(mlp_gain_term, ("ctx", "wt"), scatter_dimension=0, tiled=True),
    )
    return (gradient + hidden_part, summed)


def body(
    hidden_in,
    positions,
    cotangent,
    attn_gain,
    qkv_weight,
    qkv_bias,
    out_weight,
    mlp_gain,
    in_weight,
    down_weight,
):
    own_positions = positions[0]
    all_positions = lax.all_gather(own_positions, "ctx", axis=0, tiled=True)
    cos_table, sin_table = rope_tables(own_positions)
    hidden = hidden_in[0].astype(jnp.float32)
    stored_layers = []
    for layer_idx in range(LAYERS):
        attn_params = (
            lax.all_gather(attn_gain[layer_idx], ("ctx", "wt"), axis=0, tiled=True),
            lax.all_gather(qkv_weight[layer_idx], ("ctx", "wt"), axis=0, tiled=True),
            lax.all_gather(qkv_bias[layer_idx], ("ctx", "wt"), axis=0, tiled=True),
            lax.all_gather(out_weight[layer_idx], ("ctx", "wt"), axis=0, tiled=True),
        )
        middle, attn_stored = attention_forward(
            hidden, attn_params, cos_table, sin_table, own_positions, all_positions
        )
        mlp_params = (
            lax.all_gather(mlp_gain[layer_idx], ("ctx", "wt"), axis=0, tiled=True),
            lax.all_gather(in_weight[layer_idx], ("ctx", "wt"), axis=0, tiled=True),
            lax.all_gather(down_weight[layer_idx], ("ctx", "wt"), axis=0, tiled=True),
        )
        after, mlp_stored = mlp_forward(middle, mlp_params)
        stored_layers.append((hidden, attn_stored, middle, mlp_stored))
        hidden = after
    gradient = cotangent[0].astype(jnp.float32)
    attn_sums = []
    mlp_sums = []
    for layer_idx in reversed(range(LAYERS)):
        layer_input, attn_stored, middle, mlp_stored = stored_layers[layer_idx]
        attn_params, mlp_params = refetch_layer(
            layer_idx, attn_gain, qkv_weight, qkv_bias, out_weight, mlp_gain, in_weight, down_weight
        )
        gradient, mlp_gain_term, mlp_part = mlp_backward(gradient, middle, mlp_stored, mlp_params)
        all_keys, all_values = (
            lax.all_gather(attn_stored[2], "ctx", axis=0, tiled=True),
            lax.all_gather(attn_stored[3], "ctx", axis=0, tiled=True),
        )
        gradient, attn_part = attention_backward(
            gradient,
            layer_input,
            attn_stored,
            attn_params,
            all_keys,
            all_values,
            cos_table,
            sin_table,
            own_positions,
            all_positions,
            mlp_gain_term,
        )
        attn_sums.insert(0, attn_part)
        mlp_sums.insert(0, mlp_part)
    attn_gain_grad = jnp.stack([part[0] for part in attn_sums])
    qkv_weight_grad = jnp.stack([part[1] for part in attn_sums])
    qkv_bias_grad = jnp.stack([part[2] for part in attn_sums])
    out_weight_grad = jnp.stack([part[3] for part in attn_sums])
    mlp_gain_grad = jnp.stack([part[4] for part in attn_sums])
    in_weight_grad = jnp.stack([part[0] for part in mlp_sums])
    down_weight_grad = jnp.stack([part[1] for part in mlp_sums])
    return (
        hidden[None],
        gradient[None],
        attn_gain_grad,
        qkv_weight_grad,
        qkv_bias_grad,
        out_weight_grad,
        mlp_gain_grad,
        in_weight_grad,
        down_weight_grad,
    )


def solution(mesh):
    return jax.shard_map(
        body,
        mesh=mesh,
        in_specs=(
            P("wt", "ctx", None),
            P("wt", "ctx"),
            P("wt", "ctx", None),
            P(None, ("ctx", "wt")),
            P(None, ("ctx", "wt"), None),
            P(None, ("ctx", "wt")),
            P(None, ("ctx", "wt"), None),
            P(None, ("ctx", "wt")),
            P(None, ("ctx", "wt"), None),
            P(None, ("ctx", "wt"), None),
        ),
        out_specs=(
            P("wt", "ctx", None),
            P("wt", "ctx", None),
            P(None, ("ctx", "wt")),
            P(None, ("ctx", "wt"), None),
            P(None, ("ctx", "wt")),
            P(None, ("ctx", "wt"), None),
            P(None, ("ctx", "wt")),
            P(None, ("ctx", "wt"), None),
            P(None, ("ctx", "wt"), None),
        ),
        check_vma=False,
    )
```

profile of v0, /device:TPU:0, one launch (start us, length us, event | category | flops | bytes accessed | tf_op | source)
XLA Modules:
  0.0 4245.0 jit_solution(10865158804180908757)
XLA Ops:
  11.2 4.4 fusion.189
  20.8 42.5 %all-reduce.40 = (bf16[1152]{0:T(1024)(128)(2,1)S(1)}, bf16[896]{0:T(1024)(128)(2,1)S(1)}, bf16[896]{0:T(1024)(128)(2,1)S(1)}, bf16[1152]{0:T(1024)(128)(2,1)S(1...) all-reduce(bf16[1152]{0:T(1024)(128)(2,1)S(1)} %dynamic-update-slic, ...), channel_id=4, replica_groups=mesh['ctx'=8,'wt'=4] {'ctx','wt'}, use_global_device_ids=true, to_apply=%add.13 | all-reduce | flops 5888 | bytes 23552
  65.4 8.3 all-reduce.14
  79.5 9.9 all_gather.78
  90.8 10.1 all_gather.76
  102.8 9.3 fusion.197
  112.0 4.7 fusion.90
  116.8 19.7 all-gather.26.cloned.1.call-done
  139.1 200.9 %all-gather.28.cloned.1.call-done = bf16[1,896,9728]{2,0,1:T(2,128)(2,1)} async-done(((bf16[1,28,9728]{2,0,1:T(2,128)(2,1)}), bf16[1,896,9728]{2,0,1:T(2,128)(2,1)}) %all-gather.28.cloned.1.call-update) | async-done | bytes 17432592 | tf_op jit(solution)/shard_map/all_gather | solution.py:274
  340.0 17.4 fusion.14
  361.1 59.2 %all-gather.30.cloned.1.call-done = bf16[1,4864,896]{2,1,0:T(8,128)(2,1)} async-done(((bf16[1,152,896]{2,1,0:T(8,128)(2,1)}), bf16[1,4864,896]{2,1,0:T(8,128)(2,1)}) %all-gather.30.cloned.1.call-update) | async-done | bytes 8716304 | tf_op jit(solution)/shard_map/all_gather | solution.py:275
  420.2 5.4 multiply_reduce_fusion.7
  425.7 58.3 %all-gather.32.cloned.1.call-done = bf16[1,896,1152]{2,0,1:T(2,128)(2,1)} async-done(((bf16[1,28,1152]{2,0,1:T(2,128)(2,1)}), bf16[1,896,1152]{2,0,1:T(2,128)(2,1)}) %all-gather.32.cloned.1.call-update) | async-done | bytes 2064400 | tf_op jit(solution)/shard_map/all_gather | solution.py:265
  487.4 10.2 all_gather.87
  499.0 9.8 all_gather.86
  510.2 9.2 fusion.198
  519.4 4.7 fusion.93
  524.1 20.5 all-gather.34.cloned.1.call-done
  547.2 200.9 %all-gather.36.cloned.1.call-done = bf16[1,896,9728]{2,0,1:T(2,128)(2,1)} async-done(((bf16[1,28,9728]{2,0,1:T(2,128)(2,1)}), bf16[1,896,9728]{2,0,1:T(2,128)(2,1)}) %all-gather.36.cloned.1.call-update) | async-done | bytes 17432592 | tf_op jit(solution)/shard_map/all_gather | solution.py:274
  748.1 17.4 fusion.10
  765.5 62.9 %all-gather.38.cloned.1.call-done = bf16[1,4864,896]{2,1,0:T(8,128)(2,1)} async-done(((bf16[1,152,896]{2,1,0:T(8,128)(2,1)}), bf16[1,4864,896]{2,1,0:T(8,128)(2,1)}) %all-gather.38.cloned.1.call-update) | async-done | bytes 8716304 | tf_op jit(solution)/shard_map/all_gather | solution.py:275
  828.4 9.7 fusion.149
  838.1 20.9 multiply_reduce_fusion
  864.0 6.0 fusion.19
  879.1 6.5 fusion.66
  892.9 27.1 reduce-scatter.33.cloned.1.call-done
  921.0 35.7 reduce-scatter.35.cloned.1.call-done
  957.6 3.9 multiply_reduce_fusion.2
  961.8 11.1 fusion.148
  972.9 19.6 multiply_reduce_fusion.1
  996.4 6.5 fusion.16
  1010.9 6.2 fusion.69
  1019.1 7.6 fusion.150
  1027.7 19.3 fusion.146
  1047.0 7.5 fusion.156
  1054.6 1568.5 %fusion.5 = f32[32,9728]{1,0:T(8,128)S(1)} fusion(f32[896,9728]{1,0:T(8,128)} %fusion.146), kind=kCustom, calls=%all-reduce-scatter.5 | all-reduce-scatter fusion | flops 9961473 | bytes 36110336
  2627.2 6.3 fusion.108
  2633.4 18.2 fusion.147
  2651.6 835.4 %fusion.4 = f32[32,9728]{1,0:T(8,128)} fusion(f32[896,9728]{1,0:T(8,128)} %fusion.147), kind=kCustom, calls=%all-reduce-scatter.4 | all-reduce-scatter fusion | flops 9961473 | bytes 36110336
  3490.9 4.6 fusion.200
  3507.4 4.0 fusion.172
  3511.5 358.9 %fusion.188 = (f32[32,1152]{1,0:T(8,128)}, f32[32,1152]{1,0:T(8,128)}, f32[32,896]{1,0:T(8,128)}, f32[32,896]{1,0:T(8,128)}) fusion(f32[896,1152]{1,0:T(8,128)} %fusion.187, f32[896,1152]{1,0:T(8,128)} %fusion.172, f32[896,896]{1,0:T(8,128)S(1)} %fusion.159, f32[896,896]{1,0:T(8,128)} %fusion.153), kind=kCustom, calls=%all-reduce-scatter.6 | all-reduce-scatter fusion | flops 4194305 | bytes 15204352
  3879.3 12.7 collective-permute-start.12
  3892.0 3.8 collective-permute-start.11
  3897.2 4.2 fusion.138
  3901.4 43.0 %all-reduce.39 = (f32[896]{0:T(1024)}, f32[896]{0:T(1024)}, f32[1152]{0:T(1024)}, f32[1152]{0:T(1024)S(1)}, f32[896]{0:T(1024)}, /*index=5*/f32[896]{0:T(1024)}) all-reduce(f32[896]{0:T(1024)S(1)} %copy-done.89, f32[896]{0:T(1024)S(1)} %get-tuple-element.51, ...), channel_id=22, replica_groups=mesh['ctx'=8,'wt'=4] {'ctx','wt'}, use_global_device_ids=true, to_apply=%region_21.22.clone | all-reduce | flops 5888 | bytes 47104
  3954.4 6.6 collective-permute-start.14
  3961.1 3.8 collective-permute-start.3
  3970.1 4.2 collective-permute-start.20
  3974.3 5.2 collective-permute-start.1
  3990.4 12.3 collective-permute-done.1
  4002.7 12.1 collective-permute-start.21
  4014.8 5.7 collective-permute-start.22
  4021.3 4.4 collective-permute-start.5
  4026.2 7.9 concatenate.50
  4034.1 7.0 concatenate.51
  4042.0 29.1 collective-permute-done.5
  4071.2 36.8 collective-permute-start.6
  4109.7 7.1 concatenate.48
  4120.1 7.1 concatenate.49
  4131.5 4.9 collective-permute-start.18
  4139.6 31.5 concatenate.53
  4173.2 26.7 collective-permute-done.18
  4199.8 31.5 concatenate.52
  (411 shorter events, 151.8 us)
Async XLA Ops:
  7.2 68.8 %all-gather.24.cloned.1.call-start = ((), (), s32[]{:S(2)}) async-start(), calls=%async_computation.6 | async-start | bytes 4257792 | tf_op jit(solution)/shard_map/all_gather | solution.py:265
  9.2 127.3 %all-gather.26.cloned.1.call-start = ((), (), s32[]{:S(2)}) async-start(), calls=%async_computation.7 | async-start | bytes 3311616 | tf_op jit(solution)/shard_map/all_gather | solution.py:267
  11.2 62.8 %copy-start.28 = (bf16[1,160,896]{2,1,0:T(8,128)(2,1)S(1)}, bf16[1,160,896]{2,1,0:T(8,128)(2,1)}, u32[]{:S(2)}) copy-start(bf16[1,160,896]{2,1,0:T(8,128)(2,1)} %param.10) | copy-start | bytes 860164
  11.2 328.8 %all-gather.28.cloned.1.call-start = ((), (), s32[]{:S(2)}) async-start(), calls=%async_computation.8 | async-start | bytes 35954688 | tf_op jit(solution)/shard_map/all_gather | solution.py:274
  15.7 404.5 %all-gather.30.cloned.1.call-start = ((), (), s32[]{:S(2)}) async-start(), calls=%async_computation.9 | async-start | bytes 8988672 | tf_op jit(solution)/shard_map/all_gather | solution.py:275
  16.6 467.3 %all-gather.32.cloned.1.call-start = ((), (), s32[]{:S(2)}) async-start(), calls=%async_computation.10 | async-start | bytes 4257792 | tf_op jit(solution)/shard_map/all_gather | solution.py:265
  17.2 527.4 %all-gather.34.cloned.1.call-start = ((), (), s32[]{:S(2)}) async-start(), calls=%async_computation.11 | async-start | bytes 3311616 | tf_op jit(solution)/shard_map/all_gather | solution.py:267
  17.8 730.3 %all-gather.36.cloned.1.call-start = ((), (), s32[]{:S(2)}) async-start(), calls=%async_computation.12 | async-start | bytes 35954688 | tf_op jit(solution)/shard_map/all_gather | solution.py:274
  18.5 809.8 %all-gather.38.cloned.1.call-start = ((), (), s32[]{:S(2)}) async-start(), calls=%async_computation.13 | async-start | bytes 8988672 | tf_op jit(solution)/shard_map/all_gather | solution.py:275
  19.3 900.7 %reduce-scatter.33.cloned.1.call-start = ((), (), s32[]{:S(2)}) async-start(), calls=%async_computation.14 | async-start | bytes 368640
  74.0 815.5 %copy-start.50 = (f32[160,64]{0,1:T(8,128)}, f32[160,64]{0,1:T(8,128)S(1)}, u32[]{:S(2)}) copy-start(f32[160,64]{0,1:T(8,128)S(1)} %get-tuple-element.104) | copy-start | bytes 122884
  74.0 816.7 %copy-start.48 = (f32[160,64]{0,1:T(8,128)}, f32[160,64]{0,1:T(8,128)S(1)}, u32[]{:S(2)}) copy-start(f32[160,64]{0,1:T(8,128)S(1)} %get-tuple-element.133) | copy-start | bytes 122884
  74.0 846.9 %copy-start.31 = (f32[160,64]{0,1:T(8,128)}, f32[160,64]{0,1:T(8,128)S(1)}, u32[]{:S(2)}) copy-start(f32[160,64]{0,1:T(8,128)S(1)} %get-tuple-element.105) | copy-start | bytes 122884
  74.0 846.9 %copy-start.30 = (f32[160,64]{0,1:T(8,128)}, f32[160,64]{0,1:T(8,128)S(1)}, u32[]{:S(2)}) copy-start(f32[160,64]{0,1:T(8,128)S(1)} %get-tuple-element.132) | copy-start | bytes 122884
  116.8 223.2 %copy-start.53 = (bf16[2,64,160,7]{2,1,3,0:T(8,128)(2,1)}, bf16[2,64,160,7]{2,1,3,0:T(8,128)(2,1)S(1)}, u32[]{:S(2)}) copy-start(bf16[2,64,160,7]{2,1,3,0:T(8,128)(2,1)S(1)} %fusion.90) | copy-start | bytes 860164
  139.0 218.3 %copy-start.86 = (f32[160]{0:T(256)}, f32[160]{0:T(256)S(1)}, u32[]{:S(2)}) copy-start(f32[160]{0:T(256)S(1)} %get-tuple-element.116) | copy-start | bytes 1924
  139.1 281.2 %copy-start.13 = (f32[160,896]{1,0:T(8,128)}, f32[160,896]{1,0:T(8,128)S(1)}, u32[]{:S(2)}) copy-start(f32[160,896]{1,0:T(8,128)S(1)} %get-tuple-element.117) | copy-start | bytes 1720324
  361.1 64.6 %copy-start.1 = (bf16[160,4864]{1,0:T(8,128)(2,1)}, bf16[160,4864]{1,0:T(8,128)(2,1)S(1)}, u32[]{:S(2)}) copy-start(bf16[160,4864]{1,0:T(8,128)(2,1)S(1)} %multiply_convert_fusion.1) | copy-start | bytes 4669444
  361.1 122.9 %copy-start.85 = (f32[1152]{0:T(1024)S(1)}, f32[1152]{0:T(1024)}, u32[]{:S(2)}) copy-start(f32[1152]{0:T(1024)} %convert_element_type.234) | copy-start | bytes 13828
  425.6 535.9 %copy-start.8 = (f32[160,896]{1,0:T(8,128)}, f32[160,896]{1,0:T(8,128)S(1)}, u32[]{:S(2)}) copy-start(f32[160,896]{1,0:T(8,128)S(1)} %get-tuple-element.119) | copy-start | bytes 1720324
  524.1 241.4 %copy-start.55 = (bf16[2,64,160,7]{2,1,3,0:T(8,128)(2,1)}, bf16[2,64,160,7]{2,1,3,0:T(8,128)(2,1)S(1)}, u32[]{:S(2)}) copy-start(bf16[2,64,160,7]{2,1,3,0:T(8,128)(2,1)S(1)} %fusion.93) | copy-start | bytes 860164
  547.1 311.9 %copy-start.10 = (f32[160,896]{1,0:T(8,128)}, f32[160,896]{1,0:T(8,128)S(1)}, u32[]{:S(2)}) copy-start(f32[160,896]{1,0:T(8,128)S(1)} %get-tuple-element.123) | copy-start | bytes 1720324
  547.2 311.9 %copy-start.70 = (f32[160]{0:T(256)}, f32[160]{0:T(256)S(1)}, u32[]{:S(2)}) copy-start(f32[160]{0:T(256)S(1)} %fusion.178) | copy-start | bytes 1924
  748.1 80.3 %copy-start.41 = (bf16[1,160,896]{2,1,0:T(8,128)(2,1)S(1)}, bf16[1,160,896]{2,1,0:T(8,128)(2,1)}, u32[]{:S(2)}) copy-start(bf16[1,160,896]{2,1,0:T(8,128)(2,1)} %param.12) | copy-start | bytes 860164
  838.1 180.9 %copy-start.3 = (bf16[160,4864]{1,0:T(8,128)(2,1)}, bf16[160,4864]{1,0:T(8,128)(2,1)S(1)}, u32[]{:S(2)}) copy-start(bf16[160,4864]{1,0:T(8,128)(2,1)S(1)} %get-tuple-element.77) | copy-start | bytes 4669444
  887.5 70.1 %copy-start.78 = (f32[160]{0:T(256)S(1)}, f32[160]{0:T(256)}, u32[]{:S(2)}) copy-start(f32[160]{0:T(256)} %copy-done.77) | copy-start | bytes 1924
  887.5 69.2 %reduce-scatter.35.cloned.1.call-start = ((), (), s32[]{:S(2)}) async-start(), calls=%async_computation.15 | async-start | bytes 368640
  890.6 2611.3 %reduce-scatter.37.cloned.1.call-start = ((), (), s32[]{:S(2)}) async-start(), calls=%async_computation.16 | async-start | bytes 368640
  890.7 70.8 %copy-start.84 = (f32[160]{0:T(256)S(1)}, f32[160]{0:T(256)}, u32[]{:S(2)}) copy-start(f32[160]{0:T(256)} %copy-done.83) | copy-start | bytes 1924
  892.9 68.7 %copy-start.20 = (f32[160,896]{1,0:T(8,128)S(1)}, f32[160,896]{1,0:T(8,128)}, u32[]{:S(2)}) copy-start(f32[160,896]{1,0:T(8,128)} %copy-done.19) | copy-start | bytes 1720324
  1010.6 2492.9 %reduce-scatter.39.cloned.1.call-start = ((), (), s32[]{:S(2)}) async-start(), calls=%async_computation.17 | async-start | bytes 368640
  1019.0 3217.0 %reduce-scatter.43.cloned.1.call-start = ((), (), s32[]{:S(2)}) async-start(), calls=%async_computation.19 | async-start | bytes 17977344
  1026.7 3209.3 %reduce-scatter.41.cloned.1.call-start = ((), (), s32[]{:S(2)}) async-start(), calls=%async_computation.18 | async-start | bytes 17977344
  3870.4 74.8 %copy-start.81 = (f32[160]{0:T(256)S(1)}, f32[160]{0:T(256)}, u32[]{:S(2)}) copy-start(f32[160]{0:T(256)} %copy-done.80) | copy-start | bytes 1924
  3870.4 74.8 %copy-start.18 = (f32[160,896]{1,0:T(8,128)S(1)}, f32[160,896]{1,0:T(8,128)}, u32[]{:S(2)}) copy-start(f32[160,896]{1,0:T(8,128)} %copy-done.16) | copy-start | bytes 1720324
  3872.0 82.5 %collective-permute-start.10 = (f32[32,896]{1,0:T(8,128)}, f32[32,896]{1,0:T(8,128)}, u32[]{:S(2)}, u32[]{:S(2)}) collective-permute-start(f32[32,896]{1,0:T(8,128)} %get-tuple-element.72), channel_id=1, source_target_pairs={{0,3},{1,4},{2,5},{3,6},{4,7},{5,8},{6,9},{7,10},{8,11},{9,12},{10... | collective-permute-start | bytes 344072
  3873.9 87.2 %collective-permute-start.8 = (f32[32,896]{1,0:T(8,128)}, f32[32,896]{1,0:T(8,128)}, u32[]{:S(2)}, u32[]{:S(2)}) collective-permute-start(f32[32,896]{1,0:T(8,128)} %get-tuple-element.72), channel_id=1, source_target_pairs={{0,1},{1,2},{2,3},{3,4},{4,5},{5,6},{6,7},{7,8},{8,9},{9,10},{10,1... | collective-permute-start | bytes 344072
  3875.8 89.8 %collective-permute-start.9 = (f32[32,896]{1,0:T(8,128)}, f32[32,896]{1,0:T(8,128)}, u32[]{:S(2)}, u32[]{:S(2)}) collective-permute-start(f32[32,896]{1,0:T(8,128)} %get-tuple-element.72), channel_id=1, source_target_pairs={{0,2},{1,3},{2,4},{3,5},{4,6},{5,7},{6,8},{7,9},{8,10},{9,11},{10,... | collective-permute-start | bytes 344072
  3879.3 86.4 %copy-start.36 = (f32[32,1152]{1,0:T(8,128)S(1)}, f32[32,1152]{1,0:T(8,128)}, u32[]{:S(2)}) copy-start(f32[32,1152]{1,0:T(8,128)} %get-tuple-element.69) | copy-start | bytes 442372
  3879.3 89.1 %collective-permute-start.12 = (f32[32,896]{1,0:T(8,128)}, f32[32,896]{1,0:T(8,128)}, u32[]{:S(2)}, u32[]{:S(2)}) collective-permute-start(f32[32,896]{1,0:T(8,128)} %get-tuple-element.71), channel_id=1, source_target_pairs={{0,1},{1,2},{2,3},{3,4},{4,5},{5,6},{6,7},{7,8},{8,9},{9,10},{10,1... | collective-permute-start | bytes 344072
  3892.0 56.0 %collective-permute-start.11 = (f32[28,896]{1,0:T(8,128)}, f32[28,896]{1,0:T(8,128)}, u32[]{:S(2)}, u32[]{:S(2)}) collective-permute-start(f32[28,896]{1,0:T(8,128)} %slice.166), channel_id=1, source_target_pairs={{0,4},{1,5},{2,6},{3,7},{4,8},{5,9},{6,10},{7,11},{8,12},{9,13},{1... | collective-permute-start | bytes 301064
  3897.2 72.9 %copy-start.7 = (f32[32,9728]{1,0:T(8,128)S(1)}, f32[32,9728]{1,0:T(8,128)}, u32[]{:S(2)}) copy-start(f32[32,9728]{1,0:T(8,128)} %copy-done.6) | copy-start | bytes 3735556
  3901.4 215.4 %copy-start.5 = (f32[32,9728]{1,0:T(8,128)S(1)}, f32[32,9728]{1,0:T(8,128)}, u32[]{:S(2)}) copy-start(f32[32,9728]{1,0:T(8,128)} %fusion.4) | copy-start | bytes 3735556
  3947.3 162.4 %copy-start.37 = (f32[32,1152]{1,0:T(8,128)S(1)}, f32[32,1152]{1,0:T(8,128)}, u32[]{:S(2)}) copy-start(f32[32,1152]{1,0:T(8,128)} %get-tuple-element.70) | copy-start | bytes 442372
  3948.1 2.8 collective-permute-start.15
  3950.9 19.2 collective-permute-start.13
  3954.4 19.8 collective-permute-start.14
  3961.1 18.4 collective-permute-start.3
  3965.7 20.2 collective-permute-start
  3968.4 14.0 collective-permute-start.7
  3970.1 161.4 %collective-permute-start.20 = (f32[32,9728]{1,0:T(8,128)S(1)}, f32[32,9728]{1,0:T(8,128)}, u32[]{:S(2)}, u32[]{:S(2)}) collective-permute-start(f32[32,9728]{1,0:T(8,128)S(1)} %copy-done.7), channel_id=1, source_target_pairs={{0,1},{1,2},{2,3},{3,4},{4,5},{5,6},{6,7},{7,8},{8,9},{9,10},{10,1... | collective-permute-start | bytes 3735560
  3974.3 28.4 collective-permute-start.1
  3979.5 35.3 collective-permute-start.2
  3982.3 146.8 %collective-permute-start.23 = (f32[28,9728]{1,0:T(8,128)}, f32[28,9728]{1,0:T(8,128)}, u32[]{:S(2)}, u32[]{:S(2)}) collective-permute-start(f32[28,9728]{1,0:T(8,128)} %slice.169), channel_id=1, source_target_pairs={{0,4},{1,5},{2,6},{3,7},{4,8},{5,9},{6,10},{7,11},{8,12},{9,13},{1... | collective-permute-start | bytes 3268616
  3985.8 122.1 %copy-start.64 = (f32[32,1152]{1,0:T(8,128)}, f32[32,1152]{1,0:T(8,128)S(1)}, u32[]{:S(2)}) copy-start(f32[32,1152]{1,0:T(8,128)S(1)} %collective-permute-done) | copy-start | bytes 442372
  3985.8 35.4 collective-permute-start.4
  4002.7 134.6 %collective-permute-start.21 = (f32[32,9728]{1,0:T(8,128)S(1)}, f32[32,9728]{1,0:T(8,128)}, u32[]{:S(2)}, u32[]{:S(2)}) collective-permute-start(f32[32,9728]{1,0:T(8,128)S(1)} %copy-done.7), channel_id=1, source_target_pairs={{0,2},{1,3},{2,4},{3,5},{4,6},{5,7},{6,8},{7,9},{8,10},{9,11},{10,... | collective-permute-start | bytes 3735560
  4014.8 124.8 %collective-permute-start.22 = (f32[32,9728]{1,0:T(8,128)S(1)}, f32[32,9728]{1,0:T(8,128)}, u32[]{:S(2)}, u32[]{:S(2)}) collective-permute-start(f32[32,9728]{1,0:T(8,128)S(1)} %copy-done.7), channel_id=1, source_target_pairs={{0,3},{1,4},{2,5},{3,6},{4,7},{5,8},{6,9},{7,10},{8,11},{9,12},{10... | collective-permute-start | bytes 3735560
  4021.3 49.9 %collective-permute-start.5 = (f32[32,1152]{1,0:T(8,128)S(1)}, f32[32,1152]{1,0:T(8,128)}, u32[]{:S(2)}, u32[]{:S(2)}) collective-permute-start(f32[32,1152]{1,0:T(8,128)S(1)} %copy-done.36), channel_id=1, source_target_pairs={{0,2},{1,3},{2,4},{3,5},{4,6},{5,7},{6,8},{7,9},{8,10},{9,11},{10,... | collective-permute-start | bytes 442376
  4071.2 45.6 %collective-permute-start.6 = (f32[32,1152]{1,0:T(8,128)S(1)}, f32[32,1152]{1,0:T(8,128)}, u32[]{:S(2)}, u32[]{:S(2)}) collective-permute-start(f32[32,1152]{1,0:T(8,128)S(1)} %copy-done.36), channel_id=1, source_target_pairs={{0,3},{1,4},{2,5},{3,6},{4,7},{5,8},{6,9},{7,10},{8,11},{9,12},{10... | collective-permute-start | bytes 442376
  4116.8 55.9 %collective-permute-start.16 = (f32[32,9728]{1,0:T(8,128)S(1)}, f32[32,9728]{1,0:T(8,128)}, u32[]{:S(2)}, u32[]{:S(2)}) collective-permute-start(f32[32,9728]{1,0:T(8,128)S(1)} %copy-done.5), channel_id=1, source_target_pairs={{0,1},{1,2},{2,3},{3,4},{4,5},{5,6},{6,7},{7,8},{8,9},{9,10},{10,1... | collective-permute-start | bytes 3735560
  4129.1 44.0 %collective-permute-start.17 = (f32[32,9728]{1,0:T(8,128)S(1)}, f32[32,9728]{1,0:T(8,128)}, u32[]{:S(2)}, u32[]{:S(2)}) collective-permute-start(f32[32,9728]{1,0:T(8,128)S(1)} %copy-done.5), channel_id=1, source_target_pairs={{0,2},{1,3},{2,4},{3,5},{4,6},{5,7},{6,8},{7,9},{8,10},{9,11},{10,... | collective-permute-start | bytes 3735560
  4131.5 68.4 %collective-permute-start.18 = (f32[32,9728]{1,0:T(8,128)S(1)}, f32[32,9728]{1,0:T(8,128)}, u32[]{:S(2)}, u32[]{:S(2)}) collective-permute-start(f32[32,9728]{1,0:T(8,128)S(1)} %copy-done.5), channel_id=1, source_target_pairs={{0,3},{1,4},{2,5},{3,6},{4,7},{5,8},{6,9},{7,10},{8,11},{9,12},{10... | collective-permute-start | bytes 3735560
  4137.3 35.3 collective-permute-start.19
  (75 other events, 1006.2 us)
Sparse Core Ops, SparseCore 0:
  10.9 65.0 all-gather.23
  78.8 57.6 all-gather.25
  139.9 200.0 all-gather.27
  343.3 76.8 all-gather.29
  423.5 60.3 all-gather.31
  486.6 57.9 all-gather.33
  548.0 200.0 all-gather.35
  751.6 76.7 all-gather.37
  887.6 32.3 reduce-scatter.32
  922.9 33.7 reduce-scatter.34
  1010.7 33.8 reduce-scatter.36
  1047.5 34.0 reduce-scatter.38
  1083.9 739.4 reduce-scatter.42
  1825.5 738.7 reduce-scatter.40
where the time goes:
time: 4280 us; the launch traced here: 4240 us
  blocking collectives  2900 us (68%)
  waiting for transfers between devices  758 us (18%)
  matrix products  259 us (6%)
  local copies, waits for them, and re-layouts  154 us (4%)
  starting transfers between devices  133 us (3%)
    unnamed x6, blocking collectives  2860 us
    all_gather x2, waiting for transfers between devices, body(): lax.all_gather(in_weight[layer_idx], ('ctx', 'wt'), axis=0, tiled=True)  402 us
    unnamed x44, waiting for transfers between devices  134 us
    unnamed x30, starting transfers between devices  133 us
    unnamed x241, local copies, waits for them, and re-layouts  126 us
    all_gather x2, waiting for transfers between devices, body(): lax.all_gather(down_weight[layer_idx], ('ctx', 'wt'), axis=0, tiled=True)  122 us
  transfers between devices with their start and end apart: 38, of which 14 were waited for; matrix products, arithmetic and copies ran while one was open for 73% of the time, Pallas kernels for 0%

commit v1 on v0

v1 whole, which is shorter than its diff:
```python
import math

import jax
import jax.numpy as jnp
from jax import lax
from jax.sharding import PartitionSpec as P

HEADS = 14
KV_HEADS = 2
HEAD = 64
FF = 4864
LAYERS = 2
QW = 896
D = 896
QKV_W = 1152
KV_W = KV_HEADS * HEAD

EPSILON = 1e-06
ROPE_BASE = 1000000.0
NEGATIVE = -1e30

bf16 = jnp.bfloat16
f32 = jnp.float32


def norm_rows(hidden, norm_gain):
    return (
        hidden * lax.rsqrt(jnp.mean(hidden * hidden, axis=-1, keepdims=True) + EPSILON) * norm_gain
    )


def rope_tables(own_positions):
    half_head = HEAD // 2
    frequency = jnp.exp(
        jnp.arange(half_head, dtype=jnp.float32) * (-2.0 * math.log(ROPE_BASE) / HEAD)
    )
    angles = own_positions.astype(jnp.float32)[:, None] * frequency[None, :]
    cos_half = jnp.cos(angles)
    sin_half = jnp.sin(angles)
    return (
        jnp.concatenate([cos_half, cos_half], axis=-1),
        jnp.concatenate([sin_half, sin_half], axis=-1),
    )


def rotate(tensor, cos_table, sin_table):
    half_head = HEAD // 2
    turned = jnp.concatenate([-tensor[..., half_head:], tensor[..., :half_head]], axis=-1)
    return tensor * cos_table[:, None, :] + turned * sin_table[:, None, :]


def dot(left, right):
    return jnp.dot(left, right, preferred_element_type=f32)


def dot_rows(left, right):
    return lax.dot_general(left, right, (((0,), (0,)), ((), ())), preferred_element_type=f32)


def dot_cols(left, right):
    return lax.dot_general(left, right, (((1,), (1,)), ((), ())), preferred_element_type=f32)


class Ring:
    def __init__(self, n, m):
        self.n, self.m = n, m
        if n == 8:
            self.even = [0, 4, 2, 6, 1, 3, 5, 7]
            self.odd = [0, 2, 4, 6, 1, 5, 3, 7]
        else:
            self.even = self.odd = list(range(n))

    def swap(self, value, offset, odd_offset=None):
        odd_offset = offset if odd_offset is None else odd_offset
        return lax.ppermute(
            value, "ctx", [(i, i ^ (odd_offset if i % 2 else offset)) for i in range(self.n)]
        )

    def swap_z(self, value, offset):
        return lax.ppermute(value, "wt", [(i, i ^ offset) for i in range(self.m)])

    def offsets(self, me):
        table = jnp.where(
            me % 2 == 1, jnp.array(self.odd, jnp.int32), jnp.array(self.even, jnp.int32)
        )
        return table

    def gather(self, own):
        if self.n == 8:
            blocks = [own, self.swap(own, 4, 2), self.swap(own, 2, 4), self.swap(own, 6)]
            return jnp.stack(blocks + [self.swap(b, 1) for b in blocks])
        blocks = own[None]
        step = 1
        while step < self.n:
            blocks = jnp.concatenate([blocks, self.swap(blocks, step)])
            step *= 2
        return blocks

    def reduce(self, terms):
        if self.n == 8:
            half = terms[:4].astype(f32) + self.swap(terms[4:], 1).astype(f32)
            quarter = half[:2] + self.swap(half[2:].astype(bf16), 2, 4).astype(f32)
            return quarter[0] + self.swap(quarter[1].astype(bf16), 4, 2).astype(f32)
        step = self.n // 2
        total = terms.astype(f32)
        while step:
            total = total[:step] + self.swap(total[step:].astype(bf16), step).astype(f32)
            step //= 2
        return total[0]

    def gather_z(self, own):
        return jnp.stack([own] + [self.swap_z(own, k) for k in range(1, self.m)])

    def reduce_z(self, terms):
        total = terms[0].astype(f32)
        for k in range(1, self.m):
            total = total + self.swap_z(terms[k].astype(bf16), k).astype(f32)
        return total


def make_body(n, m):
    ring = Ring(n, m)
    rows = D // (n * m)
    bias_w = QKV_W // (n * m)
    pad_rows = -(-(rows + 2) // 8) * 8
    all_rows = n * m * pad_rows
    units = FF // n
    unit_pad = -(-units // 128) * 128

    def gather_rows(block):
        return ring.gather(ring.gather_z(block)).reshape(all_rows, block.shape[-1])

    def reduce_rows(terms):
        width = terms.shape[-1]
        part = ring.reduce(terms.astype(bf16).reshape(n, m * pad_rows, width))
        return ring.reduce_z(part.reshape(m, pad_rows, width))

    def feed_in(in_weight_layer):
        cut = in_weight_layer.reshape(rows, 2, n, units).transpose(2, 0, 1, 3)
        cut = jnp.pad(cut, ((0, 0), (0, 0), (0, 0), (0, unit_pad - units)))
        cut = cut.reshape(n, rows, 2 * unit_pad)
        got = lax.all_to_all(cut, "ctx", 0, 0, tiled=True).reshape(n * rows, 2 * unit_pad)
        full = lax.all_gather(got, "wt", axis=0, tiled=True)
        full = full.reshape(m, n, rows, 2 * unit_pad).transpose(1, 0, 2, 3)
        return full.reshape(D, 2 * unit_pad)

    def feed_in_terms(grad):
        terms = grad.astype(bf16).reshape(n, m, rows, 2 * unit_pad).transpose(1, 0, 2, 3)
        terms = terms.reshape(D, 2 * unit_pad)
        return lax.psum_scatter(terms, "wt", scatter_dimension=0, tiled=True)

    def feed_in_home(parts):
        cut = jnp.stack([p.reshape(n, rows, 2 * unit_pad) for p in parts], axis=1)
        got = lax.all_to_all(cut, "ctx", 0, 0, tiled=True)
        got = got.reshape(n, LAYERS, rows, 2, unit_pad)[..., :units].astype(f32)
        return got.transpose(1, 2, 3, 0, 4).reshape(LAYERS, rows, 2 * FF)

    def body(
        hidden_in,
        positions,
        cotangent,
        attn_gain,
        qkv_weight,
        qkv_bias,
        out_weight,
        mlp_gain,
        in_weight,
        down_weight,
    ):
        me, me_z = lax.axis_index("ctx"), lax.axis_index("wt")
        shard = me * m + me_z
        offsets = ring.offsets(me)
        own_positions = positions[0]
        row_count = own_positions.shape[0]

        bias_rows = [
            lax.dynamic_update_slice(
                jnp.zeros((1, QKV_W), bf16), qkv_bias[l][None], (0, shard * bias_w)
            )
            for l in range(LAYERS)
        ]

        def qkv_block(l):
            gains = jnp.zeros((1, QKV_W), bf16)
            gains = lax.dynamic_update_slice(gains, attn_gain[l][None], (0, 0))
            gains = lax.dynamic_update_slice(gains, mlp_gain[l][None], (0, 128))
            rest = jnp.zeros((pad_rows - rows - 2, QKV_W), bf16)
            return jnp.concatenate([qkv_weight[l], bias_rows[l], gains, rest])

        def out_block(l):
            return jnp.pad(out_weight[l], ((0, pad_rows - rows), (0, 0)))

        joint = [gather_rows(qkv_block(l)) for l in range(LAYERS)]
        out_proj = [gather_rows(out_block(l)) for l in range(LAYERS)]

        column = jnp.arange(all_rows, dtype=jnp.int32)
        in_block, block = column % pad_rows, column // pad_rows
        block_owner = ((me ^ offsets[:, None]) * m + (me_z ^ jnp.arange(m))[None, :]).reshape(-1)
        owner = jnp.repeat(block_owner, pad_rows)
        feature = jnp.where(in_block < rows, owner * rows + in_block, -1)
        perm = (jnp.arange(D, dtype=jnp.int32)[:, None] == feature[None, :]).astype(bf16)
        ones_column = (in_block == rows).astype(bf16)[None, :]

        def to_rel(value):
            return dot(value, perm).astype(bf16)

        def from_rel(value):
            return dot_cols(value, perm)

        def gains_of(l):
            kept = joint[l].reshape(n * m, pad_rows, QKV_W)[:, rows + 1, :]
            both = jnp.stack([kept[:, :pad_rows], kept[:, 128 : 128 + pad_rows]])
            return from_rel(both.reshape(2, all_rows))

        gains = [gains_of(l) for l in range(LAYERS)]
        in_proj = [feed_in(in_weight[l]) for l in range(LAYERS)]
        down_proj = [
            lax.all_gather(down_weight[l], "wt", axis=0, tiled=True) for l in range(LAYERS)
        ]

        positions_by_index = lax.all_gather(own_positions, "ctx", axis=0, tiled=False)
        all_positions = positions_by_index[me ^ offsets].reshape(-1)
        cos_table, sin_table = rope_tables(own_positions)
        allowed = all_positions[None, :] <= own_positions[:, None]

        cotangent_low = ring.gather(cotangent[0]).reshape(n * row_count, D)

        def grouped_scores(queries, all_keys):
            grouped = queries.reshape(row_count, KV_HEADS, HEADS // KV_HEADS, HEAD)
            scores = jnp.einsum(
                "tkgd,skd->tkgs", grouped, all_keys, preferred_element_type=f32
            ) * HEAD ** (-0.5)
            return (grouped, jnp.where(allowed[:, None, None, :], scores, NEGATIVE))

        def attention_forward(hidden, l):
            normed = norm_rows(hidden, gains[l][0]).astype(bf16)
            normed_rel = to_rel(normed) + ones_column
            packed = dot(normed_rel, joint[l])
            queries = rotate(
                packed[:, :QW].reshape(row_count, HEADS, HEAD), cos_table, sin_table
            ).astype(bf16)
            own_keys = rotate(
                packed[:, QW : QW + KV_W].reshape(row_count, KV_HEADS, HEAD), cos_table, sin_table
            ).astype(bf16)
            own_kv = jnp.concatenate(
                [own_keys.reshape(row_count, KV_W), packed[:, QW + KV_W :].astype(bf16)], axis=1
            )
            all_kv = ring.gather(own_kv).reshape(n * row_count, 2, KV_HEADS, HEAD)
            all_keys, all_values = all_kv[:, 0], all_kv[:, 1]
            grouped, scores = grouped_scores(queries, all_keys)
            row_max = jnp.max(scores, axis=-1, keepdims=True)
            exponent = jnp.exp(scores - row_max)
            row_sum = jnp.sum(exponent, axis=-1, keepdims=True)
            attn_probs = (exponent / row_sum).astype(bf16)
            head_mix = jnp.einsum(
                "tkgs,skd->tkgd", attn_probs, all_values, preferred_element_type=f32
            )
            heads_rel = to_rel(head_mix.reshape(row_count, QW).astype(bf16))
            middle = hidden + dot(heads_rel, out_proj[l])
            return middle, (normed_rel, queries, all_keys, all_values, row_max, row_sum, heads_rel)

        def mlp_forward(middle, l):
            normed2 = norm_rows(middle, gains[l][1]).astype(bf16)
            normed2 = ring.gather(normed2).reshape(n * row_count, D)
            gate_up = dot(normed2, in_proj[l])
            gate, up = gate_up[:, :unit_pad], gate_up[:, unit_pad:]
            activated = (jax.nn.silu(gate) * up).astype(bf16)[:, :units]
            terms = dot(activated, down_proj[l]).astype(bf16)
            after = middle + ring.reduce(terms.reshape(n, row_count, D))
            return after, (normed2, gate, up, activated)

        def mlp_backward(gradient, grad_low, middle, stored, l):
            normed2, gate, up, activated = stored
            act_grad = dot_cols(grad_low, down_proj[l])
            act_grad = jnp.pad(act_grad, ((0, 0), (0, unit_pad - units)))
            unused, unit_back = jax.vjp(lambda g, u: jax.nn.silu(g) * u, gate, up)
            gate_grad, up_grad = unit_back(act_grad)
            gate_up_grad = jnp.concatenate([gate_grad.astype(bf16), up_grad.astype(bf16)], axis=1)
            terms = dot_cols(gate_up_grad, in_proj[l]).astype(bf16)
            normed_grad = ring.reduce(terms.reshape(n, row_count, D))
            in_part = feed_in_terms(dot_rows(normed2, gate_up_grad))
            down_part = lax.psum_scatter(
                dot_rows(activated, grad_low).astype(bf16), "wt", scatter_dimension=0, tiled=True
            )
            unused, norm_back = jax.vjp(norm_rows, middle, gains[l][1])
            middle_part, gain_grad = norm_back(normed_grad)
            return gradient + middle_part, gain_grad, in_part, down_part.astype(f32)

        def attention_backward(gradient, hidden, stored, mlp_gain_term, l):
            normed_rel, queries, all_keys, all_values, row_max, row_sum, heads_rel = stored
            score_scale = HEAD ** (-0.5)
            grad_low = gradient.astype(bf16)
            out_part = reduce_rows(dot_rows(heads_rel, grad_low))
            heads_grad = from_rel(dot_cols(grad_low, out_proj[l]).astype(bf16)).astype(bf16)
            heads_grad = heads_grad.reshape(row_count, KV_HEADS, HEADS // KV_HEADS, HEAD)
            grouped, scores = grouped_scores(queries, all_keys)
            attn_probs = jnp.exp(scores - row_max) / row_sum
            prob_grad = jnp.einsum(
                "tkgd,skd->tkgs", heads_grad, all_values, preferred_element_type=f32
            )
            row_inner = jnp.sum(attn_probs * prob_grad, axis=-1, keepdims=True)
            score_grad = (attn_probs * (prob_grad - row_inner)).astype(bf16)
            key_terms = (
                jnp.einsum("tkgs,tkgd->skd", score_grad, grouped, preferred_element_type=f32)
                * score_scale
            )
            value_terms = jnp.einsum(
                "tkgs,tkgd->skd", attn_probs.astype(bf16), heads_grad, preferred_element_type=f32
            )
            kv_terms = jnp.stack([key_terms, value_terms], axis=1).astype(bf16)
            kv_grad = ring.reduce(kv_terms.reshape(n, row_count, 2 * KV_W))
            query_grad = jnp.einsum(
                "tkgs,skd->tkgd", score_grad, all_keys, preferred_element_type=f32
            )
            query_grad = query_grad.reshape(row_count, HEADS, HEAD) * score_scale

            def turn(tensor):
                return rotate(tensor, cos_table, sin_table)

            unused, query_back = jax.vjp(turn, query_grad)
            query_part = query_back(query_grad)[0].reshape(row_count, QW).astype(bf16)
            own_key_grad = kv_grad[:, :KV_W].reshape(row_count, KV_HEADS, HEAD)
            unused, key_back = jax.vjp(turn, own_key_grad)
            key_part = key_back(own_key_grad)[0].reshape(row_count, KV_W)
            kv_part = jnp.concatenate([key_part, kv_grad[:, KV_W:]], axis=1).astype(bf16)

            query_sums = reduce_rows(dot_rows(normed_rel, query_part))
            rel_grad = dot_cols(query_part, joint[l][:, :QW]) + dot_cols(
                kv_part, joint[l][:, QW:]
            )
            rel_high = rel_grad.astype(bf16)
            rel_low = (rel_grad - rel_high.astype(f32)).astype(bf16)
            normed_grad = from_rel(rel_high) + from_rel(rel_low)
            unused, norm_back = jax.vjp(norm_rows, hidden, gains[l][0])
            hidden_part, gain_grad = norm_back(normed_grad)
            gain_terms = jnp.pad(
                jnp.stack([gain_grad, mlp_gain_term]).astype(bf16), ((0, 126), (0, 0))
            )
            last_terms = jnp.concatenate(
                [dot_rows(normed_rel, kv_part), lax.dot_general(
                    perm, gain_terms, (((0,), (1,)), ((), ())), preferred_element_type=f32
                )], axis=1
            )
            last_sums = reduce_rows(last_terms)
            joint_part = jnp.concatenate([query_sums, last_sums[:, : 2 * KV_W]], axis=1)
            bias_part = lax.dynamic_slice(joint_part, (rows, shard * bias_w), (1, bias_w))[0]
            attn_gain_part = last_sums[:rows, 2 * KV_W]
            mlp_gain_part = last_sums[:rows, 2 * KV_W + 1]
            return gradient + hidden_part, (
                attn_gain_part,
                joint_part[:rows],
                bias_part,
                out_part[:rows],
                mlp_gain_part,
            )

        hidden = hidden_in[0].astype(f32)
        stored_layers = []
        for l in range(LAYERS):
            middle, attn_stored = attention_forward(hidden, l)
            after, mlp_stored = mlp_forward(middle, l)
            stored_layers.append((hidden, attn_stored, middle, mlp_stored))
            hidden = after
        gradient = cotangent[0].astype(f32)
        grad_low = cotangent_low
        attn_sums, in_sums, down_sums = [None] * LAYERS, [None] * LAYERS, [None] * LAYERS
        for l in reversed(range(LAYERS)):
            layer_input, attn_stored, middle, mlp_stored = stored_layers[l]
            if grad_low is None:
                grad_low = ring.gather(gradient.astype(bf16)).reshape(n * row_count, D)
            gradient, mlp_gain_term, in_sums[l], down_sums[l] = mlp_backward(
                gradient, grad_low, middle, mlp_stored, l
            )
            gradient, attn_sums[l] = attention_backward(
                gradient, layer_input, attn_stored, mlp_gain_term, l
            )
            grad_low = None
        in_weight_grad = feed_in_home(in_sums)
        stacked = [jnp.stack([part[i] for part in attn_sums]) for i in range(5)]
        return (
            hidden[None],
            gradient[None],
            *stacked,
            in_weight_grad,
            jnp.stack(down_sums),
        )

    return body


def solution(mesh):
    shape = dict(mesh.shape)
    return jax.shard_map(
        make_body(shape["ctx"], shape["wt"]),
        mesh=mesh,
        in_specs=(
            P("wt", "ctx", None),
            P("wt", "ctx"),
            P("wt", "ctx", None),
            P(None, ("ctx", "wt")),
            P(None, ("ctx", "wt"), None),
            P(None, ("ctx", "wt")),
            P(None, ("ctx", "wt"), None),
            P(None, ("ctx", "wt")),
            P(None, ("ctx", "wt"), None),
            P(None, ("ctx", "wt"), None),
        ),
        out_specs=(
            P("wt", "ctx", None),
            P("wt", "ctx", None),
            P(None, ("ctx", "wt")),
            P(None, ("ctx", "wt"), None),
            P(None, ("ctx", "wt")),
            P(None, ("ctx", "wt"), None),
            P(None, ("ctx", "wt")),
            P(None, ("ctx", "wt"), None),
            P(None, ("ctx", "wt"), None),
        ),
        check_vma=False,
    )
```

time: 4280 us -> 714 us (0.17)
  blocking collectives: 2900 us -> 29.1 us
  waiting for transfers between devices: 758 us -> 161 us
  matrix products: 259 us -> 139 us
    unnamed x6 -> x0, blocking collectives: 2860 us -> none
    all_gather x8 -> x4, waiting for transfers between devices: 624 us -> 0.03 us  [the longest x2 0.02 us: body(): lax.all_gather(down_weight[l], 'wt', axis=0, tiled=True)]
    ppermute x0 -> x136, waiting for transfers between devices: none -> 147 us  [the longest x106 121 us: swap(): lax.ppermute(value, 'ctx', [(i, i ^ (odd_offset if i % 2 else offset)) fo...]
    unnamed x44 -> x10, waiting for transfers between devices: 134 us -> 0.8 us
    unnamed x30 -> x2, starting transfers between devices: 133 us -> 0.47 us
    ppermute x0 -> x136, starting transfers between devices: none -> 127 us  [the longest x106 77.3 us: swap(): lax.ppermute(value, 'ctx', [(i, i ^ (odd_offset if i % 2 else offset)) fo...]
    dot_general x26 -> x42, matrix products: 208 us -> 94 us  [the longest x16 30.9 us: dot_cols(): lax.dot_general(left, right, (((1,), (1,)), ((), ())), preferred_element_...]
    unnamed x241 -> x382, local copies, waits for them, and re-layouts: 126 us -> 57 us
  transfers between devices with their start and end apart: 38 -> 146, of which waited for: 14 -> 42; matrix products, arithmetic and copies ran while one was open for 73% -> 43% of each run, Pallas kernels for 0% -> 0%
where the time goes in v1:
time: 714 us; the launch traced here: 706 us
  local copies, waits for them, and re-layouts  165 us (23%)
  waiting for transfers between devices  161 us (23%)
  matrix products  139 us (19%)
  starting transfers between devices  135 us (19%)
  other arithmetic  59.4 us (8%)
  blocking collectives  29.1 us (4%)
  between operations  18 us (3%)
    ppermute x106, waiting for transfers between devices, swap(): lax.ppermute(value, 'ctx', [(i, i ^ (odd_offset if i % 2 else offset)) fo...  121 us
    ppermute x106, starting transfers between devices, swap(): lax.ppermute(value, 'ctx', [(i, i ^ (odd_offset if i % 2 else offset)) fo...  77.3 us
    unnamed x382, local copies, waits for them, and re-layouts  57 us
    ppermute x30, starting transfers between devices, swap_z(): return lax.ppermute(value, 'wt', [(i, i ^ offset) for i in range(self.m)])  49.6 us
    dot_general x16, matrix products, dot_cols(): lax.dot_general(left, right, (((1,), (1,)), ((), ())), preferred_element_...  30.9 us
    dot_general x10, matrix products, dot_rows(): lax.dot_general(left, right, (((0,), (0,)), ((), ())), preferred_element_...  25.6 us
    ppermute x30, waiting for transfers between devices, swap_z(): return lax.ppermute(value, 'wt', [(i, i ^ offset) for i in range(self.m)])  25.4 us
    dot_general x12, matrix products, dot(): return jnp.dot(left, right, preferred_element_type=f32)  23.5 us
  transfers between devices with their start and end apart: 146, of which 42 were waited for; matrix products, arithmetic and copies ran while one was open for 43% of the time, Pallas kernels for 0%

profile of v1, /device:TPU:0, one launch (start us, length us, event | category | flops | bytes accessed | tf_op | source)
XLA Modules:
  0.0 705.9 jit_solution(11565634216184857223)
XLA Ops:
  7.2 6.5 slice_reduce_fusion
  14.8 16.2 %all_to_all.15 = bf16[8,28,1280]{2,1,0:T(8,128)(2,1)S(1)} all-to-all(bf16[8,28,1280]{2,1,0:T(8,128)(2,1)S(1)} %copy.136), channel_id=1, replica_groups=mesh['ctx'=8,'wt'=4] {'ctx'}, dimensions={0} | all-to-all | bytes 1146880 | tf_op jit(solution)/shard_map/all_to_all | solution.py:142
  43.8 3.5 all-to-all-start.1
  48.6 12.8 %all-gather.2 = s32[8,1,160]{2,1,0:T(1,128)S(1)} all-gather(s32[1,1,160]{2,1,0:T(1,128)S(1)} %bitcast.780), channel_id=1, replica_groups=mesh['ctx'=8,'wt'=4] {'ctx'}, dimensions={0}, use_global_device_ids=true | all-gather | bytes 5760 | tf_op jit(solution)/shard_map/all_gather | solution.py:221
  68.1 3.4 collective-permute-start.39
  72.6 3.4 collective-permute-start.2
  76.0 3.3 collective-permute-start.1
  79.4 5.3 collective-permute-start
  84.7 7.3 %collective-permute-done.38 = bf16[32,1152]{1,0:T(8,128)(2,1)S(1)} collective-permute-done((bf16[32,1152]{1,0:T(8,128)(2,1)S(1)}, bf16[32,1152]{1,0:T(8,128)(2,1)S(1)}, u32[]{:S(2)}, u32[]{:S(2)}) %collective-permute-start.38) | collective-permute-done | bytes 73760 | tf_op jit(solution)/shard_map/ppermute | solution.py:80
  97.9 9.9 %collective-permute-done.74 = bf16[160,896]{1,0:T(8,128)(2,1)S(1)} collective-permute-done((bf16[160,896]{1,0:T(8,128)(2,1)}, bf16[160,896]{1,0:T(8,128)(2,1)S(1)}, u32[]{:S(2)}, u32[]{:S(2)}) %collective-permute-start.74) | collective-permute-done | bytes 286752 | tf_op jit(solution)/shard_map/ppermute | solution.py:75
  113.4 4.8 collective-permute-done.57
  124.9 5.4 collective-permute-done.20
  137.6 12.8 %collective-permute-done.40 = bf16[4,32,1152]{2,1,0:T(8,128)(2,1)S(1)} collective-permute-done((bf16[4,32,1152]{2,1,0:T(8,128)(2,1)S(1)}, bf16[4,32,1152]{2,1,0:T(8,128)(2,1)S(1)}, u32[]{:S(2)}, u32[]{:S(2)}) %collective-permute-start.40) | collective-permute-done | bytes 294944 | tf_op jit(solution)/shard_map/ppermute | solution.py:75
  187.2 3.3 collective-permute-start.12
  200.9 6.7 fusion.317
  208.1 4.7 fusion.94
  222.9 4.4 collective-permute-start.29
  228.8 3.7 collective-permute-done.29
  241.5 2.8 reshape.479
  244.3 6.3 fusion.320
  255.0 3.4 convolution_convert_fusion.1
  265.9 6.9 collective-permute-done.35
  276.5 4.6 collective-permute-done.36
  298.3 6.7 fusion.318
  305.1 4.6 fusion.97
  317.0 4.8 fusion.118
  326.1 3.1 reshape.490
  336.4 5.7 fusion.322
  342.1 3.0 fusion.32
  346.8 4.6 convolution_convert_fusion.2
  351.4 4.1 reshape.507
  355.4 3.4 copy.164
  358.9 4.1 reshape.508
  363.2 6.2 convolution_convert_fusion.5
  381.5 2.8 convolution_convert_fusion.10
  387.3 6.6 collective-permute-done.72
  396.2 5.6 collective-permute-done.73
  407.5 6.2 fusion.69
  413.6 6.5 fusion.5
  425.2 2.9 fusion.186
  439.5 3.6 collective-permute-done.85
  466.7 11.7 %collective-permute-done.87 = bf16[160,896]{1,0:T(8,128)(2,1)} collective-permute-done((bf16[160,896]{1,0:T(8,128)(2,1)}, bf16[160,896]{1,0:T(8,128)(2,1)}, u32[]{:S(2)}, u32[]{:S(2)}) %collective-permute-start.87) | collective-permute-done | bytes 286752 | tf_op jit(solution)/shard_map/ppermute | solution.py:75
  496.9 2.8 convolution_convert_fusion.11
  499.7 5.0 fusion.35
  504.9 7.3 %convolution_convert_fusion.3 = bf16[896,1280]{1,0:T(8,128)(2,1)} fusion(bf16[1280,896]{1,0:T(8,128)(2,1)} %bitcast.66, bf16[1280,640]{0,1:T(8,128)(2,1)} %get-tuple-element.85, bf16[1280,640]{0,1:T(8,128)(2,1)} %get-tuple-element.84), kind=kOutput, calls=%fused_computation.47 | convolution fusion | flops 2943713280 | bytes 7864320 | tf_op jit(solution)/shard_map/dot_general | solution.py:57
  514.3 3.8 convolution_convert_fusion.4
  527.7 4.1 reshape.506
  537.4 2.8 collective-permute-done.120
  549.9 2.9 collective-permute-start.134
  552.9 6.0 collective-permute-done.122
  559.9 6.9 collective-permute-done.134
  570.2 3.1 fusion.113
  575.6 6.2 fusion.66
  581.7 7.1 %fusion.2 = (f32[160,2,7]{0,2,1:T(8,128)}, f32[2,1280,160,7]{1,2,3,0:T(8,128)S(1)}) fusion(f32[160,2,7,1280]{3,0,2,1:T(8,128)} %get-tuple-element.183, f32[160,2,7]{0,2,1:T(8,128)S(1)} %copy-done.118, bf16[160,2,7,64]{0,3,2,1:T(8,128)(2,1)S(1)} %bitcast.737, bf16[1280,2,2,64]{0,3,2,1:T(8,128)(2,1)S(1)} %copy-done.77), kind=kOutput, calls=%fused_computation.5 | convolution fusion | flops 375600960 | bytes 23749376 | tf_op jit(solution)/shard_map/tkgd,skd->tkgs/dot_general | solution.py:298
  589.5 3.2 fusion.4
  594.0 2.9 fusion.184
  605.3 5.5 collective-permute-done.98
  632.9 4.0 collective-permute-done.101
  642.6 2.9 collective-permute-start.105
  651.8 8.0 %collective-permute-done.113 = bf16[2,128,896]{2,1,0:T(8,128)(2,1)S(1)} collective-permute-done((bf16[2,128,896]{2,1,0:T(8,128)(2,1)S(1)}, bf16[2,128,896]{2,1,0:T(8,128)(2,1)S(1)}, u32[]{:S(2)}, u32[]{:S(2)}) %collective-permute-start.113) | collective-permute-done | bytes 458784 | tf_op jit(solution)/shard_map/ppermute | solution.py:75
  661.0 2.8 collective-permute-start.129
  673.4 3.7 all-to-all-start.2
  679.6 13.9 %all-to-all-done.2 = bf16[8,2,28,1280]{3,1,2,0:T(2,128)(2,1)S(1)} async-done(((bf16[8,2,28,1280]{3,1,2,0:T(2,128)(2,1)}), bf16[8,2,28,1280]{3,1,2,0:T(2,128)(2,1)S(1)}, u32[]{:S(2)}, u32[]{:S(2)}) %all-to-all-start.2) | async-done | bytes 1146912 | tf_op jit(solution)/shard_map/all_to_all | solution.py:154
  695.3 3.6 reshape.526
  (961 shorter events, 342.0 us)
Async XLA Ops:
  7.2 230.0 %all-gather.8.cloned.1.call-start = ((), (), s32[]{:S(2)}) async-start(), calls=%async_computation.7 | async-start | bytes 2867200 | tf_op jit(solution)/shard_map/all_gather | solution.py:143
  32.0 222.0 %all-gather.12.cloned.1.call-start = ((), (), s32[]{:S(2)}) async-start(), calls=%async_computation.11 | async-start | bytes 1361920 | tf_op jit(solution)/shard_map/all_gather | solution.py:218
  33.1 34.5 %collective-permute-start.55 = (bf16[32,896]{1,0:T(8,128)(2,1)S(1)}, bf16[32,896]{1,0:T(8,128)(2,1)S(1)}, u32[]{:S(2)}, u32[]{:S(2)}) collective-permute-start(bf16[32,896]{1,0:T(8,128)(2,1)S(1)} %get-tuple-element.163), channel_id=1, source_target_pairs={{0,2},{1,3},{2,0},{3,1},{4,6},{5,7},{6,4},{7,5},{8,10},{9,11},{10,... | collective-permute-start | bytes 172040 | tf_op jit(solution)/shard_map/ppermute | solution.py:80
  35.8 32.3 %collective-permute-start.54 = (bf16[32,896]{1,0:T(8,128)(2,1)S(1)}, bf16[32,896]{1,0:T(8,128)(2,1)S(1)}, u32[]{:S(2)}, u32[]{:S(2)}) collective-permute-start(bf16[32,896]{1,0:T(8,128)(2,1)S(1)} %get-tuple-element.163), channel_id=1, source_target_pairs={{0,1},{1,0},{2,3},{3,2},{4,5},{5,4},{6,7},{7,6},{8,9},{9,8},{10,11... | collective-permute-start | bytes 172040 | tf_op jit(solution)/shard_map/ppermute | solution.py:80
  37.3 34.2 %collective-permute-start.56 = (bf16[32,896]{1,0:T(8,128)(2,1)S(1)}, bf16[32,896]{1,0:T(8,128)(2,1)S(1)}, u32[]{:S(2)}, u32[]{:S(2)}) collective-permute-start(bf16[32,896]{1,0:T(8,128)(2,1)S(1)} %get-tuple-element.163), channel_id=1, source_target_pairs={{0,3},{1,2},{2,1},{3,0},{4,7},{5,6},{6,5},{7,4},{8,11},{9,10},{10,... | collective-permute-start | bytes 172040 | tf_op jit(solution)/shard_map/ppermute | solution.py:80
  37.6 34.0 %collective-permute-start.18 = (bf16[32,896]{1,0:T(8,128)(2,1)S(1)}, bf16[32,896]{1,0:T(8,128)(2,1)S(1)}, u32[]{:S(2)}, u32[]{:S(2)}) collective-permute-start(bf16[32,896]{1,0:T(8,128)(2,1)S(1)} %get-tuple-element.165), channel_id=1, source_target_pairs={{0,2},{1,3},{2,0},{3,1},{4,6},{5,7},{6,4},{7,5},{8,10},{9,11},{10,... | collective-permute-start | bytes 172040 | tf_op jit(solution)/shard_map/ppermute | solution.py:80
  39.3 33.3 %collective-permute-start.17 = (bf16[32,896]{1,0:T(8,128)(2,1)S(1)}, bf16[32,896]{1,0:T(8,128)(2,1)S(1)}, u32[]{:S(2)}, u32[]{:S(2)}) collective-permute-start(bf16[32,896]{1,0:T(8,128)(2,1)S(1)} %get-tuple-element.165), channel_id=1, source_target_pairs={{0,1},{1,0},{2,3},{3,2},{4,5},{5,4},{6,7},{7,6},{8,9},{9,8},{10,11... | collective-permute-start | bytes 172040 | tf_op jit(solution)/shard_map/ppermute | solution.py:80
  43.8 115.0 %all-to-all-start.1 = ((bf16[8,28,1280]{2,1,0:T(8,128)(2,1)}), bf16[8,28,1280]{2,1,0:T(8,128)(2,1)S(1)}, u32[]{:S(2)}, u32[]{:S(2)}) async-start(bf16[8,28,1280]{2,1,0:T(8,128)(2,1)} %copy.147), calls=%async_computation.1 | async-start | bytes 1310720 | tf_op jit(solution)/shard_map/all_to_all | solution.py:142
  47.3 269.7 %all-gather.14.cloned.1.call-start = ((), (), s32[]{:S(2)}) async-start(), calls=%async_computation.12 | async-start | bytes 1361920 | tf_op jit(solution)/shard_map/all_gather | solution.py:218
  48.1 273.7 %all-gather.10.cloned.1.call-start = ((), (), s32[]{:S(2)}) async-start(), calls=%async_computation.8 | async-start | bytes 2867200 | tf_op jit(solution)/shard_map/all_gather | solution.py:143
  71.5 20.5 %collective-permute-start.38 = (bf16[32,1152]{1,0:T(8,128)(2,1)S(1)}, bf16[32,1152]{1,0:T(8,128)(2,1)S(1)}, u32[]{:S(2)}, u32[]{:S(2)}) collective-permute-start(bf16[32,1152]{1,0:T(8,128)(2,1)S(1)} %get-tuple-element.174), channel_id=1, source_target_pairs={{0,2},{1,3},{2,0},{3,1},{4,6},{5,7},{6,4},{7,5},{8,10},{9,11},{10,... | collective-permute-start | bytes 221192 | tf_op jit(solution)/shard_map/ppermute | solution.py:80
  71.6 21.8 %collective-permute-start.37 = (bf16[32,1152]{1,0:T(8,128)(2,1)S(1)}, bf16[32,1152]{1,0:T(8,128)(2,1)S(1)}, u32[]{:S(2)}, u32[]{:S(2)}) collective-permute-start(bf16[32,1152]{1,0:T(8,128)(2,1)S(1)} %get-tuple-element.174), channel_id=1, source_target_pairs={{0,1},{1,0},{2,3},{3,2},{4,5},{5,4},{6,7},{7,6},{8,9},{9,8},{10,11... | collective-permute-start | bytes 221192 | tf_op jit(solution)/shard_map/ppermute | solution.py:80
  72.6 21.7 %collective-permute-start.2 = (bf16[32,1152]{1,0:T(8,128)(2,1)S(1)}, bf16[32,1152]{1,0:T(8,128)(2,1)S(1)}, u32[]{:S(2)}, u32[]{:S(2)}) collective-permute-start(bf16[32,1152]{1,0:T(8,128)(2,1)S(1)} %get-tuple-element.175), channel_id=1, source_target_pairs={{0,3},{1,2},{2,1},{3,0},{4,7},{5,6},{6,5},{7,4},{8,11},{9,10},{10,... | collective-permute-start | bytes 221192 | tf_op jit(solution)/shard_map/ppermute | solution.py:80
  76.0 20.7 %collective-permute-start.1 = (bf16[32,1152]{1,0:T(8,128)(2,1)S(1)}, bf16[32,1152]{1,0:T(8,128)(2,1)S(1)}, u32[]{:S(2)}, u32[]{:S(2)}) collective-permute-start(bf16[32,1152]{1,0:T(8,128)(2,1)S(1)} %get-tuple-element.175), channel_id=1, source_target_pairs={{0,2},{1,3},{2,0},{3,1},{4,6},{5,7},{6,4},{7,5},{8,10},{9,11},{10,... | collective-permute-start | bytes 221192 | tf_op jit(solution)/shard_map/ppermute | solution.py:80
  79.4 17.5 %collective-permute-start = (bf16[32,1152]{1,0:T(8,128)(2,1)S(1)}, bf16[32,1152]{1,0:T(8,128)(2,1)S(1)}, u32[]{:S(2)}, u32[]{:S(2)}) collective-permute-start(bf16[32,1152]{1,0:T(8,128)(2,1)S(1)} %get-tuple-element.175), channel_id=1, source_target_pairs={{0,1},{1,0},{2,3},{3,2},{4,5},{5,4},{6,7},{7,6},{8,9},{9,8},{10,11... | collective-permute-start | bytes 221192 | tf_op jit(solution)/shard_map/ppermute | solution.py:80
  92.0 20.6 %collective-permute-start.76 = (bf16[160,896]{1,0:T(8,128)(2,1)}, bf16[160,896]{1,0:T(8,128)(2,1)S(1)}, u32[]{:S(2)}, u32[]{:S(2)}) collective-permute-start(bf16[160,896]{1,0:T(8,128)(2,1)} %bitcast.146), channel_id=1, source_target_pairs={{0,24},{4,28},{8,16},{12,20},{16,8},{20,12},{24,0},{28,4},{1,25},{... | collective-permute-start | bytes 860168 | tf_op jit(solution)/shard_map/ppermute | solution.py:75
  93.4 17.0 %collective-permute-start.75 = (bf16[160,896]{1,0:T(8,128)(2,1)}, bf16[160,896]{1,0:T(8,128)(2,1)S(1)}, u32[]{:S(2)}, u32[]{:S(2)}) collective-permute-start(bf16[160,896]{1,0:T(8,128)(2,1)} %bitcast.146), channel_id=1, source_target_pairs={{0,8},{4,20},{8,0},{12,28},{16,24},{20,4},{24,16},{28,12},{1,9},{5... | collective-permute-start | bytes 860168 | tf_op jit(solution)/shard_map/ppermute | solution.py:75
  94.3 13.5 %collective-permute-start.74 = (bf16[160,896]{1,0:T(8,128)(2,1)}, bf16[160,896]{1,0:T(8,128)(2,1)S(1)}, u32[]{:S(2)}, u32[]{:S(2)}) collective-permute-start(bf16[160,896]{1,0:T(8,128)(2,1)} %bitcast.146), channel_id=1, source_target_pairs={{0,16},{4,12},{8,24},{12,4},{16,0},{20,28},{24,8},{28,20},{1,17},{... | collective-permute-start | bytes 860168 | tf_op jit(solution)/shard_map/ppermute | solution.py:75
  96.8 39.2 %collective-permute-start.77 = (bf16[160,896]{1,0:T(8,128)(2,1)}, bf16[160,896]{1,0:T(8,128)(2,1)S(1)}, u32[]{:S(2)}, u32[]{:S(2)}) collective-permute-start(bf16[160,896]{1,0:T(8,128)(2,1)} %bitcast.146), channel_id=1, source_target_pairs={{0,4},{4,0},{8,12},{12,8},{16,20},{20,16},{24,28},{28,24},{1,5},{5... | collective-permute-start | bytes 860168 | tf_op jit(solution)/shard_map/ppermute | solution.py:75
  96.9 25.5 %collective-permute-start.59 = (bf16[4,32,896]{2,1,0:T(8,128)(2,1)S(1)}, bf16[4,32,896]{2,1,0:T(8,128)(2,1)}, u32[]{:S(2)}, u32[]{:S(2)}) collective-permute-start(bf16[4,32,896]{2,1,0:T(8,128)(2,1)S(1)} %pad_maximum_fusion.15), channel_id=1, source_target_pairs={{0,24},{4,28},{8,16},{12,20},{16,8},{20,12},{24,0},{28,4},{1,25},{... | collective-permute-start | bytes 688136 | tf_op jit(solution)/shard_map/ppermute | solution.py:75
  107.8 11.9 %collective-permute-start.58 = (bf16[4,32,896]{2,1,0:T(8,128)(2,1)S(1)}, bf16[4,32,896]{2,1,0:T(8,128)(2,1)}, u32[]{:S(2)}, u32[]{:S(2)}) collective-permute-start(bf16[4,32,896]{2,1,0:T(8,128)(2,1)S(1)} %pad_maximum_fusion.15), channel_id=1, source_target_pairs={{0,8},{4,20},{8,0},{12,28},{16,24},{20,4},{24,16},{28,12},{1,9},{5... | collective-permute-start | bytes 688136 | tf_op jit(solution)/shard_map/ppermute | solution.py:75
  112.6 12.2 %collective-permute-start.60 = (bf16[4,32,896]{2,1,0:T(8,128)(2,1)S(1)}, bf16[4,32,896]{2,1,0:T(8,128)(2,1)S(1)}, u32[]{:S(2)}, u32[]{:S(2)}) collective-permute-start(bf16[4,32,896]{2,1,0:T(8,128)(2,1)S(1)} %pad_maximum_fusion.15), channel_id=1, source_target_pairs={{0,4},{4,0},{8,12},{12,8},{16,20},{20,16},{24,28},{28,24},{1,5},{5... | collective-permute-start | bytes 688136 | tf_op jit(solution)/shard_map/ppermute | solution.py:75
  118.2 15.9 %collective-permute-start.22 = (bf16[4,32,896]{2,1,0:T(8,128)(2,1)S(1)}, bf16[4,32,896]{2,1,0:T(8,128)(2,1)}, u32[]{:S(2)}, u32[]{:S(2)}) collective-permute-start(bf16[4,32,896]{2,1,0:T(8,128)(2,1)S(1)} %pad_maximum_fusion.14), channel_id=1, source_target_pairs={{0,24},{4,28},{8,16},{12,20},{16,8},{20,12},{24,0},{28,4},{1,25},{... | collective-permute-start | bytes 688136 | tf_op jit(solution)/shard_map/ppermute | solution.py:75
  130.2 23.3 %collective-permute-start.42 = (bf16[4,32,1152]{2,1,0:T(8,128)(2,1)S(1)}, bf16[4,32,1152]{2,1,0:T(8,128)(2,1)}, u32[]{:S(2)}, u32[]{:S(2)}) collective-permute-start(bf16[4,32,1152]{2,1,0:T(8,128)(2,1)S(1)} %pad_maximum_fusion.12), channel_id=1, source_target_pairs={{0,24},{4,28},{8,16},{12,20},{16,8},{20,12},{24,0},{28,4},{1,25},{... | collective-permute-start | bytes 884744 | tf_op jit(solution)/shard_map/ppermute | solution.py:75
  130.6 19.9 %collective-permute-start.41 = (bf16[4,32,1152]{2,1,0:T(8,128)(2,1)S(1)}, bf16[4,32,1152]{2,1,0:T(8,128)(2,1)}, u32[]{:S(2)}, u32[]{:S(2)}) collective-permute-start(bf16[4,32,1152]{2,1,0:T(8,128)(2,1)S(1)} %pad_maximum_fusion.12), channel_id=1, source_target_pairs={{0,8},{4,20},{8,0},{12,28},{16,24},{20,4},{24,16},{28,12},{1,9},{5... | collective-permute-start | bytes 884744 | tf_op jit(solution)/shard_map/ppermute | solution.py:75
  134.1 16.3 %collective-permute-start.40 = (bf16[4,32,1152]{2,1,0:T(8,128)(2,1)S(1)}, bf16[4,32,1152]{2,1,0:T(8,128)(2,1)S(1)}, u32[]{:S(2)}, u32[]{:S(2)}) collective-permute-start(bf16[4,32,1152]{2,1,0:T(8,128)(2,1)S(1)} %pad_maximum_fusion.12), channel_id=1, source_target_pairs={{0,16},{4,12},{8,24},{12,4},{16,0},{20,28},{24,8},{28,20},{1,17},{... | collective-permute-start | bytes 884744 | tf_op jit(solution)/shard_map/ppermute | solution.py:75
  135.8 18.7 %collective-permute-start.43 = (bf16[4,32,1152]{2,1,0:T(8,128)(2,1)S(1)}, bf16[4,32,1152]{2,1,0:T(8,128)(2,1)S(1)}, u32[]{:S(2)}, u32[]{:S(2)}) collective-permute-start(bf16[4,32,1152]{2,1,0:T(8,128)(2,1)S(1)} %pad_maximum_fusion.12), channel_id=1, source_target_pairs={{0,4},{4,0},{8,12},{12,8},{16,20},{20,16},{24,28},{28,24},{1,5},{5... | collective-permute-start | bytes 884744 | tf_op jit(solution)/shard_map/ppermute | solution.py:75
  136.0 22.0 %collective-permute-start.5 = (bf16[4,32,1152]{2,1,0:T(8,128)(2,1)S(1)}, bf16[4,32,1152]{2,1,0:T(8,128)(2,1)S(1)}, u32[]{:S(2)}, u32[]{:S(2)}) collective-permute-start(bf16[4,32,1152]{2,1,0:T(8,128)(2,1)S(1)} %pad_maximum_fusion.11), channel_id=1, source_target_pairs={{0,24},{4,28},{8,16},{12,20},{16,8},{20,12},{24,0},{28,4},{1,25},{... | collective-permute-start | bytes 884744 | tf_op jit(solution)/shard_map/ppermute | solution.py:75
  159.7 407.8 %reduce-scatter.11.cloned.1.call-start = ((), (), s32[]{:S(2)}) async-start(), calls=%async_computation.10 | async-start | bytes 2867200 | tf_op jit(solution)/shard_map/reduce_scatter | solution.py:150
  161.6 97.2 %collective-permute-start.80 = (bf16[160,896]{1,0:T(8,128)(2,1)}, bf16[160,896]{1,0:T(8,128)(2,1)}, u32[]{:S(2)}, u32[]{:S(2)}) collective-permute-start(bf16[160,896]{1,0:T(8,128)(2,1)} %copy-done.104), channel_id=1, source_target_pairs={{0,4},{4,0},{8,12},{12,8},{16,20},{20,16},{24,28},{28,24},{1,5},{5... | collective-permute-start | bytes 860168 | tf_op jit(solution)/shard_map/ppermute | solution.py:75
  163.7 55.4 %collective-permute-start.79 = (bf16[160,896]{1,0:T(8,128)(2,1)}, bf16[160,896]{1,0:T(8,128)(2,1)}, u32[]{:S(2)}, u32[]{:S(2)}) collective-permute-start(bf16[160,896]{1,0:T(8,128)(2,1)} %copy-done.105), channel_id=1, source_target_pairs={{0,4},{4,0},{8,12},{12,8},{16,20},{20,16},{24,28},{28,24},{1,5},{5... | collective-permute-start | bytes 860168 | tf_op jit(solution)/shard_map/ppermute | solution.py:75
  165.4 50.5 %collective-permute-start.78 = (bf16[160,896]{1,0:T(8,128)(2,1)}, bf16[160,896]{1,0:T(8,128)(2,1)}, u32[]{:S(2)}, u32[]{:S(2)}) collective-permute-start(bf16[160,896]{1,0:T(8,128)(2,1)} %copy-done.106), channel_id=1, source_target_pairs={{0,4},{4,0},{8,12},{12,8},{16,20},{20,16},{24,28},{28,24},{1,5},{5... | collective-permute-start | bytes 860168 | tf_op jit(solution)/shard_map/ppermute | solution.py:75
  168.3 96.3 %collective-permute-start.46 = (bf16[4,32,1152]{2,1,0:T(8,128)(2,1)}, bf16[4,32,1152]{2,1,0:T(8,128)(2,1)}, u32[]{:S(2)}, u32[]{:S(2)}) collective-permute-start(bf16[4,32,1152]{2,1,0:T(8,128)(2,1)} %collective-permute-done.42), channel_id=1, source_target_pairs={{0,4},{4,0},{8,12},{12,8},{16,20},{20,16},{24,28},{28,24},{1,5},{5... | collective-permute-start | bytes 884744 | tf_op jit(solution)/shard_map/ppermute | solution.py:75
  198.1 63.5 %collective-permute-start.45 = (bf16[4,32,1152]{2,1,0:T(8,128)(2,1)}, bf16[4,32,1152]{2,1,0:T(8,128)(2,1)}, u32[]{:S(2)}, u32[]{:S(2)}) collective-permute-start(bf16[4,32,1152]{2,1,0:T(8,128)(2,1)} %collective-permute-done.41), channel_id=1, source_target_pairs={{0,4},{4,0},{8,12},{12,8},{16,20},{20,16},{24,28},{28,24},{1,5},{5... | collective-permute-start | bytes 884744 | tf_op jit(solution)/shard_map/ppermute | solution.py:75
  235.2 25.4 %collective-permute-start.44 = (bf16[4,32,1152]{2,1,0:T(8,128)(2,1)S(1)}, bf16[4,32,1152]{2,1,0:T(8,128)(2,1)}, u32[]{:S(2)}, u32[]{:S(2)}) collective-permute-start(bf16[4,32,1152]{2,1,0:T(8,128)(2,1)S(1)} %copy-done.98), channel_id=1, source_target_pairs={{0,4},{4,0},{8,12},{12,8},{16,20},{20,16},{24,28},{28,24},{1,5},{5... | collective-permute-start | bytes 884744 | tf_op jit(solution)/shard_map/ppermute | solution.py:75
  313.5 15.7 %collective-permute-start.66 = (bf16[160,896]{1,0:T(8,128)(2,1)S(1)}, bf16[160,896]{1,0:T(8,128)(2,1)S(1)}, u32[]{:S(2)}, u32[]{:S(2)}) collective-permute-start(bf16[160,896]{1,0:T(8,128)(2,1)S(1)} %get-tuple-element.79), channel_id=1, source_target_pairs={{0,24},{4,28},{8,16},{12,20},{16,8},{20,12},{24,0},{28,4},{1,25},{... | collective-permute-start | bytes 860168 | tf_op jit(solution)/shard_map/ppermute | solution.py:75
  315.2 14.5 %collective-permute-start.65 = (bf16[160,896]{1,0:T(8,128)(2,1)S(1)}, bf16[160,896]{1,0:T(8,128)(2,1)S(1)}, u32[]{:S(2)}, u32[]{:S(2)}) collective-permute-start(bf16[160,896]{1,0:T(8,128)(2,1)S(1)} %get-tuple-element.79), channel_id=1, source_target_pairs={{0,8},{4,20},{8,0},{12,28},{16,24},{20,4},{24,16},{28,12},{1,9},{5... | collective-permute-start | bytes 860168 | tf_op jit(solution)/shard_map/ppermute | solution.py:75
  315.6 14.2 %collective-permute-start.64 = (bf16[160,896]{1,0:T(8,128)(2,1)S(1)}, bf16[160,896]{1,0:T(8,128)(2,1)}, u32[]{:S(2)}, u32[]{:S(2)}) collective-permute-start(bf16[160,896]{1,0:T(8,128)(2,1)S(1)} %get-tuple-element.79), channel_id=1, source_target_pairs={{0,16},{4,12},{8,24},{12,4},{16,0},{20,28},{24,8},{28,20},{1,17},{... | collective-permute-start | bytes 860168 | tf_op jit(solution)/shard_map/ppermute | solution.py:75
  362.9 264.5 %reduce-scatter.15.cloned.1.call-start = ((), (), s32[]{:S(2)}) async-start(), calls=%async_computation.14 | async-start | bytes 1361920
  379.6 14.3 %collective-permute-start.72 = (bf16[2,160,896]{2,1,0:T(8,128)(2,1)S(1)}, bf16[2,160,896]{2,1,0:T(8,128)(2,1)}, u32[]{:S(2)}, u32[]{:S(2)}) collective-permute-start(bf16[2,160,896]{2,1,0:T(8,128)(2,1)S(1)} %slice.1227), channel_id=1, source_target_pairs={{0,8},{4,20},{8,0},{12,28},{16,24},{20,4},{24,16},{28,12},{1,9},{5... | collective-permute-start | bytes 1720328 | tf_op jit(solution)/shard_map/ppermute | solution.py:75
  384.3 243.2 %reduce-scatter.13.cloned.1.call-start = ((), (), s32[]{:S(2)}) async-start(), calls=%async_computation.13 | async-start | bytes 1361920
  430.1 55.9 %collective-permute-start.130 = (bf16[4,128,896]{2,1,0:T(8,128)(2,1)}, bf16[4,128,896]{2,1,0:T(8,128)(2,1)}, u32[]{:S(2)}, u32[]{:S(2)}) collective-permute-start(bf16[4,128,896]{2,1,0:T(8,128)(2,1)} %bitcast.237), channel_id=1, source_target_pairs={{0,4},{4,0},{8,12},{12,8},{16,20},{20,16},{24,28},{28,24},{1,5},{5... | collective-permute-start | bytes 2752520 | tf_op jit(solution)/shard_map/ppermute | solution.py:75
  446.7 41.7 %collective-permute-start.118 = (bf16[4,128,896]{2,1,0:T(8,128)(2,1)}, bf16[4,128,896]{2,1,0:T(8,128)(2,1)}, u32[]{:S(2)}, u32[]{:S(2)}) collective-permute-start(bf16[4,128,896]{2,1,0:T(8,128)(2,1)} %bitcast.227), channel_id=1, source_target_pairs={{0,4},{4,0},{8,12},{12,8},{16,20},{20,16},{24,28},{28,24},{1,5},{5... | collective-permute-start | bytes 2752520 | tf_op jit(solution)/shard_map/ppermute | solution.py:75
  461.7 18.3 %collective-permute-start.89 = (bf16[160,896]{1,0:T(8,128)(2,1)}, bf16[160,896]{1,0:T(8,128)(2,1)S(1)}, u32[]{:S(2)}, u32[]{:S(2)}) collective-permute-start(bf16[160,896]{1,0:T(8,128)(2,1)} %get-tuple-element.76), channel_id=1, source_target_pairs={{0,24},{4,28},{8,16},{12,20},{16,8},{20,12},{24,0},{28,4},{1,25},{... | collective-permute-start | bytes 860168 | tf_op jit(solution)/shard_map/ppermute | solution.py:75
  464.3 17.0 %collective-permute-start.88 = (bf16[160,896]{1,0:T(8,128)(2,1)}, bf16[160,896]{1,0:T(8,128)(2,1)}, u32[]{:S(2)}, u32[]{:S(2)}) collective-permute-start(bf16[160,896]{1,0:T(8,128)(2,1)} %get-tuple-element.76), channel_id=1, source_target_pairs={{0,8},{4,20},{8,0},{12,28},{16,24},{20,4},{24,16},{28,12},{1,9},{5... | collective-permute-start | bytes 860168 | tf_op jit(solution)/shard_map/ppermute | solution.py:75
  464.4 14.0 %collective-permute-start.87 = (bf16[160,896]{1,0:T(8,128)(2,1)}, bf16[160,896]{1,0:T(8,128)(2,1)}, u32[]{:S(2)}, u32[]{:S(2)}) collective-permute-start(bf16[160,896]{1,0:T(8,128)(2,1)} %get-tuple-element.76), channel_id=1, source_target_pairs={{0,16},{4,12},{8,24},{12,4},{16,0},{20,28},{24,8},{28,20},{1,17},{... | collective-permute-start | bytes 860168 | tf_op jit(solution)/shard_map/ppermute | solution.py:75
  481.3 13.5 %collective-permute-start.93 = (bf16[160,896]{1,0:T(8,128)(2,1)}, bf16[160,896]{1,0:T(8,128)(2,1)S(1)}, u32[]{:S(2)}, u32[]{:S(2)}) collective-permute-start(bf16[160,896]{1,0:T(8,128)(2,1)} %copy-done.107), channel_id=1, source_target_pairs={{0,4},{4,0},{8,12},{12,8},{16,20},{20,16},{24,28},{28,24},{1,5},{5... | collective-permute-start | bytes 860168 | tf_op jit(solution)/shard_map/ppermute | solution.py:75
  488.4 46.9 %collective-permute-start.131 = (bf16[2,128,896]{2,1,0:T(8,128)(2,1)}, bf16[2,128,896]{2,1,0:T(8,128)(2,1)}, u32[]{:S(2)}, u32[]{:S(2)}) collective-permute-start(bf16[2,128,896]{2,1,0:T(8,128)(2,1)} %slice.1229), channel_id=1, source_target_pairs={{0,8},{4,20},{8,0},{12,28},{16,24},{20,4},{24,16},{28,12},{1,9},{5... | collective-permute-start | bytes 1376264 | tf_op jit(solution)/shard_map/ppermute | solution.py:75
  491.9 40.8 %collective-permute-start.119 = (bf16[2,128,896]{2,1,0:T(8,128)(2,1)}, bf16[2,128,896]{2,1,0:T(8,128)(2,1)}, u32[]{:S(2)}, u32[]{:S(2)}) collective-permute-start(bf16[2,128,896]{2,1,0:T(8,128)(2,1)} %slice.1231), channel_id=1, source_target_pairs={{0,8},{4,20},{8,0},{12,28},{16,24},{20,4},{24,16},{28,12},{1,9},{5... | collective-permute-start | bytes 1376264 | tf_op jit(solution)/shard_map/ppermute | solution.py:75
  493.4 18.7 %collective-permute-start.107 = (bf16[2,128,384]{2,1,0:T(8,128)(2,1)}, bf16[2,128,384]{2,1,0:T(8,128)(2,1)}, u32[]{:S(2)}, u32[]{:S(2)}) collective-permute-start(bf16[2,128,384]{2,1,0:T(8,128)(2,1)} %slice.1235), channel_id=1, source_target_pairs={{0,8},{4,20},{8,0},{12,28},{16,24},{20,4},{24,16},{28,12},{1,9},{5... | collective-permute-start | bytes 589832 | tf_op jit(solution)/shard_map/ppermute | solution.py:75
  504.8 165.1 %reduce-scatter.9.cloned.1.call-start = ((), (), s32[]{:S(2)}) async-start(), calls=%async_computation.9 | async-start | bytes 2867200 | tf_op jit(solution)/shard_map/reduce_scatter | solution.py:150
  518.2 13.6 %collective-permute-start.109 = (bf16[32,384]{1,0:T(8,128)(2,1)S(1)}, bf16[32,384]{1,0:T(8,128)(2,1)S(1)}, u32[]{:S(2)}, u32[]{:S(2)}) collective-permute-start(bf16[32,384]{1,0:T(8,128)(2,1)S(1)} %get-tuple-element.155), channel_id=1, source_target_pairs={{0,1},{1,0},{2,3},{3,2},{4,5},{5,4},{6,7},{7,6},{8,9},{9,8},{10,11... | collective-permute-start | bytes 73736 | tf_op jit(solution)/shard_map/ppermute | solution.py:80
  518.3 13.6 %collective-permute-start.111 = (bf16[32,384]{1,0:T(8,128)(2,1)S(1)}, bf16[32,384]{1,0:T(8,128)(2,1)S(1)}, u32[]{:S(2)}, u32[]{:S(2)}) collective-permute-start(bf16[32,384]{1,0:T(8,128)(2,1)S(1)} %get-tuple-element.156), channel_id=1, source_target_pairs={{0,3},{1,2},{2,1},{3,0},{4,7},{5,6},{6,5},{7,4},{8,11},{9,10},{10,... | collective-permute-start | bytes 73736 | tf_op jit(solution)/shard_map/ppermute | solution.py:80
  531.8 12.1 %collective-permute-start.94 = (bf16[4,160,896]{2,1,0:T(8,128)(2,1)}, bf16[4,160,896]{2,1,0:T(8,128)(2,1)S(1)}, u32[]{:S(2)}, u32[]{:S(2)}) collective-permute-start(bf16[4,160,896]{2,1,0:T(8,128)(2,1)} %bitcast.189), channel_id=1, source_target_pairs={{0,4},{4,0},{8,12},{12,8},{16,20},{20,16},{24,28},{28,24},{1,5},{5... | collective-permute-start | bytes 3440648 | tf_op jit(solution)/shard_map/ppermute | solution.py:75
  543.4 15.4 %collective-permute-start.122 = (bf16[32,896]{1,0:T(8,128)(2,1)S(1)}, bf16[32,896]{1,0:T(8,128)(2,1)S(1)}, u32[]{:S(2)}, u32[]{:S(2)}) collective-permute-start(bf16[32,896]{1,0:T(8,128)(2,1)S(1)} %get-tuple-element.139), channel_id=1, source_target_pairs={{0,2},{1,3},{2,0},{3,1},{4,6},{5,7},{6,4},{7,5},{8,10},{9,11},{10,... | collective-permute-start | bytes 172040 | tf_op jit(solution)/shard_map/ppermute | solution.py:80
  544.2 15.3 %collective-permute-start.95 = (bf16[2,160,896]{2,1,0:T(8,128)(2,1)S(1)}, bf16[2,160,896]{2,1,0:T(8,128)(2,1)S(1)}, u32[]{:S(2)}, u32[]{:S(2)}) collective-permute-start(bf16[2,160,896]{2,1,0:T(8,128)(2,1)S(1)} %slice.1225), channel_id=1, source_target_pairs={{0,8},{4,20},{8,0},{12,28},{16,24},{20,4},{24,16},{28,12},{1,9},{5... | collective-permute-start | bytes 1720328 | tf_op jit(solution)/shard_map/ppermute | solution.py:75
  545.1 14.8 %collective-permute-start.133 = (bf16[32,896]{1,0:T(8,128)(2,1)S(1)}, bf16[32,896]{1,0:T(8,128)(2,1)S(1)}, u32[]{:S(2)}, u32[]{:S(2)}) collective-permute-start(bf16[32,896]{1,0:T(8,128)(2,1)S(1)} %get-tuple-element.131), channel_id=1, source_target_pairs={{0,1},{1,0},{2,3},{3,2},{4,5},{5,4},{6,7},{7,6},{8,9},{9,8},{10,11... | collective-permute-start | bytes 172040 | tf_op jit(solution)/shard_map/ppermute | solution.py:80
  549.9 16.9 %collective-permute-start.134 = (bf16[32,896]{1,0:T(8,128)(2,1)S(1)}, bf16[32,896]{1,0:T(8,128)(2,1)S(1)}, u32[]{:S(2)}, u32[]{:S(2)}) collective-permute-start(bf16[32,896]{1,0:T(8,128)(2,1)S(1)} %get-tuple-element.133), channel_id=1, source_target_pairs={{0,2},{1,3},{2,0},{3,1},{4,6},{5,7},{6,4},{7,5},{8,10},{9,11},{10,... | collective-permute-start | bytes 172040 | tf_op jit(solution)/shard_map/ppermute | solution.py:80
  598.3 39.8 %collective-permute-start.124 = (bf16[4,128,896]{2,1,0:T(8,128)(2,1)}, bf16[4,128,896]{2,1,0:T(8,128)(2,1)}, u32[]{:S(2)}, u32[]{:S(2)}) collective-permute-start(bf16[4,128,896]{2,1,0:T(8,128)(2,1)} %bitcast.232), channel_id=1, source_target_pairs={{0,4},{4,0},{8,12},{12,8},{16,20},{20,16},{24,28},{28,24},{1,5},{5... | collective-permute-start | bytes 2752520 | tf_op jit(solution)/shard_map/ppermute | solution.py:75
  627.0 19.1 %collective-permute-start.112 = (bf16[4,128,896]{2,1,0:T(8,128)(2,1)}, bf16[4,128,896]{2,1,0:T(8,128)(2,1)}, u32[]{:S(2)}, u32[]{:S(2)}) collective-permute-start(bf16[4,128,896]{2,1,0:T(8,128)(2,1)} %bitcast.222), channel_id=1, source_target_pairs={{0,4},{4,0},{8,12},{12,8},{16,20},{20,16},{24,28},{28,24},{1,5},{5... | collective-permute-start | bytes 2752520 | tf_op jit(solution)/shard_map/ppermute | solution.py:75
  639.5 12.1 %collective-permute-start.125 = (bf16[2,128,896]{2,1,0:T(8,128)(2,1)S(1)}, bf16[2,128,896]{2,1,0:T(8,128)(2,1)S(1)}, u32[]{:S(2)}, u32[]{:S(2)}) collective-permute-start(bf16[2,128,896]{2,1,0:T(8,128)(2,1)S(1)} %slice.1230), channel_id=1, source_target_pairs={{0,8},{4,20},{8,0},{12,28},{16,24},{20,4},{24,16},{28,12},{1,9},{5... | collective-permute-start | bytes 1376264 | tf_op jit(solution)/shard_map/ppermute | solution.py:75
  647.5 12.2 %collective-permute-start.113 = (bf16[2,128,896]{2,1,0:T(8,128)(2,1)S(1)}, bf16[2,128,896]{2,1,0:T(8,128)(2,1)S(1)}, u32[]{:S(2)}, u32[]{:S(2)}) collective-permute-start(bf16[2,128,896]{2,1,0:T(8,128)(2,1)S(1)} %slice.1232), channel_id=1, source_target_pairs={{0,8},{4,20},{8,0},{12,28},{16,24},{20,4},{24,16},{28,12},{1,9},{5... | collective-permute-start | bytes 1376264 | tf_op jit(solution)/shard_map/ppermute | solution.py:75
  666.3 11.7 %collective-permute-start.115 = (bf16[32,896]{1,0:T(8,128)(2,1)S(1)}, bf16[32,896]{1,0:T(8,128)(2,1)S(1)}, u32[]{:S(2)}, u32[]{:S(2)}) collective-permute-start(bf16[32,896]{1,0:T(8,128)(2,1)S(1)} %get-tuple-element.134), channel_id=1, source_target_pairs={{0,1},{1,0},{2,3},{3,2},{4,5},{5,4},{6,7},{7,6},{8,9},{9,8},{10,11... | collective-permute-start | bytes 172040 | tf_op jit(solution)/shard_map/ppermute | solution.py:80
  673.4 20.1 %all-to-all-start.2 = ((bf16[8,2,28,1280]{3,1,2,0:T(2,128)(2,1)}), bf16[8,2,28,1280]{3,1,2,0:T(2,128)(2,1)S(1)}, u32[]{:S(2)}, u32[]{:S(2)}) async-start(bf16[8,2,28,1280]{3,1,2,0:T(2,128)(2,1)} %copy.165), calls=%async_computation.4 | async-start | bytes 2293760 | tf_op jit(solution)/shard_map/all_to_all | solution.py:154
  (240 other events, 2109.7 us)
Sparse Core Ops, SparseCore 0:
  32.1 63.4 all-gather.7
  97.2 28.5 all-gather.11
  127.3 28.0 all-gather.13
  159.8 49.8 all-gather.9
  363.1 45.9 reduce-scatter.10
  411.9 26.9 reduce-scatter.14
  504.9 27.6 reduce-scatter.12
  535.1 53.0 reduce-scatter.8

commit v2 on v1

v2 whole, which is shorter than its diff:
```python
import functools
import math

import jax
import jax.numpy as jnp
from jax import lax
from jax.experimental import pallas as pl
from jax.experimental.pallas import tpu as pltpu
from jax.sharding import PartitionSpec as P

HEADS = 14
KV_HEADS = 2
GROUP = HEADS // KV_HEADS
HEAD = 64
FF = 4864
LAYERS = 2
QW = 896
D = 896
QKV_W = 1152
KV_W = KV_HEADS * HEAD

EPSILON = 1e-06
ROPE_BASE = 1000000.0
NEGATIVE = -1e30
SCALE = HEAD**-0.5

bf16 = jnp.bfloat16
f32 = jnp.float32

ANY = pl.BlockSpec(memory_space=pl.ANY)
VMEM = pl.BlockSpec(memory_space=pltpu.VMEM)
DMA = pltpu.SemaphoreType.DMA


def shape(dims, dtype):
    return jax.ShapeDtypeStruct(dims, dtype)


def dot(left, right):
    return jnp.dot(left, right, preferred_element_type=f32)


def dot_rows(left, right):
    return lax.dot_general(left, right, (((0,), (0,)), ((), ())), preferred_element_type=f32)


def dot_cols(left, right):
    return lax.dot_general(left, right, (((1,), (1,)), ((), ())), preferred_element_type=f32)


def run(kernel, ins, in_specs, outs, out_specs, scratch, flops, vmem=60):
    moved = sum(math.prod(x.shape) * x.dtype.itemsize for x in [*ins, *outs])
    return pl.pallas_call(
        kernel,
        out_shape=outs,
        in_specs=in_specs,
        out_specs=out_specs,
        scratch_shapes=scratch,
        compiler_params=pltpu.CompilerParams(vmem_limit_bytes=vmem * 2**20),
        cost_estimate=pl.CostEstimate(flops=flops, bytes_accessed=moved, transcendentals=0),
    )(*ins)


def copies(sources, targets, sems):
    made = [pltpu.make_async_copy(s, t, sems.at[i]) for i, (s, t) in enumerate(zip(sources, targets))]
    for c in made:
        c.start()
    return made


def rows_of(ref, count, size):
    return [ref.at[pl.ds(i * size, size)] for i in range(count)]


class Blocks:
    def __init__(self, arrays, places):
        self.arrays, self.places = arrays, places

    def take(self, it):
        refs = [next(it) for _ in self.arrays]
        return [refs[a].at[b] for a, b in self.places]


def turned(block):
    lane = lax.broadcasted_iota(jnp.int32, block.shape, 1)
    return jnp.where(lane % HEAD < HEAD // 2, -pltpu.roll(block, 96, 1), pltpu.roll(block, 32, 1))


def rotated(block, cos, sin):
    return block * cos + turned(block) * sin


def rotated_back(block, cos, sin):
    return block * cos - turned(block) * sin


def inverse_norm(hidden):
    return lax.rsqrt(jnp.mean(hidden * hidden, axis=-1, keepdims=True) + EPSILON)


def norm_back(normed_grad, hidden, gain):
    inverse = inverse_norm(hidden)
    scaled = normed_grad * gain
    inner = jnp.mean(scaled * hidden, axis=-1, keepdims=True)
    into = inverse * scaled - hidden * (inverse * inverse * inverse * inner)
    return into, jnp.sum(normed_grad * (hidden * inverse), axis=0, keepdims=True)


def split_dot_cols(value, right):
    high = value.astype(bf16)
    low = (value - high.astype(f32)).astype(bf16)
    return dot_cols(high, right) + dot_cols(low, right)


def first_row(row):
    return jnp.broadcast_to(row, (8, row.shape[1]))


def before_attention(cfg, base, sums, perm, cos, sin, blocks, places=None):
    n, m, rows, pad_rows = cfg
    tokens, step = base.shape[0], m * pad_rows
    all_rows = n * step
    more = [] if places is None else [places]

    def kernel(*refs):
        it = iter(refs)
        more_refs = [next(it) for _ in more]
        base_ref = next(it)
        sum_refs = [next(it) for _ in sums]
        perm_ref, cos_ref, sin_ref = next(it), next(it), next(it)
        block_refs = blocks.take(it)
        hidden_ref, rel_ref, query_ref, kv_ref, gain_ref, weight, sems = it
        waits = copies(
            [b.at[:, pl.ds(0, QKV_W)] for b in block_refs], rows_of(weight, n, step), sems
        )
        hidden = base_ref[...].astype(f32)
        for ref in sum_refs:
            hidden = hidden + ref[...].astype(f32)
        hidden_ref[...] = hidden
        scaled = hidden * inverse_norm(hidden)
        cos, sin = cos_ref[...], sin_ref[...]
        for w in waits:
            w.wait()
        last = jnp.zeros((16, QKV_W), f32)
        for i in range(n * m):
            last = last + weight[pl.ds((i + 1) * pad_rows - 16, 16), :].astype(f32)
        at = rows + 1 - (pad_rows - 16)
        gain_ref[0:8, :] = first_row(last[at : at + 1, :D])
        gain_ref[8:16, :] = first_row(last[at + 1 : at + 2, :D])
        normed = (scaled * last[at : at + 1, :D]).astype(bf16)
        rel = dot(normed, perm_ref[...])
        lane = lax.broadcasted_iota(jnp.int32, rel.shape, 1)
        rel = jnp.where(lane % pad_rows == rows, 1.0, rel).astype(bf16)
        rel_ref[...] = rel
        kv = dot(rel, weight[:, QW:])
        kv_ref[:, :KV_W] = rotated(kv[:, :KV_W], cos, sin).astype(bf16)
        kv_ref[:, KV_W : 2 * KV_W] = kv[:, KV_W:].astype(bf16)
        for ref in more_refs:
            kv_ref[:, 2 * KV_W :] = ref[...]
        query = dot(rel, weight[:, :QW])
        for i in range(QW // 128):
            part = rotated(query[:, i * 128 : (i + 1) * 128], cos, sin).astype(bf16)
            query_ref[:, i * 128 : (i + 1) * 128] = part * SCALE

    ins = [*more, base, *sums, perm, cos, sin]
    return run(
        kernel,
        [*ins, *blocks.arrays],
        [VMEM] * len(ins) + [ANY] * len(blocks.arrays),
        [
            shape((tokens, D), f32),
            shape((tokens, all_rows), bf16),
            shape((tokens, QW), bf16),
            shape((tokens, 2 * KV_W + 128 * len(more)), bf16),
            shape((16, D), f32),
        ],
        [VMEM] * 5,
        [pltpu.VMEM((all_rows, QKV_W), bf16), DMA((n,))],
        2 * tokens * all_rows * (D + QKV_W),
    )


def kv_copies(n, tokens, kv_refs, place_refs, kv, place, sems):
    return copies(
        [
            *[r.at[:, pl.ds(0, 2 * KV_W)] for r in kv_refs],
            *[r.at[:, pl.ds(2 * KV_W, 128)] for r in place_refs],
        ],
        [*rows_of(kv, n, tokens), *rows_of(place, n, tokens)],
        sems,
    )


def place_column(place, at):
    block = place[at, :].astype(f32)
    return (block[:, 0:1] * 256.0 + block[:, 1:2]).astype(jnp.int32)


def heads_to_lanes(matrix, group, tokens):
    parts = [
        matrix[(group * GROUP + h) * HEAD : (group * GROUP + h + 1) * HEAD, :] for h in range(GROUP)
    ]
    return jnp.concatenate(parts, axis=1)


def lanes_to_heads(groups, tokens):
    parts = [g[:, h * tokens : (h + 1) * tokens] for g in groups for h in range(GROUP)]
    return jnp.concatenate(parts, axis=0).T


def heads_to_rows(matrix, group):
    parts = [
        matrix[:, (group * GROUP + h) * HEAD : (group * GROUP + h + 1) * HEAD] for h in range(GROUP)
    ]
    return jnp.concatenate(parts, axis=0)


def attention(
    cfg, query, kv_blocks, own_row, place_blocks, hidden, gain, perm, perm2, out_blocks, out_at
):
    n, m, rows, pad_rows = cfg
    tokens, step = query.shape[0], m * pad_rows
    all_rows, wide = n * step, GROUP * query.shape[0]
    slots = KV_HEADS if n <= 8 else 1

    def kernel(*refs):
        it = iter(refs)
        query_ref = next(it)
        kv_refs = [next(it) for _ in range(n)]
        place_refs = [next(it) for _ in range(n)]
        row_ref, hidden_ref, gain_ref, perm_in, perm2_in = [next(it) for _ in range(5)]
        out_refs = out_blocks.take(it)
        middle_ref, normed_ref, rel_ref, mix_ref, lse_ref, turn_ref = [next(it) for _ in range(6)]
        kv, place, values_t, scores = [next(it) for _ in range(4)]
        probs = next(it) if slots > 1 else None
        perm_v, perm2_v, weight, kv_sems, sems = it
        kv_waits = kv_copies(n, tokens, kv_refs, place_refs, kv, place, kv_sems)
        waits = copies(
            [perm_in, perm2_in, *[o.at[:, pl.ds(out_at, D)] for o in out_refs]],
            [perm_v, perm2_v, *rows_of(weight, n, step)],
            sems,
        )
        query_t = query_ref[...].astype(f32).T
        for w in kv_waits:
            w.wait()
        for g in range(KV_HEADS):
            turn_ref[g * HEAD : (g + 1) * HEAD, :] = heads_to_lanes(query_t, g, tokens).astype(bf16)

        if probs is None:
            for j in range(n):
                block = kv[pl.ds(j * tokens, tokens), KV_W:]
                values_t[j] = block.astype(f32).T.astype(bf16)
        else:
            values_t[...] = kv[:, KV_W:].astype(f32).T.astype(bf16)
        own = row_ref[...]
        mixed = []
        for g in range(KV_HEADS):
            turn = turn_ref[g * HEAD : (g + 1) * HEAD, :]
            top = jnp.full((1, wide), NEGATIVE, f32)
            for j in range(n):
                at = pl.ds(j * tokens, tokens)
                s = dot(kv[at, g * HEAD : (g + 1) * HEAD], turn)
                s = jnp.where(place_column(place, at) <= own, s, NEGATIVE)
                scores[g % slots, at, :] = s
                top = jnp.maximum(top, jnp.max(s, axis=0, keepdims=True))
            total = jnp.zeros((1, wide), f32)
            out = jnp.zeros((HEAD, wide), f32)
            for j in range(n):
                at = pl.ds(j * tokens, tokens)
                p = jnp.exp(scores[g % slots, at, :] - top)
                total = total + jnp.sum(p, axis=0, keepdims=True)
                if probs is None:
                    out = out + dot(values_t[j, g * HEAD : (g + 1) * HEAD, :], p.astype(bf16))
                else:
                    probs[g, at, :] = p.astype(bf16)
            if probs is not None:
                out = dot(values_t[g * HEAD : (g + 1) * HEAD, :], probs[g])
            out = out / total
            mix_ref[g * HEAD : (g + 1) * HEAD, :] = out
            lse_ref[g * 8 : (g + 1) * 8, :] = first_row(top + jnp.log(total))
            mixed.append(out)
        heads = lanes_to_heads(mixed, tokens).astype(bf16)
        for w in waits:
            w.wait()
        rel = dot(heads, perm_v[...]).astype(bf16)
        rel_ref[...] = rel
        middle = hidden_ref[...] + dot(rel, weight[...])
        middle_ref[...] = middle
        normed = (middle * inverse_norm(middle) * gain_ref[8:9, :]).astype(bf16)
        normed_ref[...] = dot(normed, perm2_v[...]).astype(bf16)

    return run(
        kernel,
        [query, *kv_blocks, *place_blocks, own_row, hidden, gain, perm, perm2, *out_blocks.arrays],
        [VMEM] + [ANY] * (2 * n) + [VMEM] * 3 + [ANY] * (len(out_blocks.arrays) + 2),
        [
            shape((tokens, D), f32),
            shape((tokens, D), bf16),
            shape((tokens, all_rows), bf16),
            shape((KV_W, wide), f32),
            shape((16, wide), f32),
            shape((KV_W, wide), bf16),
        ],
        [VMEM] * 6,
        [
            pltpu.VMEM((n * tokens, 2 * KV_W), bf16),
            pltpu.VMEM((n * tokens, 128), bf16),
            pltpu.VMEM((KV_W, n * tokens) if slots > 1 else (n, KV_W, tokens), bf16),
            pltpu.VMEM((slots, n * tokens, wide), f32),
            *([pltpu.VMEM((slots, n * tokens, wide), bf16)] if slots > 1 else []),
            pltpu.VMEM((D, all_rows), bf16),
            pltpu.VMEM((D, D), bf16),
            pltpu.VMEM((all_rows, D), bf16),
            DMA((2 * n,)),
            DMA((n + 2,)),
        ],
        8 * tokens * n * tokens * QW,
        60,
    )


def middle_back(cfg, sums, middle, gradient, gain, perm, perm2, out_blocks, out_at):
    n, m, rows, pad_rows = cfg
    tokens, step = middle.shape[0], m * pad_rows
    all_rows = n * step

    def kernel(*refs):
        it = iter(refs)
        sum_refs = [next(it), next(it)]
        middle_ref, grad_ref, gain_ref, perm_in, perm2_ref = [next(it) for _ in range(5)]
        out_refs = out_blocks.take(it)
        mgrad_ref, low_ref, gain_grad_ref, heads_ref = [next(it) for _ in range(4)]
        perm_v, weight, sems = it
        waits = copies(
            [perm_in, *[o.at[:, pl.ds(out_at, D)] for o in out_refs]],
            [perm_v, *rows_of(weight, n, step)],
            sems,
        )
        normed_grad = split_dot_cols(
            sum_refs[0][...] + sum_refs[1][...].astype(f32), perm2_ref[...]
        )
        into, gain_grad = norm_back(normed_grad, middle_ref[...], gain_ref[8:9, :])
        middle_grad = grad_ref[...].astype(f32) + into
        mgrad_ref[...] = middle_grad
        gain_grad_ref[...] = first_row(gain_grad)
        low = middle_grad.astype(bf16)
        low_ref[...] = low
        for w in waits:
            w.wait()
        heads_rel = dot_cols(low, weight[...]).astype(bf16)
        heads_ref[...] = dot_cols(heads_rel, perm_v[...]).astype(bf16)

    return run(
        kernel,
        [*sums, middle, gradient, gain, perm, perm2, *out_blocks.arrays],
        [VMEM] * 5 + [ANY] + [VMEM] + [ANY] * len(out_blocks.arrays),
        [
            shape((tokens, D), f32),
            shape((tokens, D), bf16),
            shape((8, D), f32),
            shape((tokens, QW), bf16),
        ],
        [VMEM] * 4,
        [pltpu.VMEM((D, all_rows), bf16), pltpu.VMEM((all_rows, D), bf16), DMA((n + 1,))],
        2 * tokens * D * (2 * D + 2 * all_rows),
    )


def attention_back(
    cfg, heads_grad, mix, lse, turn, query, kv_blocks, own_row, place_blocks, cos, sin
):
    n, m, rows, pad_rows = cfg
    tokens, half = query.shape[0], n // 2
    wide = GROUP * query.shape[0]

    def kernel(*refs):
        it = iter(refs)
        heads_ref, mix_ref, lse_ref, turn_ref, query_ref = [next(it) for _ in range(5)]
        kv_refs = [next(it) for _ in range(n)]
        place_refs = [next(it) for _ in range(n)]
        row_ref, cos_ref, sin_ref = [next(it) for _ in range(3)]
        keep_ref, send_ref, part_ref = [next(it) for _ in range(3)]
        kv, place, keys_t, probs, score_grads, kv_sems = it
        kv_waits = kv_copies(n, tokens, kv_refs, place_refs, kv, place, kv_sems)
        heads = heads_ref[...]
        heads_t = heads.astype(f32).T
        for w in kv_waits:
            w.wait()
        keys_t[...] = kv[:, :KV_W].astype(f32).T.astype(bf16)
        own = row_ref[...]
        query = query_ref[...]
        sides = []
        for g in range(KV_HEADS):
            grad_t = heads_to_lanes(heads_t, g, tokens)
            inner = jnp.sum(mix_ref[g * HEAD : (g + 1) * HEAD, :] * grad_t, axis=0, keepdims=True)
            sides.append(
                (
                    turn_ref[g * HEAD : (g + 1) * HEAD, :],
                    heads_to_rows(query, g),
                    grad_t.astype(bf16),
                    heads_to_rows(heads, g),
                    inner,
                    lse_ref[g * 8 : g * 8 + 1, :],
                )
            )
        wholes = []
        for g, (turn, query_rows, grad_t, grad_rows, inner, lse) in enumerate(sides):
            for j in range(n):
                at = pl.ds(j * tokens, tokens)
                s = dot(kv[at, g * HEAD : (g + 1) * HEAD], turn)
                p = jnp.exp(jnp.where(place_column(place, at) <= own, s, NEGATIVE) - lse)
                prob_grad = dot(kv[at, KV_W + g * HEAD : KV_W + (g + 1) * HEAD], grad_t)
                probs[at, :] = p.astype(bf16)
                score_grads[at, :] = (p * (prob_grad - inner)).astype(bf16)
            for part, ref in enumerate([keep_ref, send_ref]):
                at = pl.ds(part * half * tokens, half * tokens)
                key_out = dot(score_grads[at, :], query_rows).astype(bf16)
                value_out = dot(probs[at, :], grad_rows).astype(bf16)
                ref[:, g * HEAD : (g + 1) * HEAD] = key_out
                ref[:, KV_W + g * HEAD : KV_W + (g + 1) * HEAD] = value_out
            wholes.append(dot(keys_t[g * HEAD : (g + 1) * HEAD, :], score_grads[...]))
        whole = lanes_to_heads(wholes, tokens) * SCALE
        cos, sin = cos_ref[...], sin_ref[...]
        for i in range(QW // 128):
            at = slice(i * 128, (i + 1) * 128)
            part_ref[:, at] = rotated_back(whole[:, at], cos, sin).astype(bf16)

    return run(
        kernel,
        [heads_grad, mix, lse, turn, query, *kv_blocks, *place_blocks, own_row, cos, sin],
        [VMEM] * 5 + [ANY] * (2 * n) + [VMEM] * 3,
        [
            shape((half * tokens, 2 * KV_W), bf16),
            shape((half * tokens, 2 * KV_W), bf16),
            shape((tokens, QW), bf16),
        ],
        [VMEM] * 3,
        [
            pltpu.VMEM((n * tokens, 2 * KV_W), bf16),
            pltpu.VMEM((n * tokens, 128), bf16),
            pltpu.VMEM((KV_W, n * tokens), bf16),
            pltpu.VMEM((n * tokens, wide), bf16),
            pltpu.VMEM((n * tokens, wide), bf16),
            DMA((2 * n,)),
        ],
        20 * tokens * n * tokens * QW,
        60,
    )


def query_back(cfg, query_part, blocks):
    n, m, rows, pad_rows = cfg
    tokens, step = query_part.shape[0], m * pad_rows

    def kernel(*refs):
        it = iter(refs)
        part_ref, block_refs = next(it), blocks.take(it)
        out_ref, weight, sems = it
        waits = copies(
            [b.at[:, pl.ds(0, QW)] for b in block_refs], rows_of(weight, n, step), sems
        )
        for w in waits:
            w.wait()
        out_ref[...] = dot_cols(part_ref[...], weight[...])

    return run(
        kernel,
        [query_part, *blocks.arrays],
        [VMEM] + [ANY] * len(blocks.arrays),
        [shape((tokens, n * step), f32)],
        [VMEM],
        [pltpu.VMEM((n * step, QW), bf16), DMA((n,))],
        2 * tokens * n * step * QW,
    )[0]


def layer_back(cfg, sums, query_rel, hidden, middle_grad, gain, cos, sin, perm, blocks):
    n, m, rows, pad_rows = cfg
    tokens, step = hidden.shape[0], m * pad_rows

    def kernel(*refs):
        it = iter(refs)
        sum_refs = [next(it), next(it)]
        rel_ref, hidden_ref, mgrad_ref, gain_ref, cos_ref, sin_ref, perm_ref = [
            next(it) for _ in range(7)
        ]
        block_refs = blocks.take(it)
        grad_ref, low_ref, part_ref, gain_grad_ref, weight, sems = it
        waits = copies(
            [b.at[:, pl.ds(QW, 2 * KV_W)] for b in block_refs], rows_of(weight, n, step), sems
        )
        total = sum_refs[0][...] + sum_refs[1][...].astype(f32)
        keys = rotated_back(total[:, :KV_W], cos_ref[...], sin_ref[...])
        part = jnp.concatenate([keys, total[:, KV_W:]], axis=1).astype(bf16)
        part_ref[...] = part
        for w in waits:
            w.wait()
        rel = rel_ref[...] + dot_cols(part, weight[...])
        normed_grad = split_dot_cols(rel, perm_ref[...])
        into, gain_grad = norm_back(normed_grad, hidden_ref[...], gain_ref[0:1, :])
        gradient = mgrad_ref[...] + into
        grad_ref[...] = gradient
        low_ref[...] = gradient.astype(bf16)
        gain_grad_ref[...] = first_row(gain_grad)

    return run(
        kernel,
        [*sums, query_rel, hidden, middle_grad, gain, cos, sin, perm, *blocks.arrays],
        [VMEM] * 9 + [ANY] * len(blocks.arrays),
        [
            shape((tokens, D), f32),
            shape((tokens, D), bf16),
            shape((tokens, 2 * KV_W), bf16),
            shape((8, D), f32),
        ],
        [VMEM] * 4,
        [pltpu.VMEM((n * step, 2 * KV_W), bf16), DMA((n,))],
        2 * tokens * n * step * (2 * KV_W + 2 * D),
    )


def gated(gate, up):
    return gate * jax.nn.sigmoid(gate) * up


def gated_back(act_grad, gate, up):
    sig = jax.nn.sigmoid(gate)
    gate_grad = act_grad * up * (sig * (1.0 + gate * (1.0 - sig)))
    return gate_grad, act_grad * (gate * sig)


def feed_forward(x_blocks, in_proj, down_proj):
    n, tokens, units, width = len(x_blocks), x_blocks[0].shape[0], down_proj.shape[0], in_proj.shape[1]
    half, pad, total = n // 2, width // 2, n * tokens

    def kernel(*refs):
        x_refs, (in_ref, down_ref) = refs[:n], refs[n : n + 2]
        keep_ref, send_ref, all_ref, unit_ref, act_ref = refs[n + 2 : n + 7]
        x, w_in, w_down, units_v, act_v, terms, x_sems, w_sems, o_sems = refs[n + 7 :]
        in_wait, down_wait = copies([in_ref, down_ref], [w_in, w_down.at[pl.ds(0, units)]], w_sems)
        x_waits = copies(x_refs, rows_of(x, n, tokens), x_sems)
        if pad > units:
            w_down[units:, :] = jnp.zeros((pad - units, D), bf16)
        in_wait.wait()
        down_wait.wait()
        outs = []

        def put(src, dst, slot):
            copy = pltpu.make_async_copy(src, dst, o_sems.at[slot])
            copy.start()
            outs.append(copy)

        big = half * tokens
        for i, (part, target) in enumerate([(1, send_ref), (0, keep_ref)]):
            at = pl.ds(part * big, big)
            for w in x_waits[part * half : (part + 1) * half]:
                w.wait()
            put(x.at[at], all_ref.at[at], 4 * i)
            both = dot(x[at, :], w_in[...])
            units_v[at, :] = both.astype(bf16)
            put(units_v.at[at], unit_ref.at[at], 4 * i + 1)
            act = gated(both[:, :pad], both[:, pad:]).astype(bf16)
            act_v[at, :] = act
            put(act_v.at[at], act_ref.at[at], 4 * i + 2)
            terms[part] = dot(act, w_down[...]).astype(bf16)
            put(terms.at[part], target, 4 * i + 3)
        for copy in outs:
            copy.wait()

    return run(
        kernel,
        [*x_blocks, in_proj, down_proj],
        [ANY] * (n + 2),
        [
            shape((half * tokens, D), bf16),
            shape((half * tokens, D), bf16),
            shape((total, D), bf16),
            shape((total, width), bf16),
            shape((total, pad), bf16),
        ],
        [ANY] * 5,
        [
            pltpu.VMEM((total, D), bf16),
            pltpu.VMEM((D, width), bf16),
            pltpu.VMEM((pad, D), bf16),
            pltpu.VMEM((total, width), bf16),
            pltpu.VMEM((total, pad), bf16),
            pltpu.VMEM((2, half * tokens, D), bf16),
            DMA((n,)),
            DMA((2,)),
            DMA((8,)),
        ],
        2 * total * D * (width + pad),
        60,
    )


def feed_forward_back(x_blocks, units_all, grad_blocks, in_proj, down_proj):
    n, tokens = len(grad_blocks), grad_blocks[0].shape[0]
    units, width = down_proj.shape[0], in_proj.shape[1]
    half, pad, total = n // 2, width // 2, n * tokens
    fresh = units_all is None

    def kernel(*refs):
        it = iter(refs)
        x_refs = [next(it) for _ in range(n)] if fresh else []
        unit_ref = None if fresh else next(it)
        g_refs = [next(it) for _ in range(n)]
        in_ref, down_ref = next(it), next(it)
        keep_ref, send_ref, gall_ref, ugrad_ref = [next(it) for _ in range(4)]
        all_ref, act_ref = (next(it), next(it)) if fresh else (None, None)
        g, w_in, w_down, ugrad, terms = [next(it) for _ in range(5)]
        x, act_v = (next(it), next(it)) if fresh else (None, None)
        units_v = None if fresh else next(it)
        g_sems, w_sems, o_sems, x_sems = it
        in_wait, down_wait = copies([in_ref, down_ref], [w_in, w_down.at[pl.ds(0, units)]], w_sems)
        g_waits = copies(g_refs, rows_of(g, n, tokens), g_sems)
        if fresh:
            x_waits = copies(x_refs, rows_of(x, n, tokens), x_sems)
        else:
            x_waits = copies(rows_of(unit_ref, n, tokens), rows_of(units_v, n, tokens), x_sems)
        if pad > units:
            w_down[units:, :] = jnp.zeros((pad - units, D), bf16)
        in_wait.wait()
        down_wait.wait()
        outs = []

        def put(src, dst, slot):
            copy = pltpu.make_async_copy(src, dst, o_sems.at[slot])
            copy.start()
            outs.append(copy)

        big = half * tokens
        for i, (part, target) in enumerate([(1, send_ref), (0, keep_ref)]):
            at = pl.ds(part * big, big)
            for w in x_waits[part * half : (part + 1) * half]:
                w.wait()
            if fresh:
                put(x.at[at], all_ref.at[at], 5 * i)
                both = dot(x[at, :], w_in[...])
                gate, up = both[:, :pad], both[:, pad:]
                act_v[at, :] = gated(gate, up).astype(bf16)
                put(act_v.at[at], act_ref.at[at], 5 * i + 1)
            else:
                gate, up = units_v[at, :pad].astype(f32), units_v[at, pad:].astype(f32)
            for w in g_waits[part * half : (part + 1) * half]:
                w.wait()
            put(g.at[at], gall_ref.at[at], 5 * i + 2)
            gate_grad, up_grad = gated_back(dot_cols(g[at, :], w_down[...]), gate, up)
            ugrad[at, :pad] = gate_grad.astype(bf16)
            ugrad[at, pad:] = up_grad.astype(bf16)
            put(ugrad.at[at], ugrad_ref.at[at], 5 * i + 3)
            terms[part] = dot_cols(ugrad[at, :], w_in[...]).astype(bf16)
            put(terms.at[part], target, 5 * i + 4)
        for copy in outs:
            copy.wait()

    ins = [*(x_blocks if fresh else [units_all]), *grad_blocks, in_proj, down_proj]
    outs = [
        shape((half * tokens, D), bf16),
        shape((half * tokens, D), bf16),
        shape((total, D), bf16),
        shape((total, width), bf16),
    ]
    scratch = [
        pltpu.VMEM((total, D), bf16),
        pltpu.VMEM((D, width), bf16),
        pltpu.VMEM((pad, D), bf16),
        pltpu.VMEM((total, width), bf16),
        pltpu.VMEM((2, half * tokens, D), bf16),
    ]
    if fresh:
        outs += [shape((total, D), bf16), shape((total, pad), bf16)]
        scratch += [pltpu.VMEM((total, D), bf16), pltpu.VMEM((total, pad), bf16)]
    else:
        scratch += [pltpu.VMEM((total, width), bf16)]
    scratch += [DMA((n,)), DMA((2,)), DMA((10,)), DMA((n,))]
    return run(
        kernel,
        ins,
        [ANY] * len(ins),
        outs,
        [ANY] * len(outs),
        scratch,
        2 * total * D * (width * (2 if fresh else 1) + pad),
        60,
    )


def cut_columns(order, weights, units, unit_pad):
    n, (rows, _), layers = order.shape[0], weights[0].shape, len(weights)

    def kernel(order_ref, *refs):
        weight_refs, outs, parts = refs[:layers], refs[layers:-1], refs[-1]
        zeros = jnp.zeros((rows, unit_pad - units), bf16)
        for l in range(layers):
            for c in range(n):
                for k in range(2):
                    at, to = k * FF + c * units, k * unit_pad
                    parts[c, l, :, to : to + units] = weight_refs[l][:, at : at + units]
                    if unit_pad > units:
                        parts[c, l, :, to + units : to + unit_pad] = zeros
        for a in range(n):
            outs[a][...] = parts[order_ref[a]]

    return run(
        kernel,
        [order, *weights],
        [pl.BlockSpec(memory_space=pltpu.SMEM)] + [VMEM] * layers,
        [shape((layers, rows, 2 * unit_pad), bf16)] * n,
        [VMEM] * n,
        [pltpu.VMEM((n, layers, rows, 2 * unit_pad), bf16)],
        0,
    )


def join_rows(order, blocks):
    n, (layers, rows, width) = len(blocks), blocks[0].shape

    def kernel(order_ref, *refs):
        block_refs, outs, parts = refs[:n], refs[n:-1], refs[-1]
        for a in range(n):
            parts[order_ref[a]] = block_refs[a][...]
        for l in range(layers):
            for c in range(n):
                outs[l][c * rows : (c + 1) * rows, :] = parts[c, l]

    return run(
        kernel,
        [order, *blocks],
        [pl.BlockSpec(memory_space=pltpu.SMEM)] + [VMEM] * n,
        [shape((n * rows, width), bf16)] * layers,
        [VMEM] * layers,
        [pltpu.VMEM((n, layers, rows, width), bf16)],
        0,
    )


class Ring:
    def __init__(self, n, m):
        self.n, self.m = n, m
        if n == 8:
            self.even = [0, 4, 2, 6, 1, 3, 5, 7]
            self.odd = [0, 2, 4, 6, 1, 5, 3, 7]
        else:
            self.even = self.odd = list(range(n))

    def swap(self, value, offset, odd_offset=None):
        odd_offset = offset if odd_offset is None else odd_offset
        return lax.ppermute(
            value, "ctx", [(i, i ^ (odd_offset if i % 2 else offset)) for i in range(self.n)]
        )

    def swap_z(self, value, offset):
        return lax.ppermute(value, "wt", [(i, i ^ offset) for i in range(self.m)])

    def offsets(self, me):
        return jnp.where(
            me % 2 == 1, jnp.array(self.odd, jnp.int32), jnp.array(self.even, jnp.int32)
        )

    def gather(self, own, *behind):
        if self.n == 8:
            blocks = [own, self.swap(own, 4, 2), self.swap(own, 2, 4), self.swap(own, 6)]
            if behind:
                blocks = [held(b, *behind) for b in blocks]
            return blocks + [self.swap(b, 1) for b in blocks]
        blocks = own[None]
        step = 1
        while step < self.n:
            blocks = jnp.concatenate([blocks, self.swap(blocks, step)])
            step *= 2
        return [blocks[i] for i in range(self.n)]

    def gather_steps(self, own):
        own = own[None]
        if self.n == 8:
            pair = jnp.concatenate([own, self.swap((yield own), 2, 4)])
            pair = yield pair
            other = self.swap(pair, 4, 2)
            other = yield other
            yield Blocks(
                [pair, other, self.swap(pair, 1), self.swap(other, 1)],
                [(0, 0), (1, 0), (0, 1), (1, 1), (2, 0), (3, 0), (2, 1), (3, 1)],
            )
        else:
            blocks, step = own, 1
            count = 0
            while step < self.n:
                if count < 3:
                    blocks = yield blocks
                count += 1
                blocks = jnp.concatenate([blocks, self.swap(blocks, step)])
                step *= 2
            yield Blocks([blocks], [(0, i) for i in range(self.n)])

    def first(self, keep, send):
        count = self.n // 2
        got = self.swap(send, 1 if self.n == 8 else count)
        total = keep.astype(f32) + got.astype(f32)
        return total.reshape(count, -1, keep.shape[-1])

    def outgoing(self, total):
        return total[total.shape[0] // 2 :].astype(bf16)

    def move(self, total, out):
        count = total.shape[0] // 2
        if self.n == 8:
            return self.swap(out, 2, 4) if count == 2 else self.swap(out, 4, 2)
        return self.swap(out, count)

    def add(self, total, got):
        return total[: total.shape[0] // 2] + got.astype(f32)

    def step(self, total):
        return self.add(total, self.move(total, self.outgoing(total)))

    def finish(self, total):
        while total.shape[0] > 2:
            total = self.step(total)
        return total[0], self.move(total, self.outgoing(total))[0]

    def reduce(self, keep, send):
        return self.finish(self.first(keep, send))

    def trade(self, blocks):
        if self.n == 8:
            return [blocks[0]] + [
                self.swap(blocks[i], self.even[i], self.odd[i]) for i in range(1, self.n)
            ]
        return [blocks[0]] + [self.swap(blocks[i], i) for i in range(1, self.n)]

    def sources(self, me):
        even, odd = [0] * self.n, [0] * self.n
        for i in range(self.n):
            even[i] = self.even[i] if self.even[i] % 2 == 0 else self.odd[i]
            odd[i] = self.odd[i] if self.odd[i] % 2 == 0 else self.even[i]
        table = jnp.where(me % 2 == 1, jnp.array(odd, jnp.int32), jnp.array(even, jnp.int32))
        return me ^ table

    def gather_z(self, own):
        return jnp.stack([own] + [self.swap_z(own, k) for k in range(1, self.m)])

    def reduce_z(self, terms):
        total = terms[0].astype(f32)
        for k in range(1, self.m):
            total = total + self.swap_z(terms[k].astype(bf16), k).astype(f32)
        return total


def held(value, *others):
    return lax.optimization_barrier((value, *others))[0]


def make_body(n, m):
    ring = Ring(n, m)
    rows = D // (n * m)
    bias_w = QKV_W // (n * m)
    pad_rows = -(-(rows + 3) // 16) * 16
    step = m * pad_rows
    all_rows = n * step
    units = FF // n
    unit_pad = -(-units // 128) * 128
    cfg = (n, m, rows, pad_rows)

    in_block_row = jnp.arange(all_rows // 2, dtype=jnp.int32)[:, None] % pad_rows

    def row_terms(left, right, *extra_rows):
        cut = all_rows // 2
        halves = []
        for part in (left[:, :cut], left[:, cut:]):
            terms = dot_rows(part, right)
            for i, row in enumerate(extra_rows):
                terms = jnp.where(in_block_row == rows + 1 + i, row, terms)
            halves.append(terms.astype(bf16))
        return halves

    def z_sum(mine, got):
        total = mine + got.astype(f32)
        return ring.reduce_z(total.reshape(m, pad_rows, total.shape[-1]))

    def feed_in_home(parts):
        cut = jnp.stack([p.reshape(n, rows, 2 * unit_pad) for p in parts], axis=1)
        return lax.all_to_all(cut, "ctx", 0, 0, tiled=True)

    def feed_in_out(got):
        got = got.reshape(n, LAYERS, rows, 2, unit_pad)[..., :units].astype(f32)
        return got.transpose(1, 2, 3, 0, 4).reshape(LAYERS, rows, 2 * FF)

    def body(
        hidden_in,
        positions,
        cotangent,
        attn_gain,
        qkv_weight,
        qkv_bias,
        out_weight,
        mlp_gain,
        in_weight,
        down_weight,
    ):
        me, me_z = lax.axis_index("ctx"), lax.axis_index("wt")
        shard = me * m + me_z
        offsets = ring.offsets(me)
        own_positions = positions[0]
        tokens = own_positions.shape[0]

        def spread(vector, width):
            row = jnp.zeros((1, QKV_W), bf16)
            return lax.dynamic_update_slice(row, vector[None], (0, shard * width))

        def qkv_block(l):
            rest = jnp.zeros((pad_rows - rows - 3, QKV_W), bf16)
            return jnp.concatenate(
                [
                    qkv_weight[l],
                    spread(qkv_bias[l], bias_w),
                    spread(attn_gain[l], rows),
                    spread(mlp_gain[l], rows),
                    rest,
                ]
            )

        def out_block(l):
            return jnp.pad(out_weight[l], ((0, pad_rows - rows), (0, 0)))

        def z_blocks(block):
            return ring.gather_z(block).reshape(step, block.shape[-1])

        def both_block(l):
            return jnp.concatenate([qkv_block(l), out_block(l)], axis=1)

        def z_parts(block):
            return [block] + [ring.swap_z(block, k) for k in range(1, m)]

        def z_join(parts):
            return jnp.concatenate(parts, axis=0)

        targets, sources = me ^ offsets, ring.sources(me)
        parts0 = z_parts(both_block(0))
        down0 = lax.all_gather(held(down_weight[0], *parts0), "wt", axis=0, tiled=True)
        cut = cut_columns(targets, [in_weight[l] for l in range(LAYERS)], units, unit_pad)
        steps0 = ring.gather_steps(held(z_join(parts0), cut[0]))
        own0 = next(steps0)
        traded = ring.trade([held(c, own0) for c in cut])
        pair0 = steps0.send(own0)
        traded[-1] = held(traded[-1], pair0)
        in0_got, in1_got = join_rows(sources, traded)
        in0 = lax.all_gather(held(in0_got, down0), "wt", axis=0, tiled=True)
        both0 = steps0.send(steps0.send(pair0))

        own_row = jnp.tile(own_positions, GROUP)[None]

        half_head = HEAD // 2
        frequency = jnp.exp(
            jnp.arange(half_head, dtype=f32) * (-2.0 * math.log(ROPE_BASE) / HEAD)
        )
        angles = own_positions.astype(f32)[:, None] * frequency[None, :]
        cos = jnp.tile(jnp.cos(angles), (1, 4))
        sin = jnp.tile(jnp.sin(angles), (1, 4))

        column = jnp.arange(all_rows, dtype=jnp.int32)
        in_block = column % pad_rows
        block_owner = ((me ^ offsets[:, None]) * m + (me_z ^ jnp.arange(m))[None, :]).reshape(-1)
        owner = jnp.repeat(block_owner, pad_rows)
        feature = jnp.where(in_block < rows, owner * rows + in_block, -1)
        every = jnp.arange(D, dtype=jnp.int32)
        perm = (every[:, None] == feature[None, :]).astype(bf16)
        second, first, inside = every // (n * rows), (every // rows) % n, every % rows
        perm2 = (every[:, None] == ((first * m + second) * rows + inside)[None, :]).astype(bf16)

        lane = jnp.arange(128, dtype=jnp.int32)[None]
        places = jnp.where(
            lane == 0, own_positions[:, None] // 256, jnp.where(lane == 1, own_positions[:, None] % 256, 0)
        ).astype(bf16)

        hidden0, rel0, query0, kv0, gain0 = before_attention(
            cfg, hidden_in[0], [], perm, cos, sin, both0, places
        )
        kvs0 = ring.gather(kv0)
        middle0, normed0, heads0, mix0, lse0, turn0 = attention(
            cfg, query0, kvs0, own_row, kvs0, hidden0, gain0, perm, perm2, both0, QKV_W
        )
        xs0 = ring.gather(normed0)
        steps1 = ring.gather_steps(z_join(z_parts(held(both_block(1), normed0))))
        own1 = next(steps1)
        xs0[-1] = held(xs0[-1], own1)
        keep, send, x_all0, units0, act0 = feed_forward(xs0, in0, down0)
        pair1 = held(steps1.send(own1), keep)
        in1 = lax.all_gather(held(in1_got, in0, xs0[1]), "wt", axis=0, tiled=True)
        total = ring.first(keep, send)
        while total.shape[0] > 2:
            total = ring.step(total)
        out = ring.outgoing(total)
        sums = (total[0], ring.move(total, out)[0])
        both1 = steps1.send(held(steps1.send(pair1), out))
        hidden1, rel1, query1, kv1, gain1 = before_attention(
            cfg, middle0, list(sums), perm, cos, sin, both1
        )
        kvs1 = ring.gather(kv1)
        down1_own = held(down_weight[1], in1, *kvs1)
        cotangent_late = held(cotangent[0], *kvs1)
        down1 = lax.all_gather(down1_own, "wt", axis=0, tiled=True)
        middle1, normed1, heads1, mix1, lse1, turn1 = attention(
            cfg, held(query1, down1_own, cotangent_late), kvs1, own_row, kvs0, hidden1, gain1, perm, perm2, both1, QKV_W
        )
        grads1 = ring.gather(cotangent_late, normed1)
        xs1 = ring.gather(normed1)

        def feed_reduce(keep, send, x_all, ugrad, act, g_all, *sc_behind):
            total = ring.first(keep, send)
            out = ring.outgoing(total)
            got = ring.move(total, out)
            in_terms = dot_rows(held(x_all, out), ugrad).astype(bf16)
            in_part = lax.psum_scatter(
                held(in_terms, *sc_behind), "wt", scatter_dimension=0, tiled=True
            )
            total = ring.add(total, got)
            while total.shape[0] > 2:
                total = ring.step(total)
            out = held(ring.outgoing(total), in_terms)
            got = ring.move(total, out)[0]
            down_terms = dot_rows(held(act, out), g_all)[:units].astype(bf16)
            return (total[0], held(got, down_terms)), in_part, down_terms

        keep, send, g_all1, ugrad1, x_all1, act1 = feed_forward_back(xs1, None, grads1, in1, down1)
        sums, in_part1, down_terms1 = feed_reduce(keep, send, x_all1, ugrad1, act1, g_all1)
        down_part1 = lax.psum_scatter(down_terms1, "wt", scatter_dimension=0, tiled=True)
        mgrad1, low1, mlp_gain_grad1, heads_grad1 = middle_back(
            cfg, sums, middle1, cotangent[0], gain1, perm, perm2, both1, QKV_W
        )
        keep, send, part1 = attention_back(
            cfg, heads_grad1, mix1, lse1, turn1, query1, kvs1, own_row, kvs0, cos, sin
        )
        kv_total = ring.first(keep, send)
        kv_out = ring.outgoing(kv_total)
        kv_got = ring.move(kv_total, kv_out)
        query_rel1 = query_back(cfg, held(part1, kv_out), both1)
        kv_sums = ring.finish(ring.add(kv_total, held(kv_got, query_rel1)))
        grad1, grad1_low, kv_part1, attn_gain_grad1 = layer_back(
            cfg, kv_sums, query_rel1, hidden1, mgrad1, gain1, cos, sin, perm, both1
        )
        grads0 = ring.gather(grad1_low)

        def wide_row(row):
            return jnp.pad(row[:1], ((0, 0), (0, QKV_W - D)))

        out_keep1, out_send1 = row_terms(heads1, held(low1, grad1_low))
        joint_keep1, joint_send1 = row_terms(
            rel1,
            jnp.concatenate([part1, kv_part1], axis=1),
            wide_row(attn_gain_grad1),
            wide_row(mlp_gain_grad1),
        )
        total1 = jnp.concatenate(
            [ring.first(out_keep1, out_send1), ring.first(joint_keep1, joint_send1)], axis=2
        )
        out1 = ring.outgoing(total1)
        cut = n // 2 * tokens
        act_late = held(act1, joint_send1)[:, :units]
        last_keep = dot(act_late[:cut], down1).astype(bf16)
        last_send = dot(act_late[cut:], down1).astype(bf16)
        hidden_total = ring.first(last_keep, last_send)
        hidden_out1 = ring.outgoing(hidden_total)
        grads0[-1] = held(grads0[-1], out1, hidden_out1)
        keep, send, g_all0, ugrad0 = feed_forward_back(None, units0, grads0, in0, down0)
        got1 = ring.move(total1, out1)
        hidden_got = ring.move(hidden_total, hidden_out1)
        sums, in_part0, down_terms0 = feed_reduce(
            keep, held(send, got1, hidden_got), x_all0, ugrad0, act0, g_all0, down_part1
        )
        mgrad0, low0, mlp_gain_grad0, heads_grad0 = middle_back(
            cfg, sums, middle0, grad1, gain0, perm, perm2, both0, QKV_W
        )
        total1 = ring.add(total1, held(got1, heads_grad0))
        while total1.shape[0] > 2:
            total1 = ring.step(total1)
        out1 = ring.outgoing(total1)
        hidden_total = ring.add(hidden_total, held(hidden_got, heads_grad0))
        while hidden_total.shape[0] > 2:
            hidden_total = ring.step(hidden_total)
        hidden_out1 = ring.outgoing(hidden_total)
        keep, send, part0 = attention_back(
            cfg, held(heads_grad0, out1, hidden_out1), mix0, lse0, turn0, query0, kvs0,
            own_row, kvs0, cos, sin,
        )
        got1 = ring.move(total1, out1)[0]
        hidden_got = ring.move(hidden_total, hidden_out1)[0]
        send = held(send, got1, hidden_got)
        kv_total = ring.first(keep, send)
        kv_out = ring.outgoing(kv_total)
        kv_got = ring.move(kv_total, kv_out)
        query_rel0 = query_back(cfg, held(part0, kv_out), both0)
        out_keep0, out_send0 = row_terms(heads0, held(low0, kv_out), mlp_gain_grad0[:1])
        kv_total = ring.add(kv_total, held(kv_got, query_rel0, out_send0))
        while kv_total.shape[0] > 2:
            kv_total = ring.step(kv_total)
        kv_out = ring.outgoing(kv_total)
        kv_got = ring.move(kv_total, kv_out)[0]
        query_keep0, query_send0 = row_terms(rel0, held(part0, kv_out))
        kv_sums = (kv_total[0], held(kv_got, query_send0))
        first0 = jnp.concatenate(
            [
                ring.first(out_keep0, out_send0),
                held(ring.first(query_keep0, query_send0), *kv_sums),
            ],
            axis=2,
        )
        first_out0 = ring.outgoing(first0)
        first_got0 = ring.move(first0, first_out0)
        down_in0 = held(down_terms0, in_part0)
        z_out1 = (total1[0] + held(got1, kv_got).astype(f32)).astype(bf16)
        z_out1 = z_out1.reshape(m, pad_rows, z_out1.shape[-1])
        z_got1 = [ring.swap_z(z_out1[k], k) for k in range(1, m)]
        grad0, unused, kv_part0, attn_gain_grad0 = layer_back(
            cfg, (kv_sums[0], held(kv_sums[1], first_out0, down_in0, z_out1)), query_rel0, hidden0, mgrad0, gain0, cos, sin, perm, both0
        )
        down_part0 = lax.psum_scatter(down_in0, "wt", scatter_dimension=0, tiled=True)
        hidden_out = middle1 + hidden_total[0] + held(hidden_got, grad0).astype(f32)
        first0 = ring.add(first0, first_got0)
        gain_rows = jnp.pad(attn_gain_grad0[:1], ((0, 127), (0, 0))).astype(bf16)
        columns = lax.dot_general(
            perm, gain_rows, (((0,), (1,)), ((), ())), preferred_element_type=f32
        ).astype(bf16)
        cut = all_rows // 2
        kv_keep0, kv_send0 = [
            jnp.concatenate([half, columns[i * cut : (i + 1) * cut]], axis=1)
            for i, half in enumerate(row_terms(rel0, kv_part0))
        ]
        last0 = ring.first(kv_keep0, kv_send0)
        last_out0 = ring.outgoing(last0)
        last_got0 = ring.move(last0, last_out0)
        home = feed_in_home([held(in_part0, last_got0), in_part1])
        last0 = ring.add(last0, last_got0)
        total0 = jnp.concatenate([first0, last0], axis=2)
        while total0.shape[0] > 2:
            total0 = ring.step(total0)
        last_got0 = ring.move(total0, ring.outgoing(total0))[0]
        last_sum0 = (total0[0] + held(last_got0, down_part0).astype(f32)).astype(bf16)
        layer0 = ring.reduce_z(last_sum0.reshape(m, pad_rows, last_sum0.shape[-1]))
        layer1 = sum((held(g, layer0).astype(f32) for g in z_got1), z_out1[0].astype(f32))
        gain_at = QW + QKV_W

        def own_part(row, width):
            return lax.dynamic_slice(row, (0, shard * width), (1, width))[0]

        stacked = [
            jnp.stack([layer0[:rows, gain_at], own_part(layer1[rows + 1 : rows + 2, QW:], rows)]),
            jnp.stack([layer[:rows, QW : QW + QKV_W] for layer in (layer0, layer1)]),
            jnp.stack(
                [own_part(l[rows : rows + 1, QW : QW + QKV_W], bias_w) for l in (layer0, layer1)]
            ),
            jnp.stack([layer[:rows, :QW] for layer in (layer0, layer1)]),
            jnp.stack(
                [
                    own_part(layer0[rows + 1 : rows + 2, :QW], rows),
                    own_part(layer1[rows + 2 : rows + 3, QW:], rows),
                ]
            ),
        ]
        in_weight_grad = feed_in_out(held(home, last_sum0))
        down_weight_grad = jnp.stack([down_part0, down_part1]).astype(f32)
        return (hidden_out[None], grad0[None], *stacked, in_weight_grad, down_weight_grad)

    return body


def solution(mesh):
    sizes = dict(mesh.shape)
    rows = P("wt", "ctx", None)
    vector = P(None, ("ctx", "wt"))
    matrix = P(None, ("ctx", "wt"), None)
    return jax.shard_map(
        make_body(sizes["ctx"], sizes["wt"]),
        mesh=mesh,
        in_specs=(
            rows, P("wt", "ctx"), rows, vector, matrix, vector, matrix, vector, matrix, matrix,
        ),
        out_specs=(rows, rows, vector, matrix, vector, matrix, vector, matrix, matrix),
        check_vma=False,
    )
```

time: 714 us -> 512 us (0.72)
  Pallas kernels: 0 us -> 136 us
  matrix products: 139 us -> 32.2 us
  local copies, waits for them, and re-layouts: 165 us -> 59.4 us
  starting transfers between devices: 135 us -> 78.2 us
  blocking collectives: 29.1 us -> 0 us
  other arithmetic: 59.4 us -> 34.3 us
  waiting for transfers between devices: 161 us -> 146 us
    pallas_call x0 -> x17, Pallas kernels: none -> 136 us  [run(): pl.pallas_call(kernel, out_shape=outs, in_specs=in_specs, out_specs=out_s...]
    dot_general x28 -> x1, matrix products: 76 us -> 0.81 us  [body(): lax.dot_general(perm, gain_rows, (((0,), (1,)), ((), ())), preferred_elem...]
    unnamed x382 -> x261, local copies, waits for them, and re-layouts: 57 us -> 20.9 us
    ppermute x30 -> x12, starting transfers between devices: 49.6 us -> 16.6 us  [swap_z(): return lax.ppermute(value, 'wt', [(i, i ^ offset) for i in range(self.m)])]
    reshape x23 -> x3, local copies, waits for them, and re-layouts: 37.3 us -> 4.6 us  [the longest x2 3.85 us: feed_in_out(): return got.transpose(1, 2, 3, 0, 4).reshape(LAYERS, rows, 2 * FF)]
    slice x66 -> x41, local copies, waits for them, and re-layouts: 37.5 us -> 14.5 us  [the longest x2 2.14 us: feed_reduce(): down_terms = dot_rows(held(act, out), g_all)[:units].astype(bf16)]
    ppermute x106 -> x85, starting transfers between devices: 77.3 us -> 57.3 us  [swap(): lax.ppermute(value, 'ctx', [(i, i ^ (odd_offset if i % 2 else offset)) fo...]
    dot_general x12 -> x2, matrix products: 23.5 us -> 3.74 us  [dot(): return jnp.dot(left, right, preferred_element_type=f32)]
  transfers between devices with their start and end apart: 146 -> 106, of which waited for: 42 -> 48; matrix products, arithmetic and copies ran while one was open for 43% -> 18% of each run, Pallas kernels for 0% -> 18%
where the time goes in v2:
time: 512 us; the launch traced here: 503 us
  waiting for transfers between devices  146 us (29%)
  Pallas kernels  136 us (27%)
  starting transfers between devices  78.2 us (15%)
  local copies, waits for them, and re-layouts  59.4 us (12%)
  other arithmetic  34.3 us (7%)
  matrix products  32.2 us (6%)
  between operations  16.4 us (3%)
    pallas_call x17, Pallas kernels, run(): pl.pallas_call(kernel, out_shape=outs, in_specs=in_specs, out_specs=out_s...  136 us
    ppermute x85, waiting for transfers between devices, swap(): lax.ppermute(value, 'ctx', [(i, i ^ (odd_offset if i % 2 else offset)) fo...  108 us
    ppermute x85, starting transfers between devices, swap(): lax.ppermute(value, 'ctx', [(i, i ^ (odd_offset if i % 2 else offset)) fo...  57.3 us
    dot_general x14, matrix products, dot_rows(): lax.dot_general(left, right, (((0,), (0,)), ((), ())), preferred_element_...  27.7 us
    ppermute x12, waiting for transfers between devices, swap_z(): return lax.ppermute(value, 'wt', [(i, i ^ offset) for i in range(self.m)])  23.8 us
    unnamed x261, local copies, waits for them, and re-layouts  20.9 us
    ppermute x12, starting transfers between devices, swap_z(): return lax.ppermute(value, 'wt', [(i, i ^ offset) for i in range(self.m)])  16.6 us
  transfers between devices with their start and end apart: 106, of which 48 were waited for; matrix products, arithmetic and copies ran while one was open for 18% of the time, Pallas kernels for 18%

profile of v2, /device:TPU:0, one launch (start us, length us, event | category | flops | bytes accessed | tf_op | source)
XLA Modules:
  0.0 503.0 jit_solution(5363375703974781673)
XLA Ops:
  14.8 5.4 %collective-permute-start.2 = (bf16[32,2048]{1,0:T(8,128)(2,1)S(1)}, bf16[32,2048]{1,0:T(8,128)(2,1)S(1)}, u32[]{:S(2)}, u32[]{:S(2)}) collective-permute-start(bf16[32,2048]{1,0:T(8,128)(2,1)S(1)} %pad_maximum_fusion.10), channel_id=1, source_target_pairs={{0,3},{1,2},{2,1},{3,0},{4,7},{5,6},{6,5},{7,4},{8,11},{9,10},{10,... | collective-permute-start | bytes 393224 | tf_op jit(solution)/shard_map/ppermute | solution.py:755
  24.6 6.6 %collective-permute-done.1 = bf16[32,2048]{1,0:T(8,128)(2,1)S(1)} collective-permute-done((bf16[32,2048]{1,0:T(8,128)(2,1)S(1)}, bf16[32,2048]{1,0:T(8,128)(2,1)S(1)}, u32[]{:S(2)}, u32[]{:S(2)}) %collective-permute-start.1) | collective-permute-done | bytes 131104 | tf_op jit(solution)/shard_map/ppermute | solution.py:755
  34.4 2.7 shard_map.214
  42.8 5.0 collective-permute-done.24.refs_1_
  47.8 4.4 collective-permute-done.30.refs_7_
  52.2 2.2 collective-permute-start.28
  56.6 2.6 collective-permute-done.28.refs_5_
  60.9 2.6 shard_map.217
  63.5 2.0 collective-permute-start.4
  67.7 10.7 %collective-permute-done.4.refs_6_.refs_23_.refs_8_.refs_2_.refs_10_ = bf16[2,128,2048]{2,1,0:T(8,128)(2,1)S(1)} collective-permute-done((bf16[2,128,2048]{2,1,0:T(8,128)(2,1)S(1)}, bf16[2,128,2048]{2,1,0:T(8,128)(2,1)S(1)}, u32[]{:S(2)}, u32[]{:S(2)}) %collective-permute-start.4) | collective-permute-done | bytes 1048608 | tf_op jit(solution)/shard_map/ppermute | solution.py:750
  79.3 2.0 fusion.1.refs_2_.refs_20_.refs_3_.refs_5_.refs_8_
  82.8 5.4 %shard_map.215 = (f32[160,896]{1,0:T(8,128)}, bf16[160,1024]{1,0:T(8,128)(2,1)}, bf16[160,896]{1,0:T(8,128)(2,1)}, bf16[160,384]{1,0:T(8,128)(2,1)}, f32[16,896]{1,0:T(8,128)}) custom-call(bf16[160,128]{1,0:T(8,128)(2,1)} %select_convert_fusion.2.refs_0_, bf16[160,896]{1,0:T(8,128)(2,1)} %bitcast.149, ...), custom_call_target="tpu_custom_call" | custom-call | flops 671088640 | bytes 7888896 | tf_op jit(solution)/shard_map/pallas_call | solution.py:53
  88.2 2.9 collective-permute-start.9
  91.9 3.4 collective-permute-done.9.refs_4_.refs_12_.refs_16_.refs_8_
  95.3 2.8 collective-permute-done.8.refs_3_.refs_11_.refs_15_.refs_7_
  98.6 1.8 fusion.4.refs_21_.refs_6_
  103.1 11.8 %shard_map.216 = (f32[160,896]{1,0:T(8,128)}, bf16[160,896]{1,0:T(8,128)(2,1)}, bf16[160,1024]{1,0:T(8,128)(2,1)}, f32[128,1120]{1,0:T(8,128)}, f32[16,1120]{1,0:T(8,128)}, /*index=5*/bf16[128,1120]{1,0:T(8,128)(2,1)}) custom-call(bf16[160,896]{1,0:T(8,128)(2,1)} %get-tuple-element.138.refs_0_.refs_4_, ...), custom_call_target="tpu_custom_call" | custom-call | flops 1468006400 | bytes 12642688 | tf_op jit(solution)/shard_map/pallas_call | solution.py:53
  118.5 2.6 collective-permute-start.23
  121.1 5.8 %collective-permute-done.23 = bf16[32,2048]{1,0:T(8,128)(2,1)S(1)} collective-permute-done((bf16[32,2048]{1,0:T(8,128)(2,1)S(1)}, bf16[32,2048]{1,0:T(8,128)(2,1)S(1)}, u32[]{:S(2)}, u32[]{:S(2)}) %collective-permute-start.23) | collective-permute-done | bytes 131104 | tf_op jit(solution)/shard_map/ppermute | solution.py:755
  126.9 4.0 collective-permute-done.22
  134.1 10.7 %shard_map.218 = (bf16[640,896]{1,0:T(8,128)(2,1)}, bf16[640,896]{1,0:T(8,128)(2,1)}, bf16[1280,896]{1,0:T(8,128)(2,1)}, bf16[1280,1280]{1,0:T(8,128)(2,1)}, bf16[1280,640]{1,0:T(8,128)(2,1)}) custom-call(bf16[160,896]{1,0:T(8,128)(2,1)} %get-tuple-element.143.refs_0_, bf16[160,896]{1,0:T(8,128)(2,1)} %copy-done.103, bf16[160,896]{1,0:T(8,128)(2,1)} %copy-done.101, ...), custom_call_target="tpu_custom_call" | custom-call | flops 4404019200 | bytes 15179776 | tf_op jit(solution)/shard_map/pallas_call | solution.py:53
  146.6 7.7 %collective-permute-done.34 = bf16[1,128,2048]{2,1,0:T(8,128)(2,1)S(1)} collective-permute-done((bf16[1,128,2048]{2,1,0:T(8,128)(2,1)S(1)}, bf16[1,128,2048]{2,1,0:T(8,128)(2,1)S(1)}, u32[]{:S(2)}, u32[]{:S(2)}) %collective-permute-start.34) | collective-permute-done | bytes 524320 | tf_op jit(solution)/shard_map/ppermute | solution.py:750
  157.2 15.0 %collective-permute-done.32 = bf16[2,160,896]{2,1,0:T(8,128)(2,1)S(1)} collective-permute-done((bf16[2,160,896]{2,1,0:T(8,128)(2,1)S(1)}, bf16[2,160,896]{2,1,0:T(8,128)(2,1)S(1)}, u32[]{:S(2)}, u32[]{:S(2)}) %collective-permute-start.32) | collective-permute-done | bytes 573472 | tf_op jit(solution)/shard_map/ppermute | solution.py:750
  172.4 3.1 collective-permute-done.35.refs_7_.refs_23_.refs_8_.refs_2_.refs_10_
  177.2 4.9 collective-permute-done.33
  183.2 5.4 %shard_map.219 = (f32[160,896]{1,0:T(8,128)}, bf16[160,1024]{1,0:T(8,128)(2,1)}, bf16[160,896]{1,0:T(8,128)(2,1)}, bf16[160,256]{1,0:T(8,128)(2,1)}, f32[16,896]{1,0:T(8,128)}) custom-call(f32[160,896]{1,0:T(8,128)} %get-tuple-element.142.refs_0_.refs_2_, f32[160,896]{1,0:T(8,128)} %slice_bitcast_fusion.4.refs_1_, bf16[160,896]{1,0:T(8,128)(2,1)} %bitcast.158, ...), custom_call_target="tpu_custom_call" | custom-call | flops 671088640 | bytes 8953856 | tf_op jit(solution)/shard_map/pallas_call | solution.py:53
  192.2 2.6 collective-permute-done.40.refs_4_.refs_8_
  200.7 12.1 %shard_map.220 = (f32[160,896]{1,0:T(8,128)}, bf16[160,896]{1,0:T(8,128)(2,1)}, bf16[160,1024]{1,0:T(8,128)(2,1)}, f32[128,1120]{1,0:T(8,128)}, f32[16,1120]{1,0:T(8,128)}, /*index=5*/bf16[128,1120]{1,0:T(8,128)(2,1)}) custom-call(bf16[160,896]{1,0:T(8,128)(2,1)} %get-tuple-element.175.refs_0_.refs_4_, bf16[160,256]{1,0:T(8,128)(2,1)} %get-tuple-element.172.refs_1_.refs_5_, ...), custom_call_target="tpu_custom_call" | custom-call | flops 1468006400 | bytes 12315008 | tf_op jit(solution)/shard_map/pallas_call | solution.py:53
  217.7 6.8 %collective-permute-done.47.refs_3_ = bf16[160,896]{1,0:T(8,128)(2,1)S(1)} collective-permute-done((bf16[160,896]{1,0:T(8,128)(2,1)}, bf16[160,896]{1,0:T(8,128)(2,1)S(1)}, u32[]{:S(2)}, u32[]{:S(2)}) %collective-permute-start.47) | collective-permute-done | bytes 286752 | tf_op jit(solution)/shard_map/ppermute | solution.py:750
  224.5 5.1 %collective-permute-done.46.refs_2_ = bf16[160,896]{1,0:T(8,128)(2,1)S(1)} collective-permute-done((bf16[160,896]{1,0:T(8,128)(2,1)}, bf16[160,896]{1,0:T(8,128)(2,1)S(1)}, u32[]{:S(2)}, u32[]{:S(2)}) %collective-permute-start.46) | collective-permute-done | bytes 286752 | tf_op jit(solution)/shard_map/ppermute | solution.py:750
  232.0 16.1 %shard_map.221 = (bf16[640,896]{1,0:T(8,128)(2,1)}, bf16[640,896]{1,0:T(8,128)(2,1)}, bf16[1280,896]{1,0:T(8,128)(2,1)}, bf16[1280,1280]{1,0:T(8,128)(2,1)}, bf1...) custom-call(bf16[160,896]{1,0:T(8,128)(2,1)} %get-tuple-element.179.refs_0_, bf16[160,896]{1,0:T(8,128)(2,1)} %copy-done.105, ...), custom_call_target="tpu_custom_call" | custom-call | flops 7340032000 | bytes 19767296 | tf_op jit(solution)/shard_map/pallas_call | solution.py:53
  248.6 2.7 collective-permute-done.59
  254.9 4.7 convolution_convert_fusion.1
  259.7 3.2 collective-permute-done.60
  264.2 3.5 fusion.74
  270.4 6.1 %shard_map.222 = (f32[160,896]{1,0:T(8,128)}, bf16[160,896]{1,0:T(8,128)(2,1)}, f32[8,896]{1,0:T(8,128)}, bf16[160,896]{1,0:T(8,128)(2,1)}) custom-call(f32[160,896]{1,0:T(8,128)} %slice_bitcast_fusion.3.refs_0_, bf16[160,896]{1,0:T(8,128)(2,1)} %bitcast.159, f32[160,896]{1,0:T(8,128)} %get-tuple-element.178.refs_2_, bf16[160,896]{1,0:T(8,128)(2,1)} %bitcast.153, ...), custom_call_target="tpu_custom_call" | custom-call | flops 1101004800 | bytes 10588160 | tf_op jit(solution)/shard_map/pallas_call | solution.py:53
  276.6 12.3 %shard_map.223 = (bf16[640,256]{1,0:T(8,128)(2,1)}, bf16[640,256]{1,0:T(8,128)(2,1)}, bf16[160,896]{1,0:T(8,128)(2,1)}) custom-call(bf16[160,896]{1,0:T(8,128)(2,1)} %get-tuple-element.195.refs_0_, f32[128,1120]{1,0:T(8,128)} %get-tuple-element.196.refs_1_, f32[16,1120]{1,0:T(8,128)} %get-tuple-element.197.refs_2_, ...), custom_call_target="tpu_custom_call" | custom-call | flops 3670016000 | bytes 4254080 | tf_op jit(solution)/shard_map/pallas_call | solution.py:53
  293.9 4.2 shard_map.224.refs_2_
  299.9 2.8 collective-permute-done.64
  303.3 6.0 %shard_map.225 = (f32[160,896]{1,0:T(8,128)}, bf16[160,896]{1,0:T(8,128)(2,1)}, bf16[160,256]{1,0:T(8,128)(2,1)}, f32[8,896]{1,0:T(8,128)}) custom-call(f32[160,256]{1,0:T(8,128)} %slice_bitcast_fusion.8.refs_0_, bf16[160,256]{1,0:T(8,128)(2,1)} %bitcast.168, f32[160,1024]{1,0:T(8,128)} %shard_map.224.refs_2_, ...), custom_call_target="tpu_custom_call" | custom-call | flops 671088640 | bytes 9269248 | tf_op jit(solution)/shard_map/pallas_call | solution.py:53
  316.6 2.6 convolution_convert_fusion.2
  321.1 1.9 fusion.8
  325.8 4.0 collective-permute-done.68.refs_3_
  336.0 11.8 %shard_map.226 = (bf16[640,896]{1,0:T(8,128)(2,1)}, bf16[640,896]{1,0:T(8,128)(2,1)}, bf16[1280,896]{1,0:T(8,128)(2,1)}, bf16[1280,1280]{1,0:T(8,128)(2,1)}) custom-call(bf16[1280,1280]{1,0:T(8,128)(2,1)} %get-tuple-element.209.refs_0_, bf16[160,896]{1,0:T(8,128)(2,1)} %get-tuple-element.210.refs_1_, bf16[160,896]{1,0:T(8,128)(2,1)} %copy-done.102, ...), custom_call_target="tpu_custom_call" | custom-call | flops 4404019200 | bytes 16818176 | tf_op jit(solution)/shard_map/pallas_call | solution.py:53
  347.9 3.0 collective-permute-done.77
  353.6 5.1 %convolution_convert_fusion = bf16[896,1280]{1,0:T(8,128)(2,1)} fusion(bf16[1280,896]{1,0:T(8,128)(2,1)S(1)} %copy-done.126, bf16[1280,1280]{1,0:T(8,128)(2,1)S(1)} %copy-done.124), kind=kOutput, calls=%fused_computation.7 | convolution fusion | flops 2937159680 | bytes 7864320 | tf_op jit(solution)/shard_map/dot_general | solution.py:44
  358.8 2.4 collective-permute-done.78
  364.7 3.3 fusion.75
  371.2 6.7 %shard_map.227 = (f32[160,896]{1,0:T(8,128)}, bf16[160,896]{1,0:T(8,128)(2,1)}, f32[8,896]{1,0:T(8,128)}, bf16[160,896]{1,0:T(8,128)(2,1)}) custom-call(f32[160,896]{1,0:T(8,128)} %slice_bitcast_fusion.2.refs_0_, bf16[160,896]{1,0:T(8,128)(2,1)} %bitcast.150, f32[160,896]{1,0:T(8,128)} %get-tuple-element.142.refs_0_.refs_2_, ...), custom_call_target="tpu_custom_call" | custom-call | flops 1101004800 | bytes 10874880 | tf_op jit(solution)/shard_map/pallas_call | solution.py:53
  382.1 12.3 %shard_map.228 = (bf16[640,256]{1,0:T(8,128)(2,1)}, bf16[640,256]{1,0:T(8,128)(2,1)}, bf16[160,896]{1,0:T(8,128)(2,1)}) custom-call(bf16[160,896]{1,0:T(8,128)(2,1)} %get-tuple-element.230.refs_0_, f32[128,1120]{1,0:T(8,128)} %get-tuple-element.231.refs_1_, f32[16,1120]{1,0:T(8,128)} %get-tuple-element.232.refs_2_, ...), custom_call_target="tpu_custom_call" | custom-call | flops 3670016000 | bytes 4581760 | tf_op jit(solution)/shard_map/pallas_call | solution.py:53
  399.7 4.2 shard_map.229.refs_2_
  405.8 2.0 stack_reshape.7
  411.0 2.7 collective-permute-done.84
  419.6 5.9 %shard_map.230 = (f32[160,896]{1,0:T(8,128)}, bf16[160,896]{1,0:T(8,128)(2,1)}, bf16[160,256]{1,0:T(8,128)(2,1)}, f32[8,896]{1,0:T(8,128)}) custom-call(f32[160,256]{1,0:T(8,128)} %slice_bitcast_fusion.7.refs_0_, bf16[160,256]{1,0:T(8,128)(2,1)} %bitcast.167, f32[160,1024]{1,0:T(8,128)} %shard_map.229.refs_2_, ...), custom_call_target="tpu_custom_call" | custom-call | flops 671088640 | bytes 9269248 | tf_op jit(solution)/shard_map/pallas_call | solution.py:53
  435.0 2.9 fusion.14
  444.0 2.0 collective-permute-start.96
  449.3 2.2 copy.102
  451.5 3.8 all-to-all-start
  455.3 7.2 %reduce-scatter.15.cloned.1.call-done = bf16[152,896]{1,0:T(8,128)(2,1)} async-done(((bf16[608,896]{1,0:T(8,128)(2,1)}), bf16[152,896]{1,0:T(8,128)(2,1)}) %reduce-scatter.15.cloned.1.call-update) | async-done | bytes 272400
  464.4 7.2 %all-to-all-done = bf16[8,2,28,1280]{3,1,2,0:T(2,128)(2,1)S(1)} async-done(((bf16[8,2,28,1280]{3,1,2,0:T(2,128)(2,1)}), bf16[8,2,28,1280]{3,1,2,0:T(2,128)(2,1)S(1)}, u32[]{:S(2)}, u32[]{:S(2)}) %all-to-all-start) | async-done | bytes 1146912 | tf_op jit(solution)/shard_map/all_to_all | solution.py:884
  473.6 1.8 collective-permute-start.93
  477.1 3.6 reshape.332
  481.7 2.4 collective-permute-start.95
  484.1 5.4 %collective-permute-done.92 = bf16[32,2176]{1,0:T(8,128)(2,1)} collective-permute-done((bf16[32,2176]{1,0:T(8,128)(2,1)S(1)}, bf16[32,2176]{1,0:T(8,128)(2,1)}, u32[]{:S(2)}, u32[]{:S(2)}) %collective-permute-start.92) | collective-permute-done | bytes 139296 | tf_op jit(solution)/shard_map/ppermute | solution.py:755
  (600 shorter events, 158.5 us)
Async XLA Ops:
  7.2 56.3 %all-gather.5.cloned.1.call-start = ((), (), s32[]{:S(2)}) async-start(), calls=%async_computation.5 | async-start | bytes 1361920 | tf_op jit(solution)/shard_map/all_gather | solution.py:941
  14.8 9.8 %collective-permute-start.2 = (bf16[32,2048]{1,0:T(8,128)(2,1)S(1)}, bf16[32,2048]{1,0:T(8,128)(2,1)S(1)}, u32[]{:S(2)}, u32[]{:S(2)}) collective-permute-start(bf16[32,2048]{1,0:T(8,128)(2,1)S(1)} %pad_maximum_fusion.10), channel_id=1, source_target_pairs={{0,3},{1,2},{2,1},{3,0},{4,7},{5,6},{6,5},{7,4},{8,11},{9,10},{10,... | collective-permute-start | bytes 393224 | tf_op jit(solution)/shard_map/ppermute | solution.py:755
  20.2 11.1 %collective-permute-start.1 = (bf16[32,2048]{1,0:T(8,128)(2,1)S(1)}, bf16[32,2048]{1,0:T(8,128)(2,1)S(1)}, u32[]{:S(2)}, u32[]{:S(2)}) collective-permute-start(bf16[32,2048]{1,0:T(8,128)(2,1)S(1)} %pad_maximum_fusion.10), channel_id=1, source_target_pairs={{0,2},{1,3},{2,0},{3,1},{4,6},{5,7},{6,4},{7,5},{8,10},{9,11},{10,... | collective-permute-start | bytes 393224 | tf_op jit(solution)/shard_map/ppermute | solution.py:755
  20.2 11.1 %collective-permute-start = (bf16[32,2048]{1,0:T(8,128)(2,1)S(1)}, bf16[32,2048]{1,0:T(8,128)(2,1)S(1)}, u32[]{:S(2)}, u32[]{:S(2)}) collective-permute-start(bf16[32,2048]{1,0:T(8,128)(2,1)S(1)} %pad_maximum_fusion.10), channel_id=1, source_target_pairs={{0,1},{1,0},{2,3},{3,2},{4,5},{5,4},{6,7},{7,6},{8,9},{9,8},{10,11... | collective-permute-start | bytes 393224 | tf_op jit(solution)/shard_map/ppermute | solution.py:755
  32.6 100.8 %all-gather.7.cloned.1.call-start = ((), (), s32[]{:S(2)}) async-start(), calls=%async_computation.6 | async-start | bytes 2867200 | tf_op jit(solution)/shard_map/all_gather | solution.py:949
  37.2 17.2 %collective-permute-start.3 = (bf16[1,128,2048]{2,1,0:T(8,128)(2,1)S(1)}, bf16[1,128,2048]{2,1,0:T(8,128)(2,1)S(1)}, u32[]{:S(2)}, u32[]{:S(2)}) collective-permute-start(bf16[1,128,2048]{2,1,0:T(8,128)(2,1)S(1)} %bitcast.137), channel_id=1, source_target_pairs={{0,8},{4,20},{8,0},{12,28},{16,24},{20,4},{24,16},{28,12},{1,9},{5... | collective-permute-start | bytes 1572872 | tf_op jit(solution)/shard_map/ppermute | solution.py:750
  38.7 9.0 %collective-permute-start.24 = (bf16[2,28,1280]{2,1,0:T(8,128)(2,1)}, bf16[2,28,1280]{2,1,0:T(8,128)(2,1)S(1)}, u32[]{:S(2)}, u32[]{:S(2)}) collective-permute-start(bf16[2,28,1280]{2,1,0:T(8,128)(2,1)} %get-tuple-element.148), channel_id=1, source_target_pairs={{0,16},{4,12},{8,24},{12,4},{16,0},{20,28},{24,8},{28,20},{1,17},{... | collective-permute-start | bytes 430088 | tf_op jit(solution)/shard_map/ppermute | solution.py:750
  40.2 12.0 %collective-permute-start.30 = (bf16[2,28,1280]{2,1,0:T(8,128)(2,1)}, bf16[2,28,1280]{2,1,0:T(8,128)(2,1)S(1)}, u32[]{:S(2)}, u32[]{:S(2)}) collective-permute-start(bf16[2,28,1280]{2,1,0:T(8,128)(2,1)} %get-tuple-element.160), channel_id=1, source_target_pairs={{0,28},{4,24},{8,20},{12,16},{16,12},{20,8},{24,4},{28,0},{1,29},{... | collective-permute-start | bytes 430088 | tf_op jit(solution)/shard_map/ppermute | solution.py:750
  40.8 14.1 %collective-permute-start.25 = (bf16[2,28,1280]{2,1,0:T(8,128)(2,1)}, bf16[2,28,1280]{2,1,0:T(8,128)(2,1)S(1)}, u32[]{:S(2)}, u32[]{:S(2)}) collective-permute-start(bf16[2,28,1280]{2,1,0:T(8,128)(2,1)} %get-tuple-element.150), channel_id=1, source_target_pairs={{0,8},{4,20},{8,0},{12,28},{16,24},{20,4},{24,16},{28,12},{1,9},{5... | collective-permute-start | bytes 430088 | tf_op jit(solution)/shard_map/ppermute | solution.py:750
  41.3 15.3 %collective-permute-start.26 = (bf16[2,28,1280]{2,1,0:T(8,128)(2,1)}, bf16[2,28,1280]{2,1,0:T(8,128)(2,1)S(1)}, u32[]{:S(2)}, u32[]{:S(2)}) collective-permute-start(bf16[2,28,1280]{2,1,0:T(8,128)(2,1)} %get-tuple-element.152), channel_id=1, source_target_pairs={{0,24},{4,28},{8,16},{12,20},{16,8},{20,12},{24,0},{28,4},{1,25},{... | collective-permute-start | bytes 430088 | tf_op jit(solution)/shard_map/ppermute | solution.py:750
  47.8 8.9 %collective-permute-start.27 = (bf16[2,28,1280]{2,1,0:T(8,128)(2,1)}, bf16[2,28,1280]{2,1,0:T(8,128)(2,1)S(1)}, u32[]{:S(2)}, u32[]{:S(2)}) collective-permute-start(bf16[2,28,1280]{2,1,0:T(8,128)(2,1)} %get-tuple-element.154), channel_id=1, source_target_pairs={{0,4},{4,0},{8,12},{12,8},{16,20},{20,16},{24,28},{28,24},{1,5},{5... | collective-permute-start | bytes 430088 | tf_op jit(solution)/shard_map/ppermute | solution.py:750
  52.2 7.0 %collective-permute-start.28 = (bf16[2,28,1280]{2,1,0:T(8,128)(2,1)}, bf16[2,28,1280]{2,1,0:T(8,128)(2,1)S(1)}, u32[]{:S(2)}, u32[]{:S(2)}) collective-permute-start(bf16[2,28,1280]{2,1,0:T(8,128)(2,1)} %get-tuple-element.156), channel_id=1, source_target_pairs={{0,12},{4,16},{8,4},{12,24},{16,28},{20,0},{24,20},{28,8},{1,13},{... | collective-permute-start | bytes 430088 | tf_op jit(solution)/shard_map/ppermute | solution.py:750
  63.5 133.5 %all-gather.9.cloned.1.call-start = ((), (), s32[]{:S(2)}) async-start(), calls=%async_computation.7 | async-start | bytes 2867200 | tf_op jit(solution)/shard_map/all_gather | solution.py:990
  63.5 14.9 %collective-permute-start.4 = (bf16[2,128,2048]{2,1,0:T(8,128)(2,1)S(1)}, bf16[2,128,2048]{2,1,0:T(8,128)(2,1)S(1)}, u32[]{:S(2)}, u32[]{:S(2)}) collective-permute-start(bf16[2,128,2048]{2,1,0:T(8,128)(2,1)S(1)} %pad_maximum_fusion.4.refs_5_.refs_22_.refs_7_.refs_1_.refs_9_), channel_id=1, source_target_pairs={{0,16},{4,12},{8,24},{12,4},{16,0},{20,28},{24,8},{28,20},{1,17},{... | collective-permute-start | bytes 3145736 | tf_op jit(solution)/shard_map/ppermute | solution.py:750
  67.5 13.8 %collective-permute-start.5 = (bf16[2,128,2048]{2,1,0:T(8,128)(2,1)S(1)}, bf16[2,128,2048]{2,1,0:T(8,128)(2,1)S(1)}, u32[]{:S(2)}, u32[]{:S(2)}) collective-permute-start(bf16[2,128,2048]{2,1,0:T(8,128)(2,1)S(1)} %pad_maximum_fusion.4.refs_5_.refs_22_.refs_7_.refs_1_.refs_9_), channel_id=1, source_target_pairs={{0,4},{4,0},{8,12},{12,8},{16,20},{20,16},{24,28},{28,24},{1,5},{5... | collective-permute-start | bytes 3145736 | tf_op jit(solution)/shard_map/ppermute | solution.py:750
  91.8 10.4 %collective-permute-start.10 = (bf16[160,384]{1,0:T(8,128)(2,1)}, bf16[160,384]{1,0:T(8,128)(2,1)S(1)}, u32[]{:S(2)}, u32[]{:S(2)}) collective-permute-start(bf16[160,384]{1,0:T(8,128)(2,1)} %get-tuple-element.139.refs_1_.refs_9_.refs_13_.refs_5_), channel_id=1, source_target_pairs={{0,4},{4,0},{8,12},{12,8},{16,20},{20,16},{24,28},{28,24},{1,5},{5... | collective-permute-start | bytes 368648 | tf_op jit(solution)/shard_map/ppermute | solution.py:750
  114.9 12.0 %collective-permute-start.16 = (bf16[160,896]{1,0:T(8,128)(2,1)}, bf16[160,896]{1,0:T(8,128)(2,1)S(1)}, u32[]{:S(2)}, u32[]{:S(2)}) collective-permute-start(bf16[160,896]{1,0:T(8,128)(2,1)} %get-tuple-element.143.refs_0_), channel_id=1, source_target_pairs={{0,24},{4,28},{8,16},{12,20},{16,8},{20,12},{24,0},{28,4},{1,25},{... | collective-permute-start | bytes 860168 | tf_op jit(solution)/shard_map/ppermute | solution.py:750
  116.7 14.7 %collective-permute-start.15 = (bf16[160,896]{1,0:T(8,128)(2,1)}, bf16[160,896]{1,0:T(8,128)(2,1)S(1)}, u32[]{:S(2)}, u32[]{:S(2)}) collective-permute-start(bf16[160,896]{1,0:T(8,128)(2,1)} %get-tuple-element.143.refs_0_), channel_id=1, source_target_pairs={{0,8},{4,20},{8,0},{12,28},{16,24},{20,4},{24,16},{28,12},{1,9},{5... | collective-permute-start | bytes 860168 | tf_op jit(solution)/shard_map/ppermute | solution.py:750
  117.8 13.6 %collective-permute-start.14 = (bf16[160,896]{1,0:T(8,128)(2,1)}, bf16[160,896]{1,0:T(8,128)(2,1)S(1)}, u32[]{:S(2)}, u32[]{:S(2)}) collective-permute-start(bf16[160,896]{1,0:T(8,128)(2,1)} %get-tuple-element.143.refs_0_), channel_id=1, source_target_pairs={{0,16},{4,12},{8,24},{12,4},{16,0},{20,28},{24,8},{28,20},{1,17},{... | collective-permute-start | bytes 860168 | tf_op jit(solution)/shard_map/ppermute | solution.py:750
  118.5 8.4 %collective-permute-start.23 = (bf16[32,2048]{1,0:T(8,128)(2,1)S(1)}, bf16[32,2048]{1,0:T(8,128)(2,1)S(1)}, u32[]{:S(2)}, u32[]{:S(2)}) collective-permute-start(bf16[32,2048]{1,0:T(8,128)(2,1)S(1)} %fusion.41), channel_id=1, source_target_pairs={{0,3},{1,2},{2,1},{3,0},{4,7},{5,6},{6,5},{7,4},{8,11},{9,10},{10,... | collective-permute-start | bytes 393224 | tf_op jit(solution)/shard_map/ppermute | solution.py:755
  121.0 9.9 %collective-permute-start.22 = (bf16[32,2048]{1,0:T(8,128)(2,1)S(1)}, bf16[32,2048]{1,0:T(8,128)(2,1)S(1)}, u32[]{:S(2)}, u32[]{:S(2)}) collective-permute-start(bf16[32,2048]{1,0:T(8,128)(2,1)S(1)} %fusion.41), channel_id=1, source_target_pairs={{0,2},{1,3},{2,0},{3,1},{4,6},{5,7},{6,4},{7,5},{8,10},{9,11},{10,... | collective-permute-start | bytes 393224 | tf_op jit(solution)/shard_map/ppermute | solution.py:755
  144.8 11.1 %collective-permute-start.31 = (bf16[640,896]{1,0:T(8,128)(2,1)}, bf16[640,896]{1,0:T(8,128)(2,1)S(1)}, u32[]{:S(2)}, u32[]{:S(2)}) collective-permute-start(bf16[640,896]{1,0:T(8,128)(2,1)} %get-tuple-element.166), channel_id=1, source_target_pairs={{0,4},{4,0},{8,12},{12,8},{16,20},{20,16},{24,28},{28,24},{1,5},{5... | collective-permute-start | bytes 3440648 | tf_op jit(solution)/shard_map/ppermute | solution.py:750
  145.0 86.9 %all-gather.11.cloned.1.call-start = ((), (), s32[]{:S(2)}) async-start(), calls=%async_computation.8 | async-start | bytes 1361920 | tf_op jit(solution)/shard_map/all_gather | solution.py:1003
  145.1 9.2 %collective-permute-start.34 = (bf16[1,128,2048]{2,1,0:T(8,128)(2,1)S(1)}, bf16[1,128,2048]{2,1,0:T(8,128)(2,1)S(1)}, u32[]{:S(2)}, u32[]{:S(2)}) collective-permute-start(bf16[1,128,2048]{2,1,0:T(8,128)(2,1)S(1)} %maximum_bitcast_fusion), channel_id=1, source_target_pairs={{0,8},{4,20},{8,0},{12,28},{16,24},{20,4},{24,16},{28,12},{1,9},{5... | collective-permute-start | bytes 1572872 | tf_op jit(solution)/shard_map/ppermute | solution.py:750
  154.4 21.0 %collective-permute-start.35 = (bf16[2,128,2048]{2,1,0:T(8,128)(2,1)S(1)}, bf16[2,128,2048]{2,1,0:T(8,128)(2,1)S(1)}, u32[]{:S(2)}, u32[]{:S(2)}) collective-permute-start(bf16[2,128,2048]{2,1,0:T(8,128)(2,1)S(1)} %pad_maximum_fusion.5.refs_6_.refs_22_.refs_7_.refs_1_.refs_9_), channel_id=1, source_target_pairs={{0,16},{4,12},{8,24},{12,4},{16,0},{20,28},{24,8},{28,20},{1,17},{... | collective-permute-start | bytes 3145736 | tf_op jit(solution)/shard_map/ppermute | solution.py:750
  156.2 16.0 %collective-permute-start.32 = (bf16[2,160,896]{2,1,0:T(8,128)(2,1)S(1)}, bf16[2,160,896]{2,1,0:T(8,128)(2,1)S(1)}, u32[]{:S(2)}, u32[]{:S(2)}) collective-permute-start(bf16[2,160,896]{2,1,0:T(8,128)(2,1)S(1)} %bitcast.145), channel_id=1, source_target_pairs={{0,8},{4,20},{8,0},{12,28},{16,24},{20,4},{24,16},{28,12},{1,9},{5... | collective-permute-start | bytes 1720328 | tf_op jit(solution)/shard_map/ppermute | solution.py:750
  157.1 20.1 %collective-permute-start.36 = (bf16[2,128,2048]{2,1,0:T(8,128)(2,1)S(1)}, bf16[2,128,2048]{2,1,0:T(8,128)(2,1)S(1)}, u32[]{:S(2)}, u32[]{:S(2)}) collective-permute-start(bf16[2,128,2048]{2,1,0:T(8,128)(2,1)S(1)} %pad_maximum_fusion.5.refs_6_.refs_22_.refs_7_.refs_1_.refs_9_), channel_id=1, source_target_pairs={{0,4},{4,0},{8,12},{12,8},{16,20},{20,16},{24,28},{28,24},{1,5},{5... | collective-permute-start | bytes 3145736 | tf_op jit(solution)/shard_map/ppermute | solution.py:750
  197.0 161.7 %reduce-scatter.13.cloned.1.call-start = ((), (), s32[]{:S(2)}) async-start(), calls=%async_computation.11 | async-start | bytes 1361920
  197.1 18.0 %collective-permute-start.54 = (bf16[160,896]{1,0:T(8,128)(2,1)S(1)}, bf16[160,896]{1,0:T(8,128)(2,1)S(1)}, u32[]{:S(2)}, u32[]{:S(2)}) collective-permute-start(bf16[160,896]{1,0:T(8,128)(2,1)S(1)} %bitcast.154), channel_id=1, source_target_pairs={{0,24},{4,28},{8,16},{12,20},{16,8},{20,12},{24,0},{28,4},{1,25},{... | collective-permute-start | bytes 860168 | tf_op jit(solution)/shard_map/ppermute | solution.py:750
  198.6 14.2 %collective-permute-start.53 = (bf16[160,896]{1,0:T(8,128)(2,1)S(1)}, bf16[160,896]{1,0:T(8,128)(2,1)S(1)}, u32[]{:S(2)}, u32[]{:S(2)}) collective-permute-start(bf16[160,896]{1,0:T(8,128)(2,1)S(1)} %bitcast.155), channel_id=1, source_target_pairs={{0,8},{4,20},{8,0},{12,28},{16,24},{20,4},{24,16},{28,12},{1,9},{5... | collective-permute-start | bytes 860168 | tf_op jit(solution)/shard_map/ppermute | solution.py:750
  199.7 13.4 %collective-permute-start.52 = (bf16[160,896]{1,0:T(8,128)(2,1)S(1)}, bf16[160,896]{1,0:T(8,128)(2,1)S(1)}, u32[]{:S(2)}, u32[]{:S(2)}) collective-permute-start(bf16[160,896]{1,0:T(8,128)(2,1)S(1)} %bitcast.156), channel_id=1, source_target_pairs={{0,16},{4,12},{8,24},{12,4},{16,0},{20,28},{24,8},{28,20},{1,17},{... | collective-permute-start | bytes 860168 | tf_op jit(solution)/shard_map/ppermute | solution.py:750
  213.7 10.8 %collective-permute-start.47 = (bf16[160,896]{1,0:T(8,128)(2,1)}, bf16[160,896]{1,0:T(8,128)(2,1)S(1)}, u32[]{:S(2)}, u32[]{:S(2)}) collective-permute-start(bf16[160,896]{1,0:T(8,128)(2,1)} %get-tuple-element.179.refs_0_), channel_id=1, source_target_pairs={{0,24},{4,28},{8,16},{12,20},{16,8},{20,12},{24,0},{28,4},{1,25},{... | collective-permute-start | bytes 860168 | tf_op jit(solution)/shard_map/ppermute | solution.py:750
  215.1 14.5 %collective-permute-start.46 = (bf16[160,896]{1,0:T(8,128)(2,1)}, bf16[160,896]{1,0:T(8,128)(2,1)S(1)}, u32[]{:S(2)}, u32[]{:S(2)}) collective-permute-start(bf16[160,896]{1,0:T(8,128)(2,1)} %get-tuple-element.179.refs_0_), channel_id=1, source_target_pairs={{0,8},{4,20},{8,0},{12,28},{16,24},{20,4},{24,16},{28,12},{1,9},{5... | collective-permute-start | bytes 860168 | tf_op jit(solution)/shard_map/ppermute | solution.py:750
  216.3 13.7 %collective-permute-start.45 = (bf16[160,896]{1,0:T(8,128)(2,1)}, bf16[160,896]{1,0:T(8,128)(2,1)S(1)}, u32[]{:S(2)}, u32[]{:S(2)}) collective-permute-start(bf16[160,896]{1,0:T(8,128)(2,1)} %get-tuple-element.179.refs_0_), channel_id=1, source_target_pairs={{0,16},{4,12},{8,24},{12,4},{16,0},{20,28},{24,8},{28,20},{1,17},{... | collective-permute-start | bytes 860168 | tf_op jit(solution)/shard_map/ppermute | solution.py:750
  217.2 13.0 %collective-permute-start.48 = (bf16[160,896]{1,0:T(8,128)(2,1)}, bf16[160,896]{1,0:T(8,128)(2,1)S(1)}, u32[]{:S(2)}, u32[]{:S(2)}) collective-permute-start(bf16[160,896]{1,0:T(8,128)(2,1)} %get-tuple-element.179.refs_0_), channel_id=1, source_target_pairs={{0,4},{4,0},{8,12},{12,8},{16,20},{20,16},{24,28},{28,24},{1,5},{5... | collective-permute-start | bytes 860168 | tf_op jit(solution)/shard_map/ppermute | solution.py:750
  217.2 12.9 %collective-permute-start.58 = (bf16[160,896]{1,0:T(8,128)(2,1)S(1)}, bf16[160,896]{1,0:T(8,128)(2,1)S(1)}, u32[]{:S(2)}, u32[]{:S(2)}) collective-permute-start(bf16[160,896]{1,0:T(8,128)(2,1)S(1)} %collective-permute-done.54.refs_11_), channel_id=1, source_target_pairs={{0,4},{4,0},{8,12},{12,8},{16,20},{20,16},{24,28},{28,24},{1,5},{5... | collective-permute-start | bytes 860168 | tf_op jit(solution)/shard_map/ppermute | solution.py:750
  253.1 9.8 %collective-permute-start.60 = (bf16[2,160,896]{2,1,0:T(8,128)(2,1)S(1)}, bf16[2,160,896]{2,1,0:T(8,128)(2,1)S(1)}, u32[]{:S(2)}, u32[]{:S(2)}) collective-permute-start(bf16[2,160,896]{2,1,0:T(8,128)(2,1)S(1)} %bitcast.144), channel_id=1, source_target_pairs={{0,8},{4,20},{8,0},{12,28},{16,24},{20,4},{24,16},{28,12},{1,9},{5... | collective-permute-start | bytes 1720328 | tf_op jit(solution)/shard_map/ppermute | solution.py:750
  289.0 116.8 %reduce-scatter.11.cloned.1.call-start = ((), (), s32[]{:S(2)}) async-start(), calls=%async_computation.10 | async-start | bytes 2867200 | tf_op jit(solution)/shard_map/reduce_scatter | solution.py:1015
  310.6 9.2 %collective-permute-start.74 = (bf16[512,896]{1,0:T(8,128)(2,1)S(1)}, bf16[512,896]{1,0:T(8,128)(2,1)S(1)}, u32[]{:S(2)}, u32[]{:S(2)}) collective-permute-start(bf16[512,896]{1,0:T(8,128)(2,1)S(1)} %convolution_convert_fusion.6), channel_id=1, source_target_pairs={{0,4},{4,0},{8,12},{12,8},{16,20},{20,16},{24,28},{28,24},{1,5},{5... | collective-permute-start | bytes 2752520 | tf_op jit(solution)/shard_map/ppermute | solution.py:750
  313.3 7.8 %collective-permute-start.75 = (bf16[512,1152]{1,0:T(8,128)(2,1)}, bf16[512,1152]{1,0:T(8,128)(2,1)}, u32[]{:S(2)}, u32[]{:S(2)}) collective-permute-start(bf16[512,1152]{1,0:T(8,128)(2,1)} %fusion.5), channel_id=1, source_target_pairs={{0,4},{4,0},{8,12},{12,8},{16,20},{20,16},{24,28},{28,24},{1,5},{5... | collective-permute-start | bytes 3538952 | tf_op jit(solution)/shard_map/ppermute | solution.py:750
  313.8 105.8 %reduce-scatter.9.cloned.1.call-start = ((), (), s32[]{:S(2)}) async-start(), calls=%async_computation.9 | async-start | bytes 2867200 | tf_op jit(solution)/shard_map/reduce_scatter | solution.py:1015
  314.1 11.7 %collective-permute-start.69 = (bf16[160,896]{1,0:T(8,128)(2,1)}, bf16[160,896]{1,0:T(8,128)(2,1)S(1)}, u32[]{:S(2)}, u32[]{:S(2)}) collective-permute-start(bf16[160,896]{1,0:T(8,128)(2,1)} %get-tuple-element.210.refs_1_), channel_id=1, source_target_pairs={{0,24},{4,28},{8,16},{12,20},{16,8},{20,12},{24,0},{28,4},{1,25},{... | collective-permute-start | bytes 860168 | tf_op jit(solution)/shard_map/ppermute | solution.py:750
  315.6 14.1 %collective-permute-start.68 = (bf16[160,896]{1,0:T(8,128)(2,1)}, bf16[160,896]{1,0:T(8,128)(2,1)S(1)}, u32[]{:S(2)}, u32[]{:S(2)}) collective-permute-start(bf16[160,896]{1,0:T(8,128)(2,1)} %get-tuple-element.210.refs_1_), channel_id=1, source_target_pairs={{0,8},{4,20},{8,0},{12,28},{16,24},{20,4},{24,16},{28,12},{1,9},{5... | collective-permute-start | bytes 860168 | tf_op jit(solution)/shard_map/ppermute | solution.py:750
  319.2 11.1 %collective-permute-start.65 = (bf16[640,896]{1,0:T(8,128)(2,1)S(1)}, bf16[640,896]{1,0:T(8,128)(2,1)S(1)}, u32[]{:S(2)}, u32[]{:S(2)}) collective-permute-start(bf16[640,896]{1,0:T(8,128)(2,1)S(1)} %convolution_convert_fusion.2), channel_id=1, source_target_pairs={{0,4},{4,0},{8,12},{12,8},{16,20},{20,16},{24,28},{28,24},{1,5},{5... | collective-permute-start | bytes 3440648 | tf_op jit(solution)/shard_map/ppermute | solution.py:750
  319.8 10.4 %collective-permute-start.67 = (bf16[160,896]{1,0:T(8,128)(2,1)}, bf16[160,896]{1,0:T(8,128)(2,1)S(1)}, u32[]{:S(2)}, u32[]{:S(2)}) collective-permute-start(bf16[160,896]{1,0:T(8,128)(2,1)} %get-tuple-element.210.refs_1_), channel_id=1, source_target_pairs={{0,16},{4,12},{8,24},{12,4},{16,0},{20,28},{24,8},{28,20},{1,17},{... | collective-permute-start | bytes 860168 | tf_op jit(solution)/shard_map/ppermute | solution.py:750
  324.8 23.0 %collective-permute-start.76 = (bf16[2,128,2048]{2,1,0:T(8,128)(2,1)}, bf16[2,128,2048]{2,1,0:T(8,128)(2,1)S(1)}, u32[]{:S(2)}, u32[]{:S(2)}) collective-permute-start(bf16[2,128,2048]{2,1,0:T(8,128)(2,1)} %fusion.10), channel_id=1, source_target_pairs={{0,8},{4,20},{8,0},{12,28},{16,24},{20,4},{24,16},{28,12},{1,9},{5... | collective-permute-start | bytes 3145736 | tf_op jit(solution)/shard_map/ppermute | solution.py:750
  325.8 8.7 %collective-permute-start.70 = (bf16[160,896]{1,0:T(8,128)(2,1)}, bf16[160,896]{1,0:T(8,128)(2,1)S(1)}, u32[]{:S(2)}, u32[]{:S(2)}) collective-permute-start(bf16[160,896]{1,0:T(8,128)(2,1)} %get-tuple-element.210.refs_1_), channel_id=1, source_target_pairs={{0,4},{4,0},{8,12},{12,8},{16,20},{20,16},{24,28},{28,24},{1,5},{5... | collective-permute-start | bytes 860168 | tf_op jit(solution)/shard_map/ppermute | solution.py:750
  333.4 14.4 %collective-permute-start.66 = (bf16[2,160,896]{2,1,0:T(8,128)(2,1)S(1)}, bf16[2,160,896]{2,1,0:T(8,128)(2,1)S(1)}, u32[]{:S(2)}, u32[]{:S(2)}) collective-permute-start(bf16[2,160,896]{2,1,0:T(8,128)(2,1)S(1)} %bitcast.142), channel_id=1, source_target_pairs={{0,8},{4,20},{8,0},{12,28},{16,24},{20,4},{24,16},{28,12},{1,9},{5... | collective-permute-start | bytes 1720328 | tf_op jit(solution)/shard_map/ppermute | solution.py:750
  351.3 9.9 %collective-permute-start.78 = (bf16[2,160,896]{2,1,0:T(8,128)(2,1)S(1)}, bf16[2,160,896]{2,1,0:T(8,128)(2,1)}, u32[]{:S(2)}, u32[]{:S(2)}) collective-permute-start(bf16[2,160,896]{2,1,0:T(8,128)(2,1)S(1)} %bitcast.143), channel_id=1, source_target_pairs={{0,8},{4,20},{8,0},{12,28},{16,24},{20,4},{24,16},{28,12},{1,9},{5... | collective-permute-start | bytes 1720328 | tf_op jit(solution)/shard_map/ppermute | solution.py:750
  358.8 103.7 %reduce-scatter.15.cloned.1.call-start = ((), (), s32[]{:S(2)}) async-start(), calls=%async_computation.12 | async-start | bytes 1361920
  363.4 7.1 %collective-permute-start.79 = (bf16[1,160,896]{2,1,0:T(8,128)(2,1)S(1)}, bf16[1,160,896]{2,1,0:T(8,128)(2,1)S(1)}, u32[]{:S(2)}, u32[]{:S(2)}) collective-permute-start(bf16[1,160,896]{2,1,0:T(8,128)(2,1)S(1)} %slice.570), channel_id=1, source_target_pairs={{0,16},{4,12},{8,24},{12,4},{16,0},{20,28},{24,8},{28,20},{1,17},{... | collective-permute-start | bytes 860168 | tf_op jit(solution)/shard_map/ppermute | solution.py:750
  379.7 14.7 %collective-permute-start.81 = (bf16[1,128,2048]{2,1,0:T(8,128)(2,1)S(1)}, bf16[1,128,2048]{2,1,0:T(8,128)(2,1)S(1)}, u32[]{:S(2)}, u32[]{:S(2)}) collective-permute-start(bf16[1,128,2048]{2,1,0:T(8,128)(2,1)S(1)} %slice.568), channel_id=1, source_target_pairs={{0,16},{4,12},{8,24},{12,4},{16,0},{20,28},{24,8},{28,20},{1,17},{... | collective-permute-start | bytes 1572872 | tf_op jit(solution)/shard_map/ppermute | solution.py:750
  381.0 13.4 %collective-permute-start.80 = (bf16[1,160,896]{2,1,0:T(8,128)(2,1)S(1)}, bf16[1,160,896]{2,1,0:T(8,128)(2,1)S(1)}, u32[]{:S(2)}, u32[]{:S(2)}) collective-permute-start(bf16[1,160,896]{2,1,0:T(8,128)(2,1)S(1)} %slice.569), channel_id=1, source_target_pairs={{0,16},{4,12},{8,24},{12,4},{16,0},{20,28},{24,8},{28,20},{1,17},{... | collective-permute-start | bytes 860168 | tf_op jit(solution)/shard_map/ppermute | solution.py:750
  399.5 14.2 %collective-permute-start.85 = (bf16[512,896]{1,0:T(8,128)(2,1)S(1)}, bf16[512,896]{1,0:T(8,128)(2,1)}, u32[]{:S(2)}, u32[]{:S(2)}) collective-permute-start(bf16[512,896]{1,0:T(8,128)(2,1)S(1)} %select_convert_fusion.1), channel_id=1, source_target_pairs={{0,4},{4,0},{8,12},{12,8},{16,20},{20,16},{24,28},{28,24},{1,5},{5... | collective-permute-start | bytes 2752520 | tf_op jit(solution)/shard_map/ppermute | solution.py:750
  405.4 9.7 %collective-permute-start.86 = (bf16[512,896]{1,0:T(8,128)(2,1)}, bf16[512,896]{1,0:T(8,128)(2,1)}, u32[]{:S(2)}, u32[]{:S(2)}) collective-permute-start(bf16[512,896]{1,0:T(8,128)(2,1)} %convolution_convert_fusion.5), channel_id=1, source_target_pairs={{0,4},{4,0},{8,12},{12,8},{16,20},{20,16},{24,28},{28,24},{1,5},{5... | collective-permute-start | bytes 2752520 | tf_op jit(solution)/shard_map/ppermute | solution.py:750
  418.4 16.6 %collective-permute-start.87 = (bf16[2,128,1792]{2,1,0:T(8,128)(2,1)}, bf16[2,128,1792]{2,1,0:T(8,128)(2,1)}, u32[]{:S(2)}, u32[]{:S(2)}) collective-permute-start(bf16[2,128,1792]{2,1,0:T(8,128)(2,1)} %fusion.13), channel_id=1, source_target_pairs={{0,8},{4,20},{8,0},{12,28},{16,24},{20,4},{24,16},{28,12},{1,9},{5... | collective-permute-start | bytes 2752520 | tf_op jit(solution)/shard_map/ppermute | solution.py:750
  442.2 13.0 %collective-permute-start.90 = (bf16[1,128,2176]{2,1,0:T(8,128)(2,1)}, bf16[1,128,2176]{2,1,0:T(8,128)(2,1)}, u32[]{:S(2)}, u32[]{:S(2)}) collective-permute-start(bf16[1,128,2176]{2,1,0:T(8,128)(2,1)} %fusion.21), channel_id=1, source_target_pairs={{0,16},{4,12},{8,24},{12,4},{16,0},{20,28},{24,8},{28,20},{1,17},{... | collective-permute-start | bytes 1671176 | tf_op jit(solution)/shard_map/ppermute | solution.py:750
  444.0 46.9 %collective-permute-start.94 = (bf16[32,2048]{1,0:T(8,128)(2,1)}, bf16[32,2048]{1,0:T(8,128)(2,1)}, u32[]{:S(2)}, u32[]{:S(2)}) collective-permute-start(bf16[32,2048]{1,0:T(8,128)(2,1)} %get-tuple-element.308), channel_id=1, source_target_pairs={{0,1},{1,0},{2,3},{3,2},{4,5},{5,4},{6,7},{7,6},{8,9},{9,8},{10,11... | collective-permute-start | bytes 393224 | tf_op jit(solution)/shard_map/ppermute | solution.py:755
  444.0 46.6 %collective-permute-start.96 = (bf16[32,2048]{1,0:T(8,128)(2,1)}, bf16[32,2048]{1,0:T(8,128)(2,1)}, u32[]{:S(2)}, u32[]{:S(2)}) collective-permute-start(bf16[32,2048]{1,0:T(8,128)(2,1)} %get-tuple-element.309), channel_id=1, source_target_pairs={{0,3},{1,2},{2,1},{3,0},{4,7},{5,6},{6,5},{7,4},{8,11},{9,10},{10,... | collective-permute-start | bytes 393224 | tf_op jit(solution)/shard_map/ppermute | solution.py:755
  451.5 20.2 %all-to-all-start = ((bf16[8,2,28,1280]{3,1,2,0:T(2,128)(2,1)}), bf16[8,2,28,1280]{3,1,2,0:T(2,128)(2,1)S(1)}, u32[]{:S(2)}, u32[]{:S(2)}) async-start(bf16[8,2,28,1280]{3,1,2,0:T(2,128)(2,1)} %copy.102), calls=%async_computation.2 | async-start | bytes 2293760 | tf_op jit(solution)/shard_map/all_to_all | solution.py:884
  472.4 9.3 %collective-permute-start.91 = (bf16[32,2176]{1,0:T(8,128)(2,1)S(1)}, bf16[32,2176]{1,0:T(8,128)(2,1)S(1)}, u32[]{:S(2)}, u32[]{:S(2)}) collective-permute-start(bf16[32,2176]{1,0:T(8,128)(2,1)S(1)} %get-tuple-element.303), channel_id=1, source_target_pairs={{0,1},{1,0},{2,3},{3,2},{4,5},{5,4},{6,7},{7,6},{8,9},{9,8},{10,11... | collective-permute-start | bytes 417800 | tf_op jit(solution)/shard_map/ppermute | solution.py:755
  473.6 10.5 %collective-permute-start.93 = (bf16[32,2176]{1,0:T(8,128)(2,1)S(1)}, bf16[32,2176]{1,0:T(8,128)(2,1)S(1)}, u32[]{:S(2)}, u32[]{:S(2)}) collective-permute-start(bf16[32,2176]{1,0:T(8,128)(2,1)S(1)} %get-tuple-element.304), channel_id=1, source_target_pairs={{0,3},{1,2},{2,1},{3,0},{4,7},{5,6},{6,5},{7,4},{8,11},{9,10},{10,... | collective-permute-start | bytes 417800 | tf_op jit(solution)/shard_map/ppermute | solution.py:755
  475.4 14.1 %collective-permute-start.92 = (bf16[32,2176]{1,0:T(8,128)(2,1)S(1)}, bf16[32,2176]{1,0:T(8,128)(2,1)}, u32[]{:S(2)}, u32[]{:S(2)}) collective-permute-start(bf16[32,2176]{1,0:T(8,128)(2,1)S(1)} %get-tuple-element.305), channel_id=1, source_target_pairs={{0,2},{1,3},{2,0},{3,1},{4,6},{5,7},{6,4},{7,5},{8,10},{9,11},{10,... | collective-permute-start | bytes 417800 | tf_op jit(solution)/shard_map/ppermute | solution.py:755
  481.7 9.1 %collective-permute-start.95 = (bf16[32,2048]{1,0:T(8,128)(2,1)}, bf16[32,2048]{1,0:T(8,128)(2,1)S(1)}, u32[]{:S(2)}, u32[]{:S(2)}) collective-permute-start(bf16[32,2048]{1,0:T(8,128)(2,1)} %get-tuple-element.310), channel_id=1, source_target_pairs={{0,2},{1,3},{2,0},{3,1},{4,6},{5,7},{6,4},{7,5},{8,10},{9,11},{10,... | collective-permute-start | bytes 393224 | tf_op jit(solution)/shard_map/ppermute | solution.py:755
  (172 other events, 858.5 us)
Sparse Core Ops, SparseCore 0:
  32.7 28.7 all-gather.4
  63.6 49.7 all-gather.6
  145.1 48.3 all-gather.8
  197.1 27.4 all-gather.10
  289.1 26.5 reduce-scatter.12
  317.9 46.3 reduce-scatter.10
  366.7 46.4 reduce-scatter.8
  430.3 32.0 reduce-scatter.14

commit v3 on v2

--- a/solution.py
+++ b/solution.py
@@ -48,7 +48,79 @@
     return lax.dot_general(left, right, (((1,), (1,)), ((), ())), preferred_element_type=f32)
 
 
-def run(kernel, ins, in_specs, outs, out_specs, scratch, flops, vmem=60):
+class Lazy:
+    def __init__(self, ref, copy):
+        self.ref, self.copy = ref, copy
+
+    def __getitem__(self, at):
+        if self.copy is not None:
+            self.copy.wait()
+            self.copy = None
+        return self.ref[at]
+
+
+class Late:
+    def __init__(self, ref, target, sem):
+        self.ref, self.copy = ref, pltpu.make_async_copy(ref, target, sem)
+        self.sent = False
+
+    def __getitem__(self, at):
+        return self.ref[at]
+
+    def __setitem__(self, at, value):
+        self.ref[at] = value
+
+    def flush(self):
+        self.copy.start()
+        self.sent = True
+
+
+def lazily(kernel, ins, in_specs, outs, out_specs, scratch):
+    n_in, n_out = len(ins), len(outs)
+    staged = [i for i, spec in enumerate(in_specs) if spec is VMEM]
+    late = [i for i, spec in enumerate(out_specs) if spec is VMEM]
+    n_scratch = len(scratch)
+
+    def whole(*refs):
+        refs = list(refs)
+        own = refs[n_in + n_out + n_scratch :]
+        ins_v, outs_v = own[: len(staged)], own[len(staged) : len(staged) + len(late)]
+        in_sems, out_sems = own[-2:]
+        for k, i in enumerate(staged):
+            copy = pltpu.make_async_copy(refs[i], ins_v[k], in_sems.at[k])
+            copy.start()
+            refs[i] = Lazy(ins_v[k], copy)
+        results = []
+        for k, i in enumerate(late):
+            results.append(Late(outs_v[k], refs[n_in + i], out_sems.at[k]))
+            refs[n_in + i] = results[-1]
+        kernel(*refs[: n_in + n_out + n_scratch])
+        for i in staged:
+            if refs[i].copy is not None:
+                refs[i].copy.wait()
+        for result in results:
+            if not result.sent:
+                result.flush()
+        for result in results:
+            result.copy.wait()
+
+    scratch = [
+        *scratch,
+        *[pltpu.VMEM(ins[i].shape, ins[i].dtype) for i in staged],
+        *[pltpu.VMEM(outs[i].shape, outs[i].dtype) for i in late],
+        DMA((max(len(staged), 1),)),
+        DMA((max(len(late), 1),)),
+    ]
+    in_specs = [ANY if spec is VMEM else spec for spec in in_specs]
+    out_specs = [ANY if spec is VMEM else spec for spec in out_specs]
+    return whole, in_specs, out_specs, scratch
+
+
+def run(kernel, ins, in_specs, outs, out_specs, scratch, flops, vmem=60, lazy=False):
+    if lazy:
+        kernel, in_specs, out_specs, scratch = lazily(
+            kernel, ins, in_specs, outs, out_specs, scratch
+        )
     moved = sum(math.prod(x.shape) * x.dtype.itemsize for x in [*ins, *outs])
     return pl.pallas_call(
         kernel,
@@ -419,6 +491,8 @@
                 ref[:, g * HEAD : (g + 1) * HEAD] = key_out
                 ref[:, KV_W + g * HEAD : KV_W + (g + 1) * HEAD] = value_out
             wholes.append(dot(keys_t[g * HEAD : (g + 1) * HEAD, :], score_grads[...]))
+        keep_ref.flush()
+        send_ref.flush()
         whole = lanes_to_heads(wholes, tokens) * SCALE
         cos, sin = cos_ref[...], sin_ref[...]
         for i in range(QW // 128):
@@ -445,6 +519,7 @@
         ],
         20 * tokens * n * tokens * QW,
         60,
+        lazy=True,
     )
 
 
@@ -471,6 +546,7 @@
         [VMEM],
         [pltpu.VMEM((n * step, QW), bf16), DMA((n,))],
         2 * tokens * n * step * QW,
+        lazy=True,
     )[0]
 
 
@@ -493,6 +569,7 @@
         keys = rotated_back(total[:, :KV_W], cos_ref[...], sin_ref[...])
         part = jnp.concatenate([keys, total[:, KV_W:]], axis=1).astype(bf16)
         part_ref[...] = part
+        part_ref.flush()
         for w in waits:
             w.wait()
         rel = rel_ref[...] + dot_cols(part, weight[...])
@@ -516,6 +593,7 @@
         [VMEM] * 4,
         [pltpu.VMEM((n * step, 2 * KV_W), bf16), DMA((n,))],
         2 * tokens * n * step * (2 * KV_W + 2 * D),
+        lazy=True,
     )
 
 
@@ -759,11 +837,11 @@
             me % 2 == 1, jnp.array(self.odd, jnp.int32), jnp.array(self.even, jnp.int32)
         )
 
-    def gather(self, own, *behind):
+    def gather(self, own, *behind, places=(0, 1, 2, 3)):
         if self.n == 8:
             blocks = [own, self.swap(own, 4, 2), self.swap(own, 2, 4), self.swap(own, 6)]
-            if behind:
-                blocks = [held(b, *behind) for b in blocks]
+            for i in places if behind else ():
+                blocks[i] = held(blocks[i], *behind)
             return blocks + [self.swap(b, 1) for b in blocks]
         blocks = own[None]
         step = 1
@@ -1015,10 +1093,10 @@
             in_part = lax.psum_scatter(
                 held(in_terms, *sc_behind), "wt", scatter_dimension=0, tiled=True
             )
-            total = ring.add(total, got)
+            total = ring.add(total, held(got, in_terms))
             while total.shape[0] > 2:
                 total = ring.step(total)
-            out = held(ring.outgoing(total), in_terms)
+            out = ring.outgoing(total)
             got = ring.move(total, out)[0]
             down_terms = dot_rows(held(act, out), g_all)[:units].astype(bf16)
             return (total[0], held(got, down_terms)), in_part, down_terms
@@ -1037,10 +1115,11 @@
         kv_got = ring.move(kv_total, kv_out)
         query_rel1 = query_back(cfg, held(part1, kv_out), both1)
         kv_sums = ring.finish(ring.add(kv_total, held(kv_got, query_rel1)))
+        kv_sums = (kv_sums[0], held(kv_sums[1], in_part1))
         grad1, grad1_low, kv_part1, attn_gain_grad1 = layer_back(
             cfg, kv_sums, query_rel1, hidden1, mgrad1, gain1, cos, sin, perm, both1
         )
-        grads0 = ring.gather(grad1_low)
+        grads0 = ring.gather(grad1_low, down_part1, places=(3,))
 
         def wide_row(row):
             return jnp.pad(row[:1], ((0, 0), (0, QKV_W - D)))
@@ -1108,14 +1187,13 @@
         )
         first_out0 = ring.outgoing(first0)
         first_got0 = ring.move(first0, first_out0)
-        down_in0 = held(down_terms0, in_part0)
+        down_part0 = lax.psum_scatter(down_terms0, "wt", scatter_dimension=0, tiled=True)
         z_out1 = (total1[0] + held(got1, kv_got).astype(f32)).astype(bf16)
         z_out1 = z_out1.reshape(m, pad_rows, z_out1.shape[-1])
         z_got1 = [ring.swap_z(z_out1[k], k) for k in range(1, m)]
         grad0, unused, kv_part0, attn_gain_grad0 = layer_back(
-            cfg, (kv_sums[0], held(kv_sums[1], first_out0, down_in0, z_out1)), query_rel0, hidden0, mgrad0, gain0, cos, sin, perm, both0
-        )
-        down_part0 = lax.psum_scatter(down_in0, "wt", scatter_dimension=0, tiled=True)
+            cfg, (kv_sums[0], held(kv_sums[1], first_out0, in_part0, z_out1)), query_rel0, hidden0, mgrad0, gain0, cos, sin, perm, both0
+        )
         hidden_out = middle1 + hidden_total[0] + held(hidden_got, grad0).astype(f32)
         first0 = ring.add(first0, first_got0)
         gain_rows = jnp.pad(attn_gain_grad0[:1], ((0, 127), (0, 0))).astype(bf16)
@@ -1135,8 +1213,8 @@
         total0 = jnp.concatenate([first0, last0], axis=2)
         while total0.shape[0] > 2:
             total0 = ring.step(total0)
-        last_got0 = ring.move(total0, ring.outgoing(total0))[0]
-        last_sum0 = (total0[0] + held(last_got0, down_part0).astype(f32)).astype(bf16)
+        last_got0 = ring.move(total0, held(ring.outgoing(total0), down_part0))[0]
+        last_sum0 = (total0[0] + last_got0.astype(f32)).astype(bf16)
         layer0 = ring.reduce_z(last_sum0.reshape(m, pad_rows, last_sum0.shape[-1]))
         layer1 = sum((held(g, layer0).astype(f32) for g in z_got1), z_out1[0].astype(f32))
         gain_at = QW + QKV_W

time: 512 us -> 506 us (0.988)
    ppermute x85, waiting for transfers between devices: 108 us -> 118 us  [swap(): lax.ppermute(value, 'ctx', [(i, i ^ (odd_offset if i % 2 else offset)) fo...]
    all_to_all x1, waiting for transfers between devices: 7.22 us -> 1.22 us  [feed_in_home(): return lax.all_to_all(cut, 'ctx', 0, 0, tiled=True)]
    dot_general x14, matrix products: 27.7 us -> 21.9 us  [dot_rows(): lax.dot_general(left, right, (((0,), (0,)), ((), ())), preferred_element_...]
    unnamed x261 -> x245, local copies, waits for them, and re-layouts: 20.9 us -> 19.1 us
  transfers between devices with their start and end apart: 106 -> 106, of which waited for: 48 -> 49; matrix products, arithmetic and copies ran while one was open for 18% -> 15% of each run, Pallas kernels for 18% -> 21%
where the time goes in v3:
time: 506 us; the launch traced here: 498 us
  waiting for transfers between devices  151 us (30%)
  Pallas kernels  133 us (26%)
  starting transfers between devices  81.1 us (16%)
  local copies, waits for them, and re-layouts  56.6 us (11%)
  other arithmetic  32.2 us (6%)
  matrix products  27.9 us (6%)
  between operations  16.3 us (3%)
    pallas_call x17, Pallas kernels, run(): pl.pallas_call(kernel, out_shape=outs, in_specs=in_specs, out_specs=out_s...  133 us
    ppermute x85, waiting for transfers between devices, swap(): lax.ppermute(value, 'ctx', [(i, i ^ (odd_offset if i % 2 else offset)) fo...  118 us
    ppermute x85, starting transfers between devices, swap(): lax.ppermute(value, 'ctx', [(i, i ^ (odd_offset if i % 2 else offset)) fo...  58.8 us
    ppermute x12, waiting for transfers between devices, swap_z(): return lax.ppermute(value, 'wt', [(i, i ^ offset) for i in range(self.m)])  25.7 us
    dot_general x14, matrix products, dot_rows(): lax.dot_general(left, right, (((0,), (0,)), ((), ())), preferred_element_...  21.9 us
    unnamed x245, local copies, waits for them, and re-layouts  19.1 us
    ppermute x12, starting transfers between devices, swap_z(): return lax.ppermute(value, 'wt', [(i, i ^ offset) for i in range(self.m)])  17.8 us
  transfers between devices with their start and end apart: 106, of which 49 were waited for; matrix products, arithmetic and copies ran while one was open for 15% of the time, Pallas kernels for 21%

profile of v3, /device:TPU:0, one launch (start us, length us, event | category | flops | bytes accessed | tf_op | source)
XLA Modules:
  0.0 498.4 jit_solution(13359787576500312621)
XLA Ops:
  13.7 5.4 %collective-permute-start.2 = (bf16[32,2048]{1,0:T(8,128)(2,1)S(1)}, bf16[32,2048]{1,0:T(8,128)(2,1)S(1)}, u32[]{:S(2)}, u32[]{:S(2)}) collective-permute-start(bf16[32,2048]{1,0:T(8,128)(2,1)S(1)} %pad_maximum_fusion.10), channel_id=1, source_target_pairs={{0,3},{1,2},{2,1},{3,0},{4,7},{5,6},{6,5},{7,4},{8,11},{9,10},{10,... | collective-permute-start | bytes 393224 | tf_op jit(solution)/shard_map/ppermute | solution.py:833
  23.5 6.6 %collective-permute-done.1 = bf16[32,2048]{1,0:T(8,128)(2,1)S(1)} collective-permute-done((bf16[32,2048]{1,0:T(8,128)(2,1)S(1)}, bf16[32,2048]{1,0:T(8,128)(2,1)S(1)}, u32[]{:S(2)}, u32[]{:S(2)}) %collective-permute-start.1) | collective-permute-done | bytes 131104 | tf_op jit(solution)/shard_map/ppermute | solution.py:833
  33.3 2.7 shard_map.214
  41.7 5.0 %collective-permute-done.24.refs_1_ = bf16[2,28,1280]{2,1,0:T(8,128)(2,1)S(1)} collective-permute-done((bf16[2,28,1280]{2,1,0:T(8,128)(2,1)}, bf16[2,28,1280]{2,1,0:T(8,128)(2,1)S(1)}, u32[]{:S(2)}, u32[]{:S(2)}) %collective-permute-start.24) | collective-permute-done | bytes 143392 | tf_op jit(solution)/shard_map/ppermute | solution.py:828
  46.7 4.4 collective-permute-done.30.refs_7_
  51.1 2.2 collective-permute-start.28
  55.6 2.6 collective-permute-done.28.refs_5_
  59.8 2.6 shard_map.217
  62.4 2.0 collective-permute-start.4
  66.6 10.7 %collective-permute-done.4.refs_6_.refs_23_.refs_8_.refs_2_.refs_10_ = bf16[2,128,2048]{2,1,0:T(8,128)(2,1)S(1)} collective-permute-done((bf16[2,128,2048]{2,1,0:T(8,128)(2,1)S(1)}, bf16[2,128,2048]{2,1,0:T(8,128)(2,1)S(1)}, u32[]{:S(2)}, u32[]{:S(2)}) %collective-permute-start.4) | collective-permute-done | bytes 1048608 | tf_op jit(solution)/shard_map/ppermute | solution.py:828
  78.3 2.0 fusion.1.refs_2_.refs_20_.refs_3_.refs_5_.refs_8_
  81.6 5.4 %shard_map.215 = (f32[160,896]{1,0:T(8,128)}, bf16[160,1024]{1,0:T(8,128)(2,1)}, bf16[160,896]{1,0:T(8,128)(2,1)}, bf16[160,384]{1,0:T(8,128)(2,1)}, f32[16,896]{1,0:T(8,128)}) custom-call(bf16[160,128]{1,0:T(8,128)(2,1)} %select_convert_fusion.2.refs_0_, bf16[160,896]{1,0:T(8,128)(2,1)} %bitcast.153, ...), custom_call_target="tpu_custom_call" | custom-call | flops 671088640 | bytes 7888896 | tf_op jit(solution)/shard_map/pallas_call | solution.py:125
  87.0 2.9 collective-permute-start.9
  90.7 3.4 collective-permute-done.9.refs_4_.refs_12_.refs_16_.refs_8_
  94.1 2.8 collective-permute-done.8.refs_3_.refs_11_.refs_15_.refs_7_
  101.8 11.8 %shard_map.216 = (f32[160,896]{1,0:T(8,128)}, bf16[160,896]{1,0:T(8,128)(2,1)}, bf16[160,1024]{1,0:T(8,128)(2,1)}, f32[128,1120]{1,0:T(8,128)}, f32[16,1120]{1,0:T(8,128)}, /*index=5*/bf16[128,1120]{1,0:T(8,128)(2,1)}) custom-call(bf16[160,896]{1,0:T(8,128)(2,1)} %get-tuple-element.138.refs_0_.refs_4_, ...), custom_call_target="tpu_custom_call" | custom-call | flops 1468006400 | bytes 12642688 | tf_op jit(solution)/shard_map/pallas_call | solution.py:125
  117.1 2.6 collective-permute-start.23
  119.7 5.8 %collective-permute-done.23 = bf16[32,2048]{1,0:T(8,128)(2,1)S(1)} collective-permute-done((bf16[32,2048]{1,0:T(8,128)(2,1)S(1)}, bf16[32,2048]{1,0:T(8,128)(2,1)S(1)}, u32[]{:S(2)}, u32[]{:S(2)}) %collective-permute-start.23) | collective-permute-done | bytes 131104 | tf_op jit(solution)/shard_map/ppermute | solution.py:833
  125.6 4.0 collective-permute-done.22
  132.7 10.7 %shard_map.218 = (bf16[640,896]{1,0:T(8,128)(2,1)}, bf16[640,896]{1,0:T(8,128)(2,1)}, bf16[1280,896]{1,0:T(8,128)(2,1)}, bf16[1280,1280]{1,0:T(8,128)(2,1)}, bf16[1280,640]{1,0:T(8,128)(2,1)}) custom-call(bf16[160,896]{1,0:T(8,128)(2,1)} %get-tuple-element.143.refs_0_, bf16[160,896]{1,0:T(8,128)(2,1)} %copy-done.96, bf16[160,896]{1,0:T(8,128)(2,1)} %copy-done.95, ...), custom_call_target="tpu_custom_call" | custom-call | flops 4404019200 | bytes 15179776 | tf_op jit(solution)/shard_map/pallas_call | solution.py:125
  145.3 7.7 %collective-permute-done.34 = bf16[1,128,2048]{2,1,0:T(8,128)(2,1)S(1)} collective-permute-done((bf16[1,128,2048]{2,1,0:T(8,128)(2,1)S(1)}, bf16[1,128,2048]{2,1,0:T(8,128)(2,1)S(1)}, u32[]{:S(2)}, u32[]{:S(2)}) %collective-permute-start.34) | collective-permute-done | bytes 524320 | tf_op jit(solution)/shard_map/ppermute | solution.py:828
  155.9 15.0 %collective-permute-done.32 = bf16[2,160,896]{2,1,0:T(8,128)(2,1)S(1)} collective-permute-done((bf16[2,160,896]{2,1,0:T(8,128)(2,1)S(1)}, bf16[2,160,896]{2,1,0:T(8,128)(2,1)S(1)}, u32[]{:S(2)}, u32[]{:S(2)}) %collective-permute-start.32) | collective-permute-done | bytes 573472 | tf_op jit(solution)/shard_map/ppermute | solution.py:828
  171.0 3.1 collective-permute-done.35.refs_7_.refs_23_.refs_8_.refs_2_.refs_10_
  175.9 4.9 collective-permute-done.33
  181.8 5.4 %shard_map.219 = (f32[160,896]{1,0:T(8,128)}, bf16[160,1024]{1,0:T(8,128)(2,1)}, bf16[160,896]{1,0:T(8,128)(2,1)}, bf16[160,256]{1,0:T(8,128)(2,1)}, f32[16,896]{1,0:T(8,128)}) custom-call(f32[160,896]{1,0:T(8,128)} %get-tuple-element.142.refs_0_.refs_2_, f32[160,896]{1,0:T(8,128)} %slice_bitcast_fusion.4.refs_1_, bf16[160,896]{1,0:T(8,128)(2,1)} %bitcast.162, ...), custom_call_target="tpu_custom_call" | custom-call | flops 671088640 | bytes 8953856 | tf_op jit(solution)/shard_map/pallas_call | solution.py:125
  190.8 2.6 collective-permute-done.40.refs_4_.refs_8_
  199.3 12.1 %shard_map.220 = (f32[160,896]{1,0:T(8,128)}, bf16[160,896]{1,0:T(8,128)(2,1)}, bf16[160,1024]{1,0:T(8,128)(2,1)}, f32[128,1120]{1,0:T(8,128)}, f32[16,1120]{1,0:T(8,128)}, /*index=5*/bf16[128,1120]{1,0:T(8,128)(2,1)}) custom-call(bf16[160,896]{1,0:T(8,128)(2,1)} %get-tuple-element.175.refs_0_.refs_4_, bf16[160,256]{1,0:T(8,128)(2,1)} %get-tuple-element.172.refs_1_.refs_5_, ...), custom_call_target="tpu_custom_call" | custom-call | flops 1468006400 | bytes 12315008 | tf_op jit(solution)/shard_map/pallas_call | solution.py:125
  216.3 6.8 %collective-permute-done.47.refs_3_ = bf16[160,896]{1,0:T(8,128)(2,1)S(1)} collective-permute-done((bf16[160,896]{1,0:T(8,128)(2,1)}, bf16[160,896]{1,0:T(8,128)(2,1)S(1)}, u32[]{:S(2)}, u32[]{:S(2)}) %collective-permute-start.47) | collective-permute-done | bytes 286752 | tf_op jit(solution)/shard_map/ppermute | solution.py:828
  223.2 5.1 %collective-permute-done.46.refs_2_ = bf16[160,896]{1,0:T(8,128)(2,1)S(1)} collective-permute-done((bf16[160,896]{1,0:T(8,128)(2,1)}, bf16[160,896]{1,0:T(8,128)(2,1)S(1)}, u32[]{:S(2)}, u32[]{:S(2)}) %collective-permute-start.46) | collective-permute-done | bytes 286752 | tf_op jit(solution)/shard_map/ppermute | solution.py:828
  230.6 15.9 %shard_map.221 = (bf16[640,896]{1,0:T(8,128)(2,1)}, bf16[640,896]{1,0:T(8,128)(2,1)}, bf16[1280,896]{1,0:T(8,128)(2,1)}, bf16[1280,1280]{1,0:T(8,128)(2,1)}, bf1...) custom-call(bf16[160,896]{1,0:T(8,128)(2,1)} %get-tuple-element.179.refs_0_, bf16[160,896]{1,0:T(8,128)(2,1)} %copy-done.98, ...), custom_call_target="tpu_custom_call" | custom-call | flops 7340032000 | bytes 19767296 | tf_op jit(solution)/shard_map/pallas_call | solution.py:125
  247.0 2.7 collective-permute-done.59
  252.7 4.7 convolution_convert_fusion.1
  259.1 8.5 %collective-permute-done.60 = bf16[2,160,896]{2,1,0:T(8,128)(2,1)S(1)} collective-permute-done((bf16[2,160,896]{2,1,0:T(8,128)(2,1)S(1)}, bf16[2,160,896]{2,1,0:T(8,128)(2,1)S(1)}, u32[]{:S(2)}, u32[]{:S(2)}) %collective-permute-start.60) | collective-permute-done | bytes 573472 | tf_op jit(solution)/shard_map/ppermute | solution.py:828
  268.9 1.9 fusion.74
  275.2 6.2 %shard_map.222 = (f32[160,896]{1,0:T(8,128)}, bf16[160,896]{1,0:T(8,128)(2,1)}, f32[8,896]{1,0:T(8,128)}, bf16[160,896]{1,0:T(8,128)(2,1)}) custom-call(f32[160,896]{1,0:T(8,128)} %slice_bitcast_fusion.3.refs_0_, bf16[160,896]{1,0:T(8,128)(2,1)} %bitcast.163, f32[160,896]{1,0:T(8,128)} %get-tuple-element.178.refs_2_, bf16[160,896]{1,0:T(8,128)(2,1)} %bitcast.157, ...), custom_call_target="tpu_custom_call" | custom-call | flops 1101004800 | bytes 10588160 | tf_op jit(solution)/shard_map/pallas_call | solution.py:125
  281.4 12.0 %shard_map.223 = (bf16[640,256]{1,0:T(8,128)(2,1)}, bf16[640,256]{1,0:T(8,128)(2,1)}, bf16[160,896]{1,0:T(8,128)(2,1)}) custom-call(bf16[160,896]{1,0:T(8,128)(2,1)} %get-tuple-element.195.refs_0_, f32[128,1120]{1,0:T(8,128)} %get-tuple-element.196.refs_1_, f32[16,1120]{1,0:T(8,128)} %get-tuple-element.197.refs_2_, ...), custom_call_target="tpu_custom_call" | custom-call | flops 3670016000 | bytes 4254080 | tf_op jit(solution)/shard_map/pallas_call | solution.py:125
  293.5 1.8 collective-permute-done.62
  298.5 3.3 shard_map.224.refs_2_
  303.7 2.8 collective-permute-done.64
  307.1 5.5 %shard_map.225 = (f32[160,896]{1,0:T(8,128)}, bf16[160,896]{1,0:T(8,128)(2,1)}, bf16[160,256]{1,0:T(8,128)(2,1)}, f32[8,896]{1,0:T(8,128)}) custom-call(f32[160,256]{1,0:T(8,128)} %slice_bitcast_fusion.8.refs_0_, bf16[160,256]{1,0:T(8,128)(2,1)} %bitcast.172, f32[160,1024]{1,0:T(8,128)} %shard_map.224.refs_2_, ...), custom_call_target="tpu_custom_call" | custom-call | flops 671088640 | bytes 9269248 | tf_op jit(solution)/shard_map/pallas_call | solution.py:125
  318.7 2.2 convolution_convert_fusion.2
  327.1 6.2 %reduce-scatter.13.cloned.1.call-done = bf16[152,896]{1,0:T(8,128)(2,1)} async-done(((bf16[608,896]{1,0:T(8,128)(2,1)}), bf16[152,896]{1,0:T(8,128)(2,1)}) %reduce-scatter.13.cloned.1.call-update) | async-done | bytes 272400
  333.9 3.0 convert_add_fusion.1
  340.0 12.3 %shard_map.226 = (bf16[640,896]{1,0:T(8,128)(2,1)}, bf16[640,896]{1,0:T(8,128)(2,1)}, bf16[1280,896]{1,0:T(8,128)(2,1)}, bf16[1280,1280]{1,0:T(8,128)(2,1)}) custom-call(bf16[1280,1280]{1,0:T(8,128)(2,1)} %get-tuple-element.210.refs_0_, bf16[160,896]{1,0:T(8,128)(2,1)} %get-tuple-element.211.refs_1_, bf16[160,896]{1,0:T(8,128)(2,1)} %collective-permute-done.67.refs_2_, ...), custom_call_target="tpu_custom_call" | custom-call | flops 4404019200 | bytes 16818176 | tf_op jit(solution)/shard_map/pallas_call | solution.py:125
  352.5 2.8 collective-permute-done.77
  359.0 4.7 convolution_convert_fusion
  365.0 8.4 %collective-permute-done.78 = bf16[2,160,896]{2,1,0:T(8,128)(2,1)S(1)} collective-permute-done((bf16[2,160,896]{2,1,0:T(8,128)(2,1)S(1)}, bf16[2,160,896]{2,1,0:T(8,128)(2,1)S(1)}, u32[]{:S(2)}, u32[]{:S(2)}) %collective-permute-start.78) | collective-permute-done | bytes 573472 | tf_op jit(solution)/shard_map/ppermute | solution.py:828
  376.2 1.9 fusion.75
  382.1 6.3 %shard_map.227 = (f32[160,896]{1,0:T(8,128)}, bf16[160,896]{1,0:T(8,128)(2,1)}, f32[8,896]{1,0:T(8,128)}, bf16[160,896]{1,0:T(8,128)(2,1)}) custom-call(f32[160,896]{1,0:T(8,128)} %slice_bitcast_fusion.2.refs_0_, bf16[160,896]{1,0:T(8,128)(2,1)} %bitcast.154, f32[160,896]{1,0:T(8,128)} %get-tuple-element.142.refs_0_.refs_2_, ...), custom_call_target="tpu_custom_call" | custom-call | flops 1101004800 | bytes 10874880 | tf_op jit(solution)/shard_map/pallas_call | solution.py:125
  393.1 12.0 %shard_map.228 = (bf16[640,256]{1,0:T(8,128)(2,1)}, bf16[640,256]{1,0:T(8,128)(2,1)}, bf16[160,896]{1,0:T(8,128)(2,1)}) custom-call(bf16[160,896]{1,0:T(8,128)(2,1)} %get-tuple-element.232.refs_0_, f32[128,1120]{1,0:T(8,128)} %get-tuple-element.233.refs_1_, f32[16,1120]{1,0:T(8,128)} %get-tuple-element.234.refs_2_, ...), custom_call_target="tpu_custom_call" | custom-call | flops 3670016000 | bytes 4581760 | tf_op jit(solution)/shard_map/pallas_call | solution.py:125
  411.1 3.4 shard_map.229.refs_2_
  419.6 2.7 collective-permute-done.84
  428.4 5.5 %shard_map.230 = (f32[160,896]{1,0:T(8,128)}, bf16[160,896]{1,0:T(8,128)(2,1)}, bf16[160,256]{1,0:T(8,128)(2,1)}, f32[8,896]{1,0:T(8,128)}) custom-call(f32[160,256]{1,0:T(8,128)} %slice_bitcast_fusion.7.refs_0_, bf16[160,256]{1,0:T(8,128)(2,1)} %bitcast.171, f32[160,1024]{1,0:T(8,128)} %shard_map.229.refs_2_, ...), custom_call_target="tpu_custom_call" | custom-call | flops 671088640 | bytes 9269248 | tf_op jit(solution)/shard_map/pallas_call | solution.py:125
  441.3 2.8 fusion.14
  449.5 1.8 fusion.66
  451.8 2.6 collective-permute-start.96
  454.5 2.1 maximum_convert_fusion
  460.3 2.6 collective-permute-start.93
  463.6 2.2 copy.102
  465.8 3.8 all-to-all-start
  469.6 2.4 collective-permute-start.95
  472.0 2.2 collective-permute-done.92
  474.4 5.2 %collective-permute-done.95 = bf16[32,2048]{1,0:T(8,128)(2,1)S(1)} collective-permute-done((bf16[32,2048]{1,0:T(8,128)(2,1)S(1)}, bf16[32,2048]{1,0:T(8,128)(2,1)S(1)}, u32[]{:S(2)}, u32[]{:S(2)}) %collective-permute-start.95) | collective-permute-done | bytes 131104 | tf_op jit(solution)/shard_map/ppermute | solution.py:833
  487.8 3.6 reshape.342
  (585 shorter events, 155.7 us)
Async XLA Ops:
  7.2 55.2 %all-gather.5.cloned.1.call-start = ((), (), s32[]{:S(2)}) async-start(), calls=%async_computation.5 | async-start | bytes 1361920 | tf_op jit(solution)/shard_map/all_gather | solution.py:1019
  13.7 9.8 %collective-permute-start.2 = (bf16[32,2048]{1,0:T(8,128)(2,1)S(1)}, bf16[32,2048]{1,0:T(8,128)(2,1)S(1)}, u32[]{:S(2)}, u32[]{:S(2)}) collective-permute-start(bf16[32,2048]{1,0:T(8,128)(2,1)S(1)} %pad_maximum_fusion.10), channel_id=1, source_target_pairs={{0,3},{1,2},{2,1},{3,0},{4,7},{5,6},{6,5},{7,4},{8,11},{9,10},{10,... | collective-permute-start | bytes 393224 | tf_op jit(solution)/shard_map/ppermute | solution.py:833
  19.1 11.1 %collective-permute-start.1 = (bf16[32,2048]{1,0:T(8,128)(2,1)S(1)}, bf16[32,2048]{1,0:T(8,128)(2,1)S(1)}, u32[]{:S(2)}, u32[]{:S(2)}) collective-permute-start(bf16[32,2048]{1,0:T(8,128)(2,1)S(1)} %pad_maximum_fusion.10), channel_id=1, source_target_pairs={{0,2},{1,3},{2,0},{3,1},{4,6},{5,7},{6,4},{7,5},{8,10},{9,11},{10,... | collective-permute-start | bytes 393224 | tf_op jit(solution)/shard_map/ppermute | solution.py:833
  19.1 11.1 %collective-permute-start = (bf16[32,2048]{1,0:T(8,128)(2,1)S(1)}, bf16[32,2048]{1,0:T(8,128)(2,1)S(1)}, u32[]{:S(2)}, u32[]{:S(2)}) collective-permute-start(bf16[32,2048]{1,0:T(8,128)(2,1)S(1)} %pad_maximum_fusion.10), channel_id=1, source_target_pairs={{0,1},{1,0},{2,3},{3,2},{4,5},{5,4},{6,7},{7,6},{8,9},{9,8},{10,11... | collective-permute-start | bytes 393224 | tf_op jit(solution)/shard_map/ppermute | solution.py:833
  31.5 100.5 %all-gather.7.cloned.1.call-start = ((), (), s32[]{:S(2)}) async-start(), calls=%async_computation.6 | async-start | bytes 2867200 | tf_op jit(solution)/shard_map/all_gather | solution.py:1027
  36.1 17.2 %collective-permute-start.3 = (bf16[1,128,2048]{2,1,0:T(8,128)(2,1)S(1)}, bf16[1,128,2048]{2,1,0:T(8,128)(2,1)S(1)}, u32[]{:S(2)}, u32[]{:S(2)}) collective-permute-start(bf16[1,128,2048]{2,1,0:T(8,128)(2,1)S(1)} %bitcast.141), channel_id=1, source_target_pairs={{0,8},{4,20},{8,0},{12,28},{16,24},{20,4},{24,16},{28,12},{1,9},{5... | collective-permute-start | bytes 1572872 | tf_op jit(solution)/shard_map/ppermute | solution.py:828
  37.7 9.0 %collective-permute-start.24 = (bf16[2,28,1280]{2,1,0:T(8,128)(2,1)}, bf16[2,28,1280]{2,1,0:T(8,128)(2,1)S(1)}, u32[]{:S(2)}, u32[]{:S(2)}) collective-permute-start(bf16[2,28,1280]{2,1,0:T(8,128)(2,1)} %get-tuple-element.148), channel_id=1, source_target_pairs={{0,16},{4,12},{8,24},{12,4},{16,0},{20,28},{24,8},{28,20},{1,17},{... | collective-permute-start | bytes 430088 | tf_op jit(solution)/shard_map/ppermute | solution.py:828
  39.1 12.0 %collective-permute-start.30 = (bf16[2,28,1280]{2,1,0:T(8,128)(2,1)}, bf16[2,28,1280]{2,1,0:T(8,128)(2,1)S(1)}, u32[]{:S(2)}, u32[]{:S(2)}) collective-permute-start(bf16[2,28,1280]{2,1,0:T(8,128)(2,1)} %get-tuple-element.160), channel_id=1, source_target_pairs={{0,28},{4,24},{8,20},{12,16},{16,12},{20,8},{24,4},{28,0},{1,29},{... | collective-permute-start | bytes 430088 | tf_op jit(solution)/shard_map/ppermute | solution.py:828
  39.7 14.1 %collective-permute-start.25 = (bf16[2,28,1280]{2,1,0:T(8,128)(2,1)}, bf16[2,28,1280]{2,1,0:T(8,128)(2,1)S(1)}, u32[]{:S(2)}, u32[]{:S(2)}) collective-permute-start(bf16[2,28,1280]{2,1,0:T(8,128)(2,1)} %get-tuple-element.150), channel_id=1, source_target_pairs={{0,8},{4,20},{8,0},{12,28},{16,24},{20,4},{24,16},{28,12},{1,9},{5... | collective-permute-start | bytes 430088 | tf_op jit(solution)/shard_map/ppermute | solution.py:828
  40.2 15.3 %collective-permute-start.26 = (bf16[2,28,1280]{2,1,0:T(8,128)(2,1)}, bf16[2,28,1280]{2,1,0:T(8,128)(2,1)S(1)}, u32[]{:S(2)}, u32[]{:S(2)}) collective-permute-start(bf16[2,28,1280]{2,1,0:T(8,128)(2,1)} %get-tuple-element.152), channel_id=1, source_target_pairs={{0,24},{4,28},{8,16},{12,20},{16,8},{20,12},{24,0},{28,4},{1,25},{... | collective-permute-start | bytes 430088 | tf_op jit(solution)/shard_map/ppermute | solution.py:828
  46.7 8.9 %collective-permute-start.27 = (bf16[2,28,1280]{2,1,0:T(8,128)(2,1)}, bf16[2,28,1280]{2,1,0:T(8,128)(2,1)S(1)}, u32[]{:S(2)}, u32[]{:S(2)}) collective-permute-start(bf16[2,28,1280]{2,1,0:T(8,128)(2,1)} %get-tuple-element.154), channel_id=1, source_target_pairs={{0,4},{4,0},{8,12},{12,8},{16,20},{20,16},{24,28},{28,24},{1,5},{5... | collective-permute-start | bytes 430088 | tf_op jit(solution)/shard_map/ppermute | solution.py:828
  51.1 7.0 %collective-permute-start.28 = (bf16[2,28,1280]{2,1,0:T(8,128)(2,1)}, bf16[2,28,1280]{2,1,0:T(8,128)(2,1)S(1)}, u32[]{:S(2)}, u32[]{:S(2)}) collective-permute-start(bf16[2,28,1280]{2,1,0:T(8,128)(2,1)} %get-tuple-element.156), channel_id=1, source_target_pairs={{0,12},{4,16},{8,4},{12,24},{16,28},{20,0},{24,20},{28,8},{1,13},{... | collective-permute-start | bytes 430088 | tf_op jit(solution)/shard_map/ppermute | solution.py:828
  62.4 133.3 %all-gather.9.cloned.1.call-start = ((), (), s32[]{:S(2)}) async-start(), calls=%async_computation.7 | async-start | bytes 2867200 | tf_op jit(solution)/shard_map/all_gather | solution.py:1068
  62.4 14.9 %collective-permute-start.4 = (bf16[2,128,2048]{2,1,0:T(8,128)(2,1)S(1)}, bf16[2,128,2048]{2,1,0:T(8,128)(2,1)S(1)}, u32[]{:S(2)}, u32[]{:S(2)}) collective-permute-start(bf16[2,128,2048]{2,1,0:T(8,128)(2,1)S(1)} %pad_maximum_fusion.4.refs_5_.refs_22_.refs_7_.refs_1_.refs_9_), channel_id=1, source_target_pairs={{0,16},{4,12},{8,24},{12,4},{16,0},{20,28},{24,8},{28,20},{1,17},{... | collective-permute-start | bytes 3145736 | tf_op jit(solution)/shard_map/ppermute | solution.py:828
  66.4 13.9 %collective-permute-start.5 = (bf16[2,128,2048]{2,1,0:T(8,128)(2,1)S(1)}, bf16[2,128,2048]{2,1,0:T(8,128)(2,1)S(1)}, u32[]{:S(2)}, u32[]{:S(2)}) collective-permute-start(bf16[2,128,2048]{2,1,0:T(8,128)(2,1)S(1)} %pad_maximum_fusion.4.refs_5_.refs_22_.refs_7_.refs_1_.refs_9_), channel_id=1, source_target_pairs={{0,4},{4,0},{8,12},{12,8},{16,20},{20,16},{24,28},{28,24},{1,5},{5... | collective-permute-start | bytes 3145736 | tf_op jit(solution)/shard_map/ppermute | solution.py:828
  87.0 7.0 %collective-permute-start.9 = (bf16[160,384]{1,0:T(8,128)(2,1)}, bf16[160,384]{1,0:T(8,128)(2,1)S(1)}, u32[]{:S(2)}, u32[]{:S(2)}) collective-permute-start(bf16[160,384]{1,0:T(8,128)(2,1)} %get-tuple-element.139.refs_1_.refs_9_.refs_13_.refs_5_), channel_id=1, source_target_pairs={{0,24},{4,28},{8,16},{12,20},{16,8},{20,12},{24,0},{28,4},{1,25},{... | collective-permute-start | bytes 368648 | tf_op jit(solution)/shard_map/ppermute | solution.py:828
  90.6 10.4 %collective-permute-start.10 = (bf16[160,384]{1,0:T(8,128)(2,1)}, bf16[160,384]{1,0:T(8,128)(2,1)S(1)}, u32[]{:S(2)}, u32[]{:S(2)}) collective-permute-start(bf16[160,384]{1,0:T(8,128)(2,1)} %get-tuple-element.139.refs_1_.refs_9_.refs_13_.refs_5_), channel_id=1, source_target_pairs={{0,4},{4,0},{8,12},{12,8},{16,20},{20,16},{24,28},{28,24},{1,5},{5... | collective-permute-start | bytes 368648 | tf_op jit(solution)/shard_map/ppermute | solution.py:828
  113.6 12.0 %collective-permute-start.16 = (bf16[160,896]{1,0:T(8,128)(2,1)}, bf16[160,896]{1,0:T(8,128)(2,1)S(1)}, u32[]{:S(2)}, u32[]{:S(2)}) collective-permute-start(bf16[160,896]{1,0:T(8,128)(2,1)} %get-tuple-element.143.refs_0_), channel_id=1, source_target_pairs={{0,24},{4,28},{8,16},{12,20},{16,8},{20,12},{24,0},{28,4},{1,25},{... | collective-permute-start | bytes 860168 | tf_op jit(solution)/shard_map/ppermute | solution.py:828
  115.3 14.7 %collective-permute-start.15 = (bf16[160,896]{1,0:T(8,128)(2,1)}, bf16[160,896]{1,0:T(8,128)(2,1)S(1)}, u32[]{:S(2)}, u32[]{:S(2)}) collective-permute-start(bf16[160,896]{1,0:T(8,128)(2,1)} %get-tuple-element.143.refs_0_), channel_id=1, source_target_pairs={{0,8},{4,20},{8,0},{12,28},{16,24},{20,4},{24,16},{28,12},{1,9},{5... | collective-permute-start | bytes 860168 | tf_op jit(solution)/shard_map/ppermute | solution.py:828
  116.5 13.6 %collective-permute-start.14 = (bf16[160,896]{1,0:T(8,128)(2,1)}, bf16[160,896]{1,0:T(8,128)(2,1)S(1)}, u32[]{:S(2)}, u32[]{:S(2)}) collective-permute-start(bf16[160,896]{1,0:T(8,128)(2,1)} %get-tuple-element.143.refs_0_), channel_id=1, source_target_pairs={{0,16},{4,12},{8,24},{12,4},{16,0},{20,28},{24,8},{28,20},{1,17},{... | collective-permute-start | bytes 860168 | tf_op jit(solution)/shard_map/ppermute | solution.py:828
  117.1 8.4 %collective-permute-start.23 = (bf16[32,2048]{1,0:T(8,128)(2,1)S(1)}, bf16[32,2048]{1,0:T(8,128)(2,1)S(1)}, u32[]{:S(2)}, u32[]{:S(2)}) collective-permute-start(bf16[32,2048]{1,0:T(8,128)(2,1)S(1)} %fusion.42), channel_id=1, source_target_pairs={{0,3},{1,2},{2,1},{3,0},{4,7},{5,6},{6,5},{7,4},{8,11},{9,10},{10,... | collective-permute-start | bytes 393224 | tf_op jit(solution)/shard_map/ppermute | solution.py:833
  119.7 9.9 %collective-permute-start.22 = (bf16[32,2048]{1,0:T(8,128)(2,1)S(1)}, bf16[32,2048]{1,0:T(8,128)(2,1)S(1)}, u32[]{:S(2)}, u32[]{:S(2)}) collective-permute-start(bf16[32,2048]{1,0:T(8,128)(2,1)S(1)} %fusion.42), channel_id=1, source_target_pairs={{0,2},{1,3},{2,0},{3,1},{4,6},{5,7},{6,4},{7,5},{8,10},{9,11},{10,... | collective-permute-start | bytes 393224 | tf_op jit(solution)/shard_map/ppermute | solution.py:833
  143.5 11.1 %collective-permute-start.31 = (bf16[640,896]{1,0:T(8,128)(2,1)}, bf16[640,896]{1,0:T(8,128)(2,1)S(1)}, u32[]{:S(2)}, u32[]{:S(2)}) collective-permute-start(bf16[640,896]{1,0:T(8,128)(2,1)} %get-tuple-element.166), channel_id=1, source_target_pairs={{0,4},{4,0},{8,12},{12,8},{16,20},{20,16},{24,28},{28,24},{1,5},{5... | collective-permute-start | bytes 3440648 | tf_op jit(solution)/shard_map/ppermute | solution.py:828
  143.7 86.8 %all-gather.11.cloned.1.call-start = ((), (), s32[]{:S(2)}) async-start(), calls=%async_computation.8 | async-start | bytes 1361920 | tf_op jit(solution)/shard_map/all_gather | solution.py:1081
  143.8 9.2 %collective-permute-start.34 = (bf16[1,128,2048]{2,1,0:T(8,128)(2,1)S(1)}, bf16[1,128,2048]{2,1,0:T(8,128)(2,1)S(1)}, u32[]{:S(2)}, u32[]{:S(2)}) collective-permute-start(bf16[1,128,2048]{2,1,0:T(8,128)(2,1)S(1)} %maximum_bitcast_fusion), channel_id=1, source_target_pairs={{0,8},{4,20},{8,0},{12,28},{16,24},{20,4},{24,16},{28,12},{1,9},{5... | collective-permute-start | bytes 1572872 | tf_op jit(solution)/shard_map/ppermute | solution.py:828
  153.1 21.0 %collective-permute-start.35 = (bf16[2,128,2048]{2,1,0:T(8,128)(2,1)S(1)}, bf16[2,128,2048]{2,1,0:T(8,128)(2,1)S(1)}, u32[]{:S(2)}, u32[]{:S(2)}) collective-permute-start(bf16[2,128,2048]{2,1,0:T(8,128)(2,1)S(1)} %pad_maximum_fusion.5.refs_6_.refs_22_.refs_7_.refs_1_.refs_9_), channel_id=1, source_target_pairs={{0,16},{4,12},{8,24},{12,4},{16,0},{20,28},{24,8},{28,20},{1,17},{... | collective-permute-start | bytes 3145736 | tf_op jit(solution)/shard_map/ppermute | solution.py:828
  154.9 16.0 %collective-permute-start.32 = (bf16[2,160,896]{2,1,0:T(8,128)(2,1)S(1)}, bf16[2,160,896]{2,1,0:T(8,128)(2,1)S(1)}, u32[]{:S(2)}, u32[]{:S(2)}) collective-permute-start(bf16[2,160,896]{2,1,0:T(8,128)(2,1)S(1)} %bitcast.149), channel_id=1, source_target_pairs={{0,8},{4,20},{8,0},{12,28},{16,24},{20,4},{24,16},{28,12},{1,9},{5... | collective-permute-start | bytes 1720328 | tf_op jit(solution)/shard_map/ppermute | solution.py:828
  155.8 20.1 %collective-permute-start.36 = (bf16[2,128,2048]{2,1,0:T(8,128)(2,1)S(1)}, bf16[2,128,2048]{2,1,0:T(8,128)(2,1)S(1)}, u32[]{:S(2)}, u32[]{:S(2)}) collective-permute-start(bf16[2,128,2048]{2,1,0:T(8,128)(2,1)S(1)} %pad_maximum_fusion.5.refs_6_.refs_22_.refs_7_.refs_1_.refs_9_), channel_id=1, source_target_pairs={{0,4},{4,0},{8,12},{12,8},{16,20},{20,16},{24,28},{28,24},{1,5},{5... | collective-permute-start | bytes 3145736 | tf_op jit(solution)/shard_map/ppermute | solution.py:828
  195.7 110.8 %reduce-scatter.9.cloned.1.call-start = ((), (), s32[]{:S(2)}) async-start(), calls=%async_computation.9 | async-start | bytes 2867200 | tf_op jit(solution)/shard_map/reduce_scatter | solution.py:1093
  195.7 18.0 %collective-permute-start.54 = (bf16[160,896]{1,0:T(8,128)(2,1)S(1)}, bf16[160,896]{1,0:T(8,128)(2,1)S(1)}, u32[]{:S(2)}, u32[]{:S(2)}) collective-permute-start(bf16[160,896]{1,0:T(8,128)(2,1)S(1)} %bitcast.158), channel_id=1, source_target_pairs={{0,24},{4,28},{8,16},{12,20},{16,8},{20,12},{24,0},{28,4},{1,25},{... | collective-permute-start | bytes 860168 | tf_op jit(solution)/shard_map/ppermute | solution.py:828
  197.3 14.2 %collective-permute-start.53 = (bf16[160,896]{1,0:T(8,128)(2,1)S(1)}, bf16[160,896]{1,0:T(8,128)(2,1)S(1)}, u32[]{:S(2)}, u32[]{:S(2)}) collective-permute-start(bf16[160,896]{1,0:T(8,128)(2,1)S(1)} %bitcast.159), channel_id=1, source_target_pairs={{0,8},{4,20},{8,0},{12,28},{16,24},{20,4},{24,16},{28,12},{1,9},{5... | collective-permute-start | bytes 860168 | tf_op jit(solution)/shard_map/ppermute | solution.py:828
  198.4 13.4 %collective-permute-start.52 = (bf16[160,896]{1,0:T(8,128)(2,1)S(1)}, bf16[160,896]{1,0:T(8,128)(2,1)S(1)}, u32[]{:S(2)}, u32[]{:S(2)}) collective-permute-start(bf16[160,896]{1,0:T(8,128)(2,1)S(1)} %bitcast.160), channel_id=1, source_target_pairs={{0,16},{4,12},{8,24},{12,4},{16,0},{20,28},{24,8},{28,20},{1,17},{... | collective-permute-start | bytes 860168 | tf_op jit(solution)/shard_map/ppermute | solution.py:828
  212.3 10.8 %collective-permute-start.47 = (bf16[160,896]{1,0:T(8,128)(2,1)}, bf16[160,896]{1,0:T(8,128)(2,1)S(1)}, u32[]{:S(2)}, u32[]{:S(2)}) collective-permute-start(bf16[160,896]{1,0:T(8,128)(2,1)} %get-tuple-element.179.refs_0_), channel_id=1, source_target_pairs={{0,24},{4,28},{8,16},{12,20},{16,8},{20,12},{24,0},{28,4},{1,25},{... | collective-permute-start | bytes 860168 | tf_op jit(solution)/shard_map/ppermute | solution.py:828
  213.7 14.5 %collective-permute-start.46 = (bf16[160,896]{1,0:T(8,128)(2,1)}, bf16[160,896]{1,0:T(8,128)(2,1)S(1)}, u32[]{:S(2)}, u32[]{:S(2)}) collective-permute-start(bf16[160,896]{1,0:T(8,128)(2,1)} %get-tuple-element.179.refs_0_), channel_id=1, source_target_pairs={{0,8},{4,20},{8,0},{12,28},{16,24},{20,4},{24,16},{28,12},{1,9},{5... | collective-permute-start | bytes 860168 | tf_op jit(solution)/shard_map/ppermute | solution.py:828
  214.9 13.7 %collective-permute-start.45 = (bf16[160,896]{1,0:T(8,128)(2,1)}, bf16[160,896]{1,0:T(8,128)(2,1)S(1)}, u32[]{:S(2)}, u32[]{:S(2)}) collective-permute-start(bf16[160,896]{1,0:T(8,128)(2,1)} %get-tuple-element.179.refs_0_), channel_id=1, source_target_pairs={{0,16},{4,12},{8,24},{12,4},{16,0},{20,28},{24,8},{28,20},{1,17},{... | collective-permute-start | bytes 860168 | tf_op jit(solution)/shard_map/ppermute | solution.py:828
  215.8 12.9 %collective-permute-start.48 = (bf16[160,896]{1,0:T(8,128)(2,1)}, bf16[160,896]{1,0:T(8,128)(2,1)S(1)}, u32[]{:S(2)}, u32[]{:S(2)}) collective-permute-start(bf16[160,896]{1,0:T(8,128)(2,1)} %get-tuple-element.179.refs_0_), channel_id=1, source_target_pairs={{0,4},{4,0},{8,12},{12,8},{16,20},{20,16},{24,28},{28,24},{1,5},{5... | collective-permute-start | bytes 860168 | tf_op jit(solution)/shard_map/ppermute | solution.py:828
  215.9 12.9 %collective-permute-start.58 = (bf16[160,896]{1,0:T(8,128)(2,1)S(1)}, bf16[160,896]{1,0:T(8,128)(2,1)S(1)}, u32[]{:S(2)}, u32[]{:S(2)}) collective-permute-start(bf16[160,896]{1,0:T(8,128)(2,1)S(1)} %collective-permute-done.54.refs_11_), channel_id=1, source_target_pairs={{0,4},{4,0},{8,12},{12,8},{16,20},{20,16},{24,28},{28,24},{1,5},{5... | collective-permute-start | bytes 860168 | tf_op jit(solution)/shard_map/ppermute | solution.py:828
  257.4 75.9 %reduce-scatter.13.cloned.1.call-start = ((), (), s32[]{:S(2)}) async-start(), calls=%async_computation.11 | async-start | bytes 1361920
  257.9 9.8 %collective-permute-start.60 = (bf16[2,160,896]{2,1,0:T(8,128)(2,1)S(1)}, bf16[2,160,896]{2,1,0:T(8,128)(2,1)S(1)}, u32[]{:S(2)}, u32[]{:S(2)}) collective-permute-start(bf16[2,160,896]{2,1,0:T(8,128)(2,1)S(1)} %bitcast.148), channel_id=1, source_target_pairs={{0,8},{4,20},{8,0},{12,28},{16,24},{20,4},{24,16},{28,12},{1,9},{5... | collective-permute-start | bytes 1720328 | tf_op jit(solution)/shard_map/ppermute | solution.py:828
  297.6 130.7 %reduce-scatter.11.cloned.1.call-start = ((), (), s32[]{:S(2)}) async-start(), calls=%async_computation.10 | async-start | bytes 2867200 | tf_op jit(solution)/shard_map/reduce_scatter | solution.py:1093
  313.2 8.3 %collective-permute-start.74 = (bf16[512,896]{1,0:T(8,128)(2,1)S(1)}, bf16[512,896]{1,0:T(8,128)(2,1)S(1)}, u32[]{:S(2)}, u32[]{:S(2)}) collective-permute-start(bf16[512,896]{1,0:T(8,128)(2,1)S(1)} %convolution_convert_fusion.6), channel_id=1, source_target_pairs={{0,4},{4,0},{8,12},{12,8},{16,20},{20,16},{24,28},{28,24},{1,5},{5... | collective-permute-start | bytes 2752520 | tf_op jit(solution)/shard_map/ppermute | solution.py:828
  315.7 7.0 %collective-permute-start.75 = (bf16[512,1152]{1,0:T(8,128)(2,1)S(1)}, bf16[512,1152]{1,0:T(8,128)(2,1)S(1)}, u32[]{:S(2)}, u32[]{:S(2)}) collective-permute-start(bf16[512,1152]{1,0:T(8,128)(2,1)S(1)} %fusion.5), channel_id=1, source_target_pairs={{0,4},{4,0},{8,12},{12,8},{16,20},{20,16},{24,28},{28,24},{1,5},{5... | collective-permute-start | bytes 3538952 | tf_op jit(solution)/shard_map/ppermute | solution.py:828
  316.3 10.8 %collective-permute-start.69 = (bf16[160,896]{1,0:T(8,128)(2,1)}, bf16[160,896]{1,0:T(8,128)(2,1)S(1)}, u32[]{:S(2)}, u32[]{:S(2)}) collective-permute-start(bf16[160,896]{1,0:T(8,128)(2,1)} %get-tuple-element.211.refs_1_), channel_id=1, source_target_pairs={{0,24},{4,28},{8,16},{12,20},{16,8},{20,12},{24,0},{28,4},{1,25},{... | collective-permute-start | bytes 860168 | tf_op jit(solution)/shard_map/ppermute | solution.py:828
  317.7 15.7 %collective-permute-start.68 = (bf16[160,896]{1,0:T(8,128)(2,1)}, bf16[160,896]{1,0:T(8,128)(2,1)}, u32[]{:S(2)}, u32[]{:S(2)}) collective-permute-start(bf16[160,896]{1,0:T(8,128)(2,1)} %get-tuple-element.211.refs_1_), channel_id=1, source_target_pairs={{0,8},{4,20},{8,0},{12,28},{16,24},{20,4},{24,16},{28,12},{1,9},{5... | collective-permute-start | bytes 860168 | tf_op jit(solution)/shard_map/ppermute | solution.py:828
  321.0 12.9 %collective-permute-start.65 = (bf16[640,896]{1,0:T(8,128)(2,1)}, bf16[640,896]{1,0:T(8,128)(2,1)}, u32[]{:S(2)}, u32[]{:S(2)}) collective-permute-start(bf16[640,896]{1,0:T(8,128)(2,1)} %convolution_convert_fusion.2), channel_id=1, source_target_pairs={{0,4},{4,0},{8,12},{12,8},{16,20},{20,16},{24,28},{28,24},{1,5},{5... | collective-permute-start | bytes 3440648 | tf_op jit(solution)/shard_map/ppermute | solution.py:828
  321.5 11.9 %collective-permute-start.67 = (bf16[160,896]{1,0:T(8,128)(2,1)}, bf16[160,896]{1,0:T(8,128)(2,1)}, u32[]{:S(2)}, u32[]{:S(2)}) collective-permute-start(bf16[160,896]{1,0:T(8,128)(2,1)} %get-tuple-element.211.refs_1_), channel_id=1, source_target_pairs={{0,16},{4,12},{8,24},{12,4},{16,0},{20,28},{24,8},{28,20},{1,17},{... | collective-permute-start | bytes 860168 | tf_op jit(solution)/shard_map/ppermute | solution.py:828
  325.3 26.9 %collective-permute-start.76 = (bf16[2,128,2048]{2,1,0:T(8,128)(2,1)}, bf16[2,128,2048]{2,1,0:T(8,128)(2,1)S(1)}, u32[]{:S(2)}, u32[]{:S(2)}) collective-permute-start(bf16[2,128,2048]{2,1,0:T(8,128)(2,1)} %fusion.10), channel_id=1, source_target_pairs={{0,8},{4,20},{8,0},{12,28},{16,24},{20,4},{24,16},{28,12},{1,9},{5... | collective-permute-start | bytes 3145736 | tf_op jit(solution)/shard_map/ppermute | solution.py:828
  327.1 12.8 %collective-permute-start.70 = (bf16[160,896]{1,0:T(8,128)(2,1)}, bf16[160,896]{1,0:T(8,128)(2,1)}, u32[]{:S(2)}, u32[]{:S(2)}) collective-permute-start(bf16[160,896]{1,0:T(8,128)(2,1)} %get-tuple-element.211.refs_1_), channel_id=1, source_target_pairs={{0,4},{4,0},{8,12},{12,8},{16,20},{20,16},{24,28},{28,24},{1,5},{5... | collective-permute-start | bytes 860168 | tf_op jit(solution)/shard_map/ppermute | solution.py:828
  338.4 13.8 %collective-permute-start.66 = (bf16[2,160,896]{2,1,0:T(8,128)(2,1)S(1)}, bf16[2,160,896]{2,1,0:T(8,128)(2,1)S(1)}, u32[]{:S(2)}, u32[]{:S(2)}) collective-permute-start(bf16[2,160,896]{2,1,0:T(8,128)(2,1)S(1)} %bitcast.146), channel_id=1, source_target_pairs={{0,8},{4,20},{8,0},{12,28},{16,24},{20,4},{24,16},{28,12},{1,9},{5... | collective-permute-start | bytes 1720328 | tf_op jit(solution)/shard_map/ppermute | solution.py:828
  363.7 84.8 %reduce-scatter.15.cloned.1.call-start = ((), (), s32[]{:S(2)}) async-start(), calls=%async_computation.12 | async-start | bytes 1361920
  363.7 9.8 %collective-permute-start.78 = (bf16[2,160,896]{2,1,0:T(8,128)(2,1)S(1)}, bf16[2,160,896]{2,1,0:T(8,128)(2,1)S(1)}, u32[]{:S(2)}, u32[]{:S(2)}) collective-permute-start(bf16[2,160,896]{2,1,0:T(8,128)(2,1)S(1)} %bitcast.147), channel_id=1, source_target_pairs={{0,8},{4,20},{8,0},{12,28},{16,24},{20,4},{24,16},{28,12},{1,9},{5... | collective-permute-start | bytes 1720328 | tf_op jit(solution)/shard_map/ppermute | solution.py:828
  390.2 14.9 %collective-permute-start.81 = (bf16[1,128,2048]{2,1,0:T(8,128)(2,1)S(1)}, bf16[1,128,2048]{2,1,0:T(8,128)(2,1)S(1)}, u32[]{:S(2)}, u32[]{:S(2)}) collective-permute-start(bf16[1,128,2048]{2,1,0:T(8,128)(2,1)S(1)} %slice.584), channel_id=1, source_target_pairs={{0,16},{4,12},{8,24},{12,4},{16,0},{20,28},{24,8},{28,20},{1,17},{... | collective-permute-start | bytes 1572872 | tf_op jit(solution)/shard_map/ppermute | solution.py:828
  391.9 13.2 %collective-permute-start.80 = (bf16[1,160,896]{2,1,0:T(8,128)(2,1)S(1)}, bf16[1,160,896]{2,1,0:T(8,128)(2,1)S(1)}, u32[]{:S(2)}, u32[]{:S(2)}) collective-permute-start(bf16[1,160,896]{2,1,0:T(8,128)(2,1)S(1)} %slice.585), channel_id=1, source_target_pairs={{0,16},{4,12},{8,24},{12,4},{16,0},{20,28},{24,8},{28,20},{1,17},{... | collective-permute-start | bytes 860168 | tf_op jit(solution)/shard_map/ppermute | solution.py:828
  411.0 11.4 %collective-permute-start.85 = (bf16[512,896]{1,0:T(8,128)(2,1)}, bf16[512,896]{1,0:T(8,128)(2,1)}, u32[]{:S(2)}, u32[]{:S(2)}) collective-permute-start(bf16[512,896]{1,0:T(8,128)(2,1)} %select_convert_fusion.1), channel_id=1, source_target_pairs={{0,4},{4,0},{8,12},{12,8},{16,20},{20,16},{24,28},{28,24},{1,5},{5... | collective-permute-start | bytes 2752520 | tf_op jit(solution)/shard_map/ppermute | solution.py:828
  415.9 7.9 %collective-permute-start.86 = (bf16[512,896]{1,0:T(8,128)(2,1)}, bf16[512,896]{1,0:T(8,128)(2,1)}, u32[]{:S(2)}, u32[]{:S(2)}) collective-permute-start(bf16[512,896]{1,0:T(8,128)(2,1)} %convolution_convert_fusion.5), channel_id=1, source_target_pairs={{0,4},{4,0},{8,12},{12,8},{16,20},{20,16},{24,28},{28,24},{1,5},{5... | collective-permute-start | bytes 2752520 | tf_op jit(solution)/shard_map/ppermute | solution.py:828
  427.1 14.2 %collective-permute-start.87 = (bf16[2,128,1792]{2,1,0:T(8,128)(2,1)}, bf16[2,128,1792]{2,1,0:T(8,128)(2,1)}, u32[]{:S(2)}, u32[]{:S(2)}) collective-permute-start(bf16[2,128,1792]{2,1,0:T(8,128)(2,1)} %fusion.13), channel_id=1, source_target_pairs={{0,8},{4,20},{8,0},{12,28},{16,24},{20,4},{24,16},{28,12},{1,9},{5... | collective-permute-start | bytes 2752520 | tf_op jit(solution)/shard_map/ppermute | solution.py:828
  448.5 10.1 %collective-permute-start.90 = (bf16[1,128,2176]{2,1,0:T(8,128)(2,1)}, bf16[1,128,2176]{2,1,0:T(8,128)(2,1)}, u32[]{:S(2)}, u32[]{:S(2)}) collective-permute-start(bf16[1,128,2176]{2,1,0:T(8,128)(2,1)} %fusion.20), channel_id=1, source_target_pairs={{0,16},{4,12},{8,24},{12,4},{16,0},{20,28},{24,8},{28,20},{1,17},{... | collective-permute-start | bytes 1671176 | tf_op jit(solution)/shard_map/ppermute | solution.py:828
  451.3 28.3 %collective-permute-start.94 = (bf16[32,2048]{1,0:T(8,128)(2,1)}, bf16[32,2048]{1,0:T(8,128)(2,1)}, u32[]{:S(2)}, u32[]{:S(2)}) collective-permute-start(bf16[32,2048]{1,0:T(8,128)(2,1)} %get-tuple-element.308), channel_id=1, source_target_pairs={{0,1},{1,0},{2,3},{3,2},{4,5},{5,4},{6,7},{7,6},{8,9},{9,8},{10,11... | collective-permute-start | bytes 393224 | tf_op jit(solution)/shard_map/ppermute | solution.py:833
  451.8 22.5 %collective-permute-start.96 = (bf16[32,2048]{1,0:T(8,128)(2,1)}, bf16[32,2048]{1,0:T(8,128)(2,1)}, u32[]{:S(2)}, u32[]{:S(2)}) collective-permute-start(bf16[32,2048]{1,0:T(8,128)(2,1)} %get-tuple-element.309), channel_id=1, source_target_pairs={{0,3},{1,2},{2,1},{3,0},{4,7},{5,6},{6,5},{7,4},{8,11},{9,10},{10,... | collective-permute-start | bytes 393224 | tf_op jit(solution)/shard_map/ppermute | solution.py:833
  459.9 9.7 %collective-permute-start.91 = (bf16[32,2176]{1,0:T(8,128)(2,1)S(1)}, bf16[32,2176]{1,0:T(8,128)(2,1)S(1)}, u32[]{:S(2)}, u32[]{:S(2)}) collective-permute-start(bf16[32,2176]{1,0:T(8,128)(2,1)S(1)} %get-tuple-element.303), channel_id=1, source_target_pairs={{0,1},{1,0},{2,3},{3,2},{4,5},{5,4},{6,7},{7,6},{8,9},{9,8},{10,11... | collective-permute-start | bytes 417800 | tf_op jit(solution)/shard_map/ppermute | solution.py:833
  460.3 11.8 %collective-permute-start.93 = (bf16[32,2176]{1,0:T(8,128)(2,1)S(1)}, bf16[32,2176]{1,0:T(8,128)(2,1)S(1)}, u32[]{:S(2)}, u32[]{:S(2)}) collective-permute-start(bf16[32,2176]{1,0:T(8,128)(2,1)S(1)} %get-tuple-element.304), channel_id=1, source_target_pairs={{0,3},{1,2},{2,1},{3,0},{4,7},{5,6},{6,5},{7,4},{8,11},{9,10},{10,... | collective-permute-start | bytes 417800 | tf_op jit(solution)/shard_map/ppermute | solution.py:833
  462.9 11.4 %collective-permute-start.92 = (bf16[32,2176]{1,0:T(8,128)(2,1)S(1)}, bf16[32,2176]{1,0:T(8,128)(2,1)S(1)}, u32[]{:S(2)}, u32[]{:S(2)}) collective-permute-start(bf16[32,2176]{1,0:T(8,128)(2,1)S(1)} %get-tuple-element.305), channel_id=1, source_target_pairs={{0,2},{1,3},{2,0},{3,1},{4,6},{5,7},{6,4},{7,5},{8,10},{9,11},{10,... | collective-permute-start | bytes 417800 | tf_op jit(solution)/shard_map/ppermute | solution.py:833
  465.8 20.2 %all-to-all-start = ((bf16[8,2,28,1280]{3,1,2,0:T(2,128)(2,1)}), bf16[8,2,28,1280]{3,1,2,0:T(2,128)(2,1)S(1)}, u32[]{:S(2)}, u32[]{:S(2)}) async-start(bf16[8,2,28,1280]{3,1,2,0:T(2,128)(2,1)} %copy.102), calls=%async_computation.2 | async-start | bytes 2293760 | tf_op jit(solution)/shard_map/all_to_all | solution.py:962
  469.6 10.0 %collective-permute-start.95 = (bf16[32,2048]{1,0:T(8,128)(2,1)S(1)}, bf16[32,2048]{1,0:T(8,128)(2,1)S(1)}, u32[]{:S(2)}, u32[]{:S(2)}) collective-permute-start(bf16[32,2048]{1,0:T(8,128)(2,1)S(1)} %copy-done.60), channel_id=1, source_target_pairs={{0,2},{1,3},{2,0},{3,1},{4,6},{5,7},{6,4},{7,5},{8,10},{9,11},{10,... | collective-permute-start | bytes 393224 | tf_op jit(solution)/shard_map/ppermute | solution.py:833
  (165 other events, 832.4 us)
Sparse Core Ops, SparseCore 0:
  31.6 28.7 all-gather.4
  62.5 49.7 all-gather.6
  143.8 48.3 all-gather.8
  195.8 27.4 all-gather.10
  257.5 45.8 reduce-scatter.8
  306.3 26.9 reduce-scatter.12
  363.8 45.6 reduce-scatter.10
  417.5 26.1 reduce-scatter.14

commit v4 on v3

--- a/solution.py
+++ b/solution.py
@@ -1178,24 +1178,22 @@
         kv_got = ring.move(kv_total, kv_out)[0]
         query_keep0, query_send0 = row_terms(rel0, held(part0, kv_out))
         kv_sums = (kv_total[0], held(kv_got, query_send0))
-        first0 = jnp.concatenate(
-            [
-                ring.first(out_keep0, out_send0),
-                held(ring.first(query_keep0, query_send0), *kv_sums),
-            ],
-            axis=2,
-        )
-        first_out0 = ring.outgoing(first0)
-        first_got0 = ring.move(first0, first_out0)
         down_part0 = lax.psum_scatter(down_terms0, "wt", scatter_dimension=0, tiled=True)
         z_out1 = (total1[0] + held(got1, kv_got).astype(f32)).astype(bf16)
         z_out1 = z_out1.reshape(m, pad_rows, z_out1.shape[-1])
         z_got1 = [ring.swap_z(z_out1[k], k) for k in range(1, m)]
         grad0, unused, kv_part0, attn_gain_grad0 = layer_back(
-            cfg, (kv_sums[0], held(kv_sums[1], first_out0, in_part0, z_out1)), query_rel0, hidden0, mgrad0, gain0, cos, sin, perm, both0
+            cfg, (kv_sums[0], held(kv_sums[1], in_part0, z_out1)), query_rel0, hidden0, mgrad0, gain0, cos, sin, perm, both0
         )
         hidden_out = middle1 + hidden_total[0] + held(hidden_got, grad0).astype(f32)
-        first0 = ring.add(first0, first_got0)
+        first0 = jnp.concatenate(
+            [
+                ring.first(held(out_keep0, grad0), out_send0),
+                ring.first(held(query_keep0, grad0), query_send0),
+            ],
+            axis=2,
+        )
+        first0 = ring.step(first0)
         gain_rows = jnp.pad(attn_gain_grad0[:1], ((0, 127), (0, 0))).astype(bf16)
         columns = lax.dot_general(
             perm, gain_rows, (((0,), (1,)), ((), ())), preferred_element_type=f32

time: 506 us -> 516 us (1.020)
  waiting for transfers between devices: 151 us -> 162 us
    all_to_all x1, waiting for transfers between devices: 1.22 us -> 11 us  [feed_in_home(): return lax.all_to_all(cut, 'ctx', 0, 0, tiled=True)]
    unnamed x245 -> x267, local copies, waits for them, and re-layouts: 19.1 us -> 21.9 us
  transfers between devices with their start and end apart: 106 -> 106, of which waited for: 49 -> 46; matrix products, arithmetic and copies ran while one was open for 15% -> 14% of each run, Pallas kernels for 21% -> 21%
where the time goes in v4:
time: 516 us; the launch traced here: 508 us
  waiting for transfers between devices  162 us (31%)
  Pallas kernels  133 us (26%)
  starting transfers between devices  80.6 us (16%)
  local copies, waits for them, and re-layouts  58.2 us (11%)
  other arithmetic  32.1 us (6%)
  matrix products  25.8 us (5%)
  between operations  16.4 us (3%)
    pallas_call x17, Pallas kernels, run(): pl.pallas_call(kernel, out_shape=outs, in_specs=in_specs, out_specs=out_s...  133 us
    ppermute x85, waiting for transfers between devices, swap(): lax.ppermute(value, 'ctx', [(i, i ^ (odd_offset if i % 2 else offset)) fo...  122 us
    ppermute x85, starting transfers between devices, swap(): lax.ppermute(value, 'ctx', [(i, i ^ (odd_offset if i % 2 else offset)) fo...  58.8 us
    ppermute x12, waiting for transfers between devices, swap_z(): return lax.ppermute(value, 'wt', [(i, i ^ offset) for i in range(self.m)])  22.6 us
    unnamed x267, local copies, waits for them, and re-layouts  21.9 us
    dot_general x14, matrix products, dot_rows(): lax.dot_general(left, right, (((0,), (0,)), ((), ())), preferred_element_...  19.8 us
    ppermute x12, starting transfers between devices, swap_z(): return lax.ppermute(value, 'wt', [(i, i ^ offset) for i in range(self.m)])  17.2 us
    all_to_all x1, waiting for transfers between devices, feed_in_home(): return lax.all_to_all(cut, 'ctx', 0, 0, tiled=True)  11 us
  transfers between devices with their start and end apart: 106, of which 46 were waited for; matrix products, arithmetic and copies ran while one was open for 14% of the time, Pallas kernels for 21%

profile of v4, /device:TPU:0, one launch (start us, length us, event | category | flops | bytes accessed | tf_op | source)
XLA Modules:
  0.0 508.1 jit_solution(8243258426541170177)
XLA Ops:
  11.0 1.8 fusion.70
  14.7 5.4 %collective-permute-start.2 = (bf16[32,2048]{1,0:T(8,128)(2,1)S(1)}, bf16[32,2048]{1,0:T(8,128)(2,1)S(1)}, u32[]{:S(2)}, u32[]{:S(2)}) collective-permute-start(bf16[32,2048]{1,0:T(8,128)(2,1)S(1)} %pad_maximum_fusion.10), channel_id=1, source_target_pairs={{0,3},{1,2},{2,1},{3,0},{4,7},{5,6},{6,5},{7,4},{8,11},{9,10},{10,... | collective-permute-start | bytes 393224 | tf_op jit(solution)/shard_map/ppermute | solution.py:833
  24.5 6.6 %collective-permute-done.1 = bf16[32,2048]{1,0:T(8,128)(2,1)S(1)} collective-permute-done((bf16[32,2048]{1,0:T(8,128)(2,1)S(1)}, bf16[32,2048]{1,0:T(8,128)(2,1)S(1)}, u32[]{:S(2)}, u32[]{:S(2)}) %collective-permute-start.1) | collective-permute-done | bytes 131104 | tf_op jit(solution)/shard_map/ppermute | solution.py:833
  34.3 2.7 shard_map.214
  42.7 5.0 collective-permute-done.24.refs_1_
  47.7 4.4 collective-permute-done.30.refs_7_
  52.2 2.2 collective-permute-start.28
  56.6 2.6 collective-permute-done.28.refs_5_
  60.8 2.5 shard_map.217
  63.4 2.0 collective-permute-start.4
  67.6 10.7 %collective-permute-done.4.refs_6_.refs_23_.refs_8_.refs_2_.refs_10_ = bf16[2,128,2048]{2,1,0:T(8,128)(2,1)S(1)} collective-permute-done((bf16[2,128,2048]{2,1,0:T(8,128)(2,1)S(1)}, bf16[2,128,2048]{2,1,0:T(8,128)(2,1)S(1)}, u32[]{:S(2)}, u32[]{:S(2)}) %collective-permute-start.4) | collective-permute-done | bytes 1048608 | tf_op jit(solution)/shard_map/ppermute | solution.py:828
  79.3 2.0 fusion.1.refs_2_.refs_20_.refs_3_.refs_5_.refs_8_
  82.6 5.4 %shard_map.215 = (f32[160,896]{1,0:T(8,128)}, bf16[160,1024]{1,0:T(8,128)(2,1)}, bf16[160,896]{1,0:T(8,128)(2,1)}, bf16[160,384]{1,0:T(8,128)(2,1)}, f32[16,896]{1,0:T(8,128)}) custom-call(bf16[160,128]{1,0:T(8,128)(2,1)} %select_convert_fusion.2.refs_0_, bf16[160,896]{1,0:T(8,128)(2,1)} %bitcast.153, ...), custom_call_target="tpu_custom_call" | custom-call | flops 671088640 | bytes 7888896 | tf_op jit(solution)/shard_map/pallas_call | solution.py:125
  88.0 2.9 collective-permute-start.9
  91.7 3.4 collective-permute-done.9.refs_4_.refs_12_.refs_16_.refs_8_
  95.1 2.8 collective-permute-done.8.refs_3_.refs_11_.refs_15_.refs_7_
  102.8 11.8 %shard_map.216 = (f32[160,896]{1,0:T(8,128)}, bf16[160,896]{1,0:T(8,128)(2,1)}, bf16[160,1024]{1,0:T(8,128)(2,1)}, f32[128,1120]{1,0:T(8,128)}, f32[16,1120]{1,0:T(8,128)}, /*index=5*/bf16[128,1120]{1,0:T(8,128)(2,1)}) custom-call(bf16[160,896]{1,0:T(8,128)(2,1)} %get-tuple-element.139.refs_0_.refs_4_, ...), custom_call_target="tpu_custom_call" | custom-call | flops 1468006400 | bytes 12642688 | tf_op jit(solution)/shard_map/pallas_call | solution.py:125
  118.2 2.6 collective-permute-start.23
  120.8 5.8 %collective-permute-done.23 = bf16[32,2048]{1,0:T(8,128)(2,1)S(1)} collective-permute-done((bf16[32,2048]{1,0:T(8,128)(2,1)S(1)}, bf16[32,2048]{1,0:T(8,128)(2,1)S(1)}, u32[]{:S(2)}, u32[]{:S(2)}) %collective-permute-start.23) | collective-permute-done | bytes 131104 | tf_op jit(solution)/shard_map/ppermute | solution.py:833
  126.7 4.0 collective-permute-done.22
  133.8 10.8 %shard_map.218 = (bf16[640,896]{1,0:T(8,128)(2,1)}, bf16[640,896]{1,0:T(8,128)(2,1)}, bf16[1280,896]{1,0:T(8,128)(2,1)}, bf16[1280,1280]{1,0:T(8,128)(2,1)}, bf16[1280,640]{1,0:T(8,128)(2,1)}) custom-call(bf16[160,896]{1,0:T(8,128)(2,1)} %get-tuple-element.144.refs_0_, bf16[160,896]{1,0:T(8,128)(2,1)} %copy-done.107, bf16[160,896]{1,0:T(8,128)(2,1)} %copy-done.106, ...), custom_call_target="tpu_custom_call" | custom-call | flops 4404019200 | bytes 15179776 | tf_op jit(solution)/shard_map/pallas_call | solution.py:125
  146.4 7.7 %collective-permute-done.34 = bf16[1,128,2048]{2,1,0:T(8,128)(2,1)S(1)} collective-permute-done((bf16[1,128,2048]{2,1,0:T(8,128)(2,1)S(1)}, bf16[1,128,2048]{2,1,0:T(8,128)(2,1)S(1)}, u32[]{:S(2)}, u32[]{:S(2)}) %collective-permute-start.34) | collective-permute-done | bytes 524320 | tf_op jit(solution)/shard_map/ppermute | solution.py:828
  157.0 15.0 %collective-permute-done.32 = bf16[2,160,896]{2,1,0:T(8,128)(2,1)S(1)} collective-permute-done((bf16[2,160,896]{2,1,0:T(8,128)(2,1)S(1)}, bf16[2,160,896]{2,1,0:T(8,128)(2,1)S(1)}, u32[]{:S(2)}, u32[]{:S(2)}) %collective-permute-start.32) | collective-permute-done | bytes 573472 | tf_op jit(solution)/shard_map/ppermute | solution.py:828
  172.2 3.1 collective-permute-done.35.refs_7_.refs_23_.refs_8_.refs_2_.refs_10_
  177.0 4.9 collective-permute-done.33
  183.0 5.4 %shard_map.219 = (f32[160,896]{1,0:T(8,128)}, bf16[160,1024]{1,0:T(8,128)(2,1)}, bf16[160,896]{1,0:T(8,128)(2,1)}, bf16[160,256]{1,0:T(8,128)(2,1)}, f32[16,896]{1,0:T(8,128)}) custom-call(f32[160,896]{1,0:T(8,128)} %get-tuple-element.143.refs_0_.refs_2_, f32[160,896]{1,0:T(8,128)} %slice_bitcast_fusion.4.refs_1_, bf16[160,896]{1,0:T(8,128)(2,1)} %bitcast.162, ...), custom_call_target="tpu_custom_call" | custom-call | flops 671088640 | bytes 8953856 | tf_op jit(solution)/shard_map/pallas_call | solution.py:125
  192.0 2.6 collective-permute-done.40.refs_4_.refs_8_
  200.5 12.1 %shard_map.220 = (f32[160,896]{1,0:T(8,128)}, bf16[160,896]{1,0:T(8,128)(2,1)}, bf16[160,1024]{1,0:T(8,128)(2,1)}, f32[128,1120]{1,0:T(8,128)}, f32[16,1120]{1,0:T(8,128)}, /*index=5*/bf16[128,1120]{1,0:T(8,128)(2,1)}) custom-call(bf16[160,896]{1,0:T(8,128)(2,1)} %get-tuple-element.176.refs_0_.refs_4_, bf16[160,256]{1,0:T(8,128)(2,1)} %get-tuple-element.173.refs_1_.refs_5_, ...), custom_call_target="tpu_custom_call" | custom-call | flops 1468006400 | bytes 12315008 | tf_op jit(solution)/shard_map/pallas_call | solution.py:125
  217.5 6.8 %collective-permute-done.47.refs_3_ = bf16[160,896]{1,0:T(8,128)(2,1)S(1)} collective-permute-done((bf16[160,896]{1,0:T(8,128)(2,1)}, bf16[160,896]{1,0:T(8,128)(2,1)S(1)}, u32[]{:S(2)}, u32[]{:S(2)}) %collective-permute-start.47) | collective-permute-done | bytes 286752 | tf_op jit(solution)/shard_map/ppermute | solution.py:828
  224.3 5.1 %collective-permute-done.46.refs_2_ = bf16[160,896]{1,0:T(8,128)(2,1)S(1)} collective-permute-done((bf16[160,896]{1,0:T(8,128)(2,1)}, bf16[160,896]{1,0:T(8,128)(2,1)S(1)}, u32[]{:S(2)}, u32[]{:S(2)}) %collective-permute-start.46) | collective-permute-done | bytes 286752 | tf_op jit(solution)/shard_map/ppermute | solution.py:828
  231.8 15.9 %shard_map.221 = (bf16[640,896]{1,0:T(8,128)(2,1)}, bf16[640,896]{1,0:T(8,128)(2,1)}, bf16[1280,896]{1,0:T(8,128)(2,1)}, bf16[1280,1280]{1,0:T(8,128)(2,1)}, bf1...) custom-call(bf16[160,896]{1,0:T(8,128)(2,1)} %get-tuple-element.180.refs_0_, bf16[160,896]{1,0:T(8,128)(2,1)} %copy-done.109, ...), custom_call_target="tpu_custom_call" | custom-call | flops 7340032000 | bytes 19767296 | tf_op jit(solution)/shard_map/pallas_call | solution.py:125
  248.2 2.7 collective-permute-done.59
  253.8 4.7 convolution_convert_fusion.1
  260.3 8.5 %collective-permute-done.60 = bf16[2,160,896]{2,1,0:T(8,128)(2,1)S(1)} collective-permute-done((bf16[2,160,896]{2,1,0:T(8,128)(2,1)S(1)}, bf16[2,160,896]{2,1,0:T(8,128)(2,1)S(1)}, u32[]{:S(2)}, u32[]{:S(2)}) %collective-permute-start.60) | collective-permute-done | bytes 573472 | tf_op jit(solution)/shard_map/ppermute | solution.py:828
  270.1 1.9 fusion.74
  276.4 6.2 %shard_map.222 = (f32[160,896]{1,0:T(8,128)}, bf16[160,896]{1,0:T(8,128)(2,1)}, f32[8,896]{1,0:T(8,128)}, bf16[160,896]{1,0:T(8,128)(2,1)}) custom-call(f32[160,896]{1,0:T(8,128)} %slice_bitcast_fusion.3.refs_0_, bf16[160,896]{1,0:T(8,128)(2,1)} %bitcast.163, f32[160,896]{1,0:T(8,128)} %get-tuple-element.179.refs_2_, bf16[160,896]{1,0:T(8,128)(2,1)} %bitcast.157, ...), custom_call_target="tpu_custom_call" | custom-call | flops 1101004800 | bytes 10588160 | tf_op jit(solution)/shard_map/pallas_call | solution.py:125
  282.6 12.0 %shard_map.223 = (bf16[640,256]{1,0:T(8,128)(2,1)}, bf16[640,256]{1,0:T(8,128)(2,1)}, bf16[160,896]{1,0:T(8,128)(2,1)}) custom-call(bf16[160,896]{1,0:T(8,128)(2,1)} %get-tuple-element.196.refs_0_, f32[128,1120]{1,0:T(8,128)} %get-tuple-element.197.refs_1_, f32[16,1120]{1,0:T(8,128)} %get-tuple-element.198.refs_2_, ...), custom_call_target="tpu_custom_call" | custom-call | flops 3670016000 | bytes 4254080 | tf_op jit(solution)/shard_map/pallas_call | solution.py:125
  294.7 1.8 collective-permute-done.62
  299.8 3.3 shard_map.224.refs_2_
  304.9 2.8 collective-permute-done.64
  308.3 5.5 %shard_map.225 = (f32[160,896]{1,0:T(8,128)}, bf16[160,896]{1,0:T(8,128)(2,1)}, bf16[160,256]{1,0:T(8,128)(2,1)}, f32[8,896]{1,0:T(8,128)}) custom-call(f32[160,256]{1,0:T(8,128)} %slice_bitcast_fusion.8.refs_0_, bf16[160,256]{1,0:T(8,128)(2,1)} %bitcast.172, f32[160,1024]{1,0:T(8,128)} %shard_map.224.refs_2_, ...), custom_call_target="tpu_custom_call" | custom-call | flops 671088640 | bytes 9269248 | tf_op jit(solution)/shard_map/pallas_call | solution.py:125
  319.9 2.2 convolution_convert_fusion.2
  328.3 6.2 %reduce-scatter.13.cloned.1.call-done = bf16[152,896]{1,0:T(8,128)(2,1)} async-done(((bf16[608,896]{1,0:T(8,128)(2,1)}), bf16[152,896]{1,0:T(8,128)(2,1)}) %reduce-scatter.13.cloned.1.call-update) | async-done | bytes 272400
  335.1 3.0 convert_add_fusion.1
  341.1 12.3 %shard_map.226 = (bf16[640,896]{1,0:T(8,128)(2,1)}, bf16[640,896]{1,0:T(8,128)(2,1)}, bf16[1280,896]{1,0:T(8,128)(2,1)}, bf16[1280,1280]{1,0:T(8,128)(2,1)}) custom-call(bf16[1280,1280]{1,0:T(8,128)(2,1)} %get-tuple-element.211.refs_0_, bf16[160,896]{1,0:T(8,128)(2,1)} %get-tuple-element.212.refs_1_, bf16[160,896]{1,0:T(8,128)(2,1)} %collective-permute-done.67.refs_2_, ...), custom_call_target="tpu_custom_call" | custom-call | flops 4404019200 | bytes 16818176 | tf_op jit(solution)/shard_map/pallas_call | solution.py:125
  353.7 2.8 collective-permute-done.77
  360.1 4.7 convolution_convert_fusion
  366.2 8.5 %collective-permute-done.78 = bf16[2,160,896]{2,1,0:T(8,128)(2,1)S(1)} collective-permute-done((bf16[2,160,896]{2,1,0:T(8,128)(2,1)S(1)}, bf16[2,160,896]{2,1,0:T(8,128)(2,1)S(1)}, u32[]{:S(2)}, u32[]{:S(2)}) %collective-permute-start.78) | collective-permute-done | bytes 573472 | tf_op jit(solution)/shard_map/ppermute | solution.py:828
  377.4 1.9 fusion.75
  383.3 6.3 %shard_map.227 = (f32[160,896]{1,0:T(8,128)}, bf16[160,896]{1,0:T(8,128)(2,1)}, f32[8,896]{1,0:T(8,128)}, bf16[160,896]{1,0:T(8,128)(2,1)}) custom-call(f32[160,896]{1,0:T(8,128)} %slice_bitcast_fusion.2.refs_0_, bf16[160,896]{1,0:T(8,128)(2,1)} %bitcast.154, f32[160,896]{1,0:T(8,128)} %get-tuple-element.143.refs_0_.refs_2_, ...), custom_call_target="tpu_custom_call" | custom-call | flops 1101004800 | bytes 10874880 | tf_op jit(solution)/shard_map/pallas_call | solution.py:125
  395.2 12.0 %shard_map.228 = (bf16[640,256]{1,0:T(8,128)(2,1)}, bf16[640,256]{1,0:T(8,128)(2,1)}, bf16[160,896]{1,0:T(8,128)(2,1)}) custom-call(bf16[160,896]{1,0:T(8,128)(2,1)} %get-tuple-element.233.refs_0_, f32[128,1120]{1,0:T(8,128)} %get-tuple-element.234.refs_1_, f32[16,1120]{1,0:T(8,128)} %get-tuple-element.235.refs_2_, ...), custom_call_target="tpu_custom_call" | custom-call | flops 3670016000 | bytes 4581760 | tf_op jit(solution)/shard_map/pallas_call | solution.py:125
  412.7 3.3 shard_map.229.refs_2_
  422.7 5.4 %shard_map.230 = (f32[160,896]{1,0:T(8,128)}, bf16[160,896]{1,0:T(8,128)(2,1)}, bf16[160,256]{1,0:T(8,128)(2,1)}, f32[8,896]{1,0:T(8,128)}) custom-call(f32[160,256]{1,0:T(8,128)} %slice_bitcast_fusion.7.refs_0_, bf16[160,256]{1,0:T(8,128)(2,1)} %bitcast.171, f32[160,1024]{1,0:T(8,128)} %shard_map.229.refs_2_, ...), custom_call_target="tpu_custom_call" | custom-call | flops 671088640 | bytes 9269248 | tf_op jit(solution)/shard_map/pallas_call | solution.py:125
  439.1 2.7 collective-permute-start.96
  442.0 8.2 %collective-permute-done.89 = bf16[2,128,384]{2,1,0:T(8,128)(2,1)S(1)} collective-permute-done((bf16[2,128,384]{2,1,0:T(8,128)(2,1)}, bf16[2,128,384]{2,1,0:T(8,128)(2,1)S(1)}, u32[]{:S(2)}, u32[]{:S(2)}) %collective-permute-start.89) | collective-permute-done | bytes 196640 | tf_op jit(solution)/shard_map/ppermute | solution.py:828
  456.6 2.0 maximum_convert_fusion
  458.7 1.9 fusion.27
  460.8 2.2 copy.102
  463.0 3.8 all-to-all-start
  469.3 2.7 collective-permute-start.93
  472.2 11.0 %all-to-all-done = bf16[8,2,28,1280]{3,1,2,0:T(2,128)(2,1)S(1)} async-done(((bf16[8,2,28,1280]{3,1,2,0:T(2,128)(2,1)}), bf16[8,2,28,1280]{3,1,2,0:T(2,128)(2,1)S(1)}, u32[]{:S(2)}, u32[]{:S(2)}) %all-to-all-start) | async-done | bytes 1146912 | tf_op jit(solution)/shard_map/all_to_all | solution.py:962
  485.1 3.6 reshape.342
  488.6 1.8 collective-permute-start.95
  491.5 4.4 collective-permute-done.95
  (607 shorter events, 153.7 us)
Async XLA Ops:
  7.2 56.2 %all-gather.5.cloned.1.call-start = ((), (), s32[]{:S(2)}) async-start(), calls=%async_computation.5 | async-start | bytes 1361920 | tf_op jit(solution)/shard_map/all_gather | solution.py:1019
  14.7 9.8 %collective-permute-start.2 = (bf16[32,2048]{1,0:T(8,128)(2,1)S(1)}, bf16[32,2048]{1,0:T(8,128)(2,1)S(1)}, u32[]{:S(2)}, u32[]{:S(2)}) collective-permute-start(bf16[32,2048]{1,0:T(8,128)(2,1)S(1)} %pad_maximum_fusion.10), channel_id=1, source_target_pairs={{0,3},{1,2},{2,1},{3,0},{4,7},{5,6},{6,5},{7,4},{8,11},{9,10},{10,... | collective-permute-start | bytes 393224 | tf_op jit(solution)/shard_map/ppermute | solution.py:833
  20.1 11.1 %collective-permute-start.1 = (bf16[32,2048]{1,0:T(8,128)(2,1)S(1)}, bf16[32,2048]{1,0:T(8,128)(2,1)S(1)}, u32[]{:S(2)}, u32[]{:S(2)}) collective-permute-start(bf16[32,2048]{1,0:T(8,128)(2,1)S(1)} %pad_maximum_fusion.10), channel_id=1, source_target_pairs={{0,2},{1,3},{2,0},{3,1},{4,6},{5,7},{6,4},{7,5},{8,10},{9,11},{10,... | collective-permute-start | bytes 393224 | tf_op jit(solution)/shard_map/ppermute | solution.py:833
  20.1 11.1 %collective-permute-start = (bf16[32,2048]{1,0:T(8,128)(2,1)S(1)}, bf16[32,2048]{1,0:T(8,128)(2,1)S(1)}, u32[]{:S(2)}, u32[]{:S(2)}) collective-permute-start(bf16[32,2048]{1,0:T(8,128)(2,1)S(1)} %pad_maximum_fusion.10), channel_id=1, source_target_pairs={{0,1},{1,0},{2,3},{3,2},{4,5},{5,4},{6,7},{7,6},{8,9},{9,8},{10,11... | collective-permute-start | bytes 393224 | tf_op jit(solution)/shard_map/ppermute | solution.py:833
  32.5 100.6 %all-gather.7.cloned.1.call-start = ((), (), s32[]{:S(2)}) async-start(), calls=%async_computation.6 | async-start | bytes 2867200 | tf_op jit(solution)/shard_map/all_gather | solution.py:1027
  37.1 17.2 %collective-permute-start.3 = (bf16[1,128,2048]{2,1,0:T(8,128)(2,1)S(1)}, bf16[1,128,2048]{2,1,0:T(8,128)(2,1)S(1)}, u32[]{:S(2)}, u32[]{:S(2)}) collective-permute-start(bf16[1,128,2048]{2,1,0:T(8,128)(2,1)S(1)} %bitcast.141), channel_id=1, source_target_pairs={{0,8},{4,20},{8,0},{12,28},{16,24},{20,4},{24,16},{28,12},{1,9},{5... | collective-permute-start | bytes 1572872 | tf_op jit(solution)/shard_map/ppermute | solution.py:828
  38.7 9.0 %collective-permute-start.24 = (bf16[2,28,1280]{2,1,0:T(8,128)(2,1)}, bf16[2,28,1280]{2,1,0:T(8,128)(2,1)S(1)}, u32[]{:S(2)}, u32[]{:S(2)}) collective-permute-start(bf16[2,28,1280]{2,1,0:T(8,128)(2,1)} %get-tuple-element.149), channel_id=1, source_target_pairs={{0,16},{4,12},{8,24},{12,4},{16,0},{20,28},{24,8},{28,20},{1,17},{... | collective-permute-start | bytes 430088 | tf_op jit(solution)/shard_map/ppermute | solution.py:828
  40.2 12.0 %collective-permute-start.30 = (bf16[2,28,1280]{2,1,0:T(8,128)(2,1)}, bf16[2,28,1280]{2,1,0:T(8,128)(2,1)S(1)}, u32[]{:S(2)}, u32[]{:S(2)}) collective-permute-start(bf16[2,28,1280]{2,1,0:T(8,128)(2,1)} %get-tuple-element.161), channel_id=1, source_target_pairs={{0,28},{4,24},{8,20},{12,16},{16,12},{20,8},{24,4},{28,0},{1,29},{... | collective-permute-start | bytes 430088 | tf_op jit(solution)/shard_map/ppermute | solution.py:828
  40.7 14.1 %collective-permute-start.25 = (bf16[2,28,1280]{2,1,0:T(8,128)(2,1)}, bf16[2,28,1280]{2,1,0:T(8,128)(2,1)S(1)}, u32[]{:S(2)}, u32[]{:S(2)}) collective-permute-start(bf16[2,28,1280]{2,1,0:T(8,128)(2,1)} %get-tuple-element.151), channel_id=1, source_target_pairs={{0,8},{4,20},{8,0},{12,28},{16,24},{20,4},{24,16},{28,12},{1,9},{5... | collective-permute-start | bytes 430088 | tf_op jit(solution)/shard_map/ppermute | solution.py:828
  41.3 15.3 %collective-permute-start.26 = (bf16[2,28,1280]{2,1,0:T(8,128)(2,1)}, bf16[2,28,1280]{2,1,0:T(8,128)(2,1)S(1)}, u32[]{:S(2)}, u32[]{:S(2)}) collective-permute-start(bf16[2,28,1280]{2,1,0:T(8,128)(2,1)} %get-tuple-element.153), channel_id=1, source_target_pairs={{0,24},{4,28},{8,16},{12,20},{16,8},{20,12},{24,0},{28,4},{1,25},{... | collective-permute-start | bytes 430088 | tf_op jit(solution)/shard_map/ppermute | solution.py:828
  47.7 8.9 %collective-permute-start.27 = (bf16[2,28,1280]{2,1,0:T(8,128)(2,1)}, bf16[2,28,1280]{2,1,0:T(8,128)(2,1)S(1)}, u32[]{:S(2)}, u32[]{:S(2)}) collective-permute-start(bf16[2,28,1280]{2,1,0:T(8,128)(2,1)} %get-tuple-element.155), channel_id=1, source_target_pairs={{0,4},{4,0},{8,12},{12,8},{16,20},{20,16},{24,28},{28,24},{1,5},{5... | collective-permute-start | bytes 430088 | tf_op jit(solution)/shard_map/ppermute | solution.py:828
  52.2 7.0 %collective-permute-start.28 = (bf16[2,28,1280]{2,1,0:T(8,128)(2,1)}, bf16[2,28,1280]{2,1,0:T(8,128)(2,1)S(1)}, u32[]{:S(2)}, u32[]{:S(2)}) collective-permute-start(bf16[2,28,1280]{2,1,0:T(8,128)(2,1)} %get-tuple-element.157), channel_id=1, source_target_pairs={{0,12},{4,16},{8,4},{12,24},{16,28},{20,0},{24,20},{28,8},{1,13},{... | collective-permute-start | bytes 430088 | tf_op jit(solution)/shard_map/ppermute | solution.py:828
  63.4 133.4 %all-gather.9.cloned.1.call-start = ((), (), s32[]{:S(2)}) async-start(), calls=%async_computation.7 | async-start | bytes 2867200 | tf_op jit(solution)/shard_map/all_gather | solution.py:1068
  63.4 14.9 %collective-permute-start.4 = (bf16[2,128,2048]{2,1,0:T(8,128)(2,1)S(1)}, bf16[2,128,2048]{2,1,0:T(8,128)(2,1)S(1)}, u32[]{:S(2)}, u32[]{:S(2)}) collective-permute-start(bf16[2,128,2048]{2,1,0:T(8,128)(2,1)S(1)} %pad_maximum_fusion.4.refs_5_.refs_22_.refs_7_.refs_1_.refs_9_), channel_id=1, source_target_pairs={{0,16},{4,12},{8,24},{12,4},{16,0},{20,28},{24,8},{28,20},{1,17},{... | collective-permute-start | bytes 3145736 | tf_op jit(solution)/shard_map/ppermute | solution.py:828
  67.4 13.8 %collective-permute-start.5 = (bf16[2,128,2048]{2,1,0:T(8,128)(2,1)S(1)}, bf16[2,128,2048]{2,1,0:T(8,128)(2,1)S(1)}, u32[]{:S(2)}, u32[]{:S(2)}) collective-permute-start(bf16[2,128,2048]{2,1,0:T(8,128)(2,1)S(1)} %pad_maximum_fusion.4.refs_5_.refs_22_.refs_7_.refs_1_.refs_9_), channel_id=1, source_target_pairs={{0,4},{4,0},{8,12},{12,8},{16,20},{20,16},{24,28},{28,24},{1,5},{5... | collective-permute-start | bytes 3145736 | tf_op jit(solution)/shard_map/ppermute | solution.py:828
  91.6 10.4 %collective-permute-start.10 = (bf16[160,384]{1,0:T(8,128)(2,1)}, bf16[160,384]{1,0:T(8,128)(2,1)S(1)}, u32[]{:S(2)}, u32[]{:S(2)}) collective-permute-start(bf16[160,384]{1,0:T(8,128)(2,1)} %get-tuple-element.140.refs_1_.refs_9_.refs_13_.refs_5_), channel_id=1, source_target_pairs={{0,4},{4,0},{8,12},{12,8},{16,20},{20,16},{24,28},{28,24},{1,5},{5... | collective-permute-start | bytes 368648 | tf_op jit(solution)/shard_map/ppermute | solution.py:828
  114.6 12.0 %collective-permute-start.16 = (bf16[160,896]{1,0:T(8,128)(2,1)}, bf16[160,896]{1,0:T(8,128)(2,1)S(1)}, u32[]{:S(2)}, u32[]{:S(2)}) collective-permute-start(bf16[160,896]{1,0:T(8,128)(2,1)} %get-tuple-element.144.refs_0_), channel_id=1, source_target_pairs={{0,24},{4,28},{8,16},{12,20},{16,8},{20,12},{24,0},{28,4},{1,25},{... | collective-permute-start | bytes 860168 | tf_op jit(solution)/shard_map/ppermute | solution.py:828
  116.4 14.7 %collective-permute-start.15 = (bf16[160,896]{1,0:T(8,128)(2,1)}, bf16[160,896]{1,0:T(8,128)(2,1)S(1)}, u32[]{:S(2)}, u32[]{:S(2)}) collective-permute-start(bf16[160,896]{1,0:T(8,128)(2,1)} %get-tuple-element.144.refs_0_), channel_id=1, source_target_pairs={{0,8},{4,20},{8,0},{12,28},{16,24},{20,4},{24,16},{28,12},{1,9},{5... | collective-permute-start | bytes 860168 | tf_op jit(solution)/shard_map/ppermute | solution.py:828
  117.5 13.6 %collective-permute-start.14 = (bf16[160,896]{1,0:T(8,128)(2,1)}, bf16[160,896]{1,0:T(8,128)(2,1)S(1)}, u32[]{:S(2)}, u32[]{:S(2)}) collective-permute-start(bf16[160,896]{1,0:T(8,128)(2,1)} %get-tuple-element.144.refs_0_), channel_id=1, source_target_pairs={{0,16},{4,12},{8,24},{12,4},{16,0},{20,28},{24,8},{28,20},{1,17},{... | collective-permute-start | bytes 860168 | tf_op jit(solution)/shard_map/ppermute | solution.py:828
  118.2 8.4 %collective-permute-start.23 = (bf16[32,2048]{1,0:T(8,128)(2,1)S(1)}, bf16[32,2048]{1,0:T(8,128)(2,1)S(1)}, u32[]{:S(2)}, u32[]{:S(2)}) collective-permute-start(bf16[32,2048]{1,0:T(8,128)(2,1)S(1)} %fusion.42), channel_id=1, source_target_pairs={{0,3},{1,2},{2,1},{3,0},{4,7},{5,6},{6,5},{7,4},{8,11},{9,10},{10,... | collective-permute-start | bytes 393224 | tf_op jit(solution)/shard_map/ppermute | solution.py:833
  120.8 9.9 %collective-permute-start.22 = (bf16[32,2048]{1,0:T(8,128)(2,1)S(1)}, bf16[32,2048]{1,0:T(8,128)(2,1)S(1)}, u32[]{:S(2)}, u32[]{:S(2)}) collective-permute-start(bf16[32,2048]{1,0:T(8,128)(2,1)S(1)} %fusion.42), channel_id=1, source_target_pairs={{0,2},{1,3},{2,0},{3,1},{4,6},{5,7},{6,4},{7,5},{8,10},{9,11},{10,... | collective-permute-start | bytes 393224 | tf_op jit(solution)/shard_map/ppermute | solution.py:833
  144.6 11.1 %collective-permute-start.31 = (bf16[640,896]{1,0:T(8,128)(2,1)}, bf16[640,896]{1,0:T(8,128)(2,1)S(1)}, u32[]{:S(2)}, u32[]{:S(2)}) collective-permute-start(bf16[640,896]{1,0:T(8,128)(2,1)} %get-tuple-element.167), channel_id=1, source_target_pairs={{0,4},{4,0},{8,12},{12,8},{16,20},{20,16},{24,28},{28,24},{1,5},{5... | collective-permute-start | bytes 3440648 | tf_op jit(solution)/shard_map/ppermute | solution.py:828
  144.8 86.9 %all-gather.11.cloned.1.call-start = ((), (), s32[]{:S(2)}) async-start(), calls=%async_computation.8 | async-start | bytes 1361920 | tf_op jit(solution)/shard_map/all_gather | solution.py:1081
  144.9 9.2 %collective-permute-start.34 = (bf16[1,128,2048]{2,1,0:T(8,128)(2,1)S(1)}, bf16[1,128,2048]{2,1,0:T(8,128)(2,1)S(1)}, u32[]{:S(2)}, u32[]{:S(2)}) collective-permute-start(bf16[1,128,2048]{2,1,0:T(8,128)(2,1)S(1)} %maximum_bitcast_fusion), channel_id=1, source_target_pairs={{0,8},{4,20},{8,0},{12,28},{16,24},{20,4},{24,16},{28,12},{1,9},{5... | collective-permute-start | bytes 1572872 | tf_op jit(solution)/shard_map/ppermute | solution.py:828
  154.2 21.0 %collective-permute-start.35 = (bf16[2,128,2048]{2,1,0:T(8,128)(2,1)S(1)}, bf16[2,128,2048]{2,1,0:T(8,128)(2,1)S(1)}, u32[]{:S(2)}, u32[]{:S(2)}) collective-permute-start(bf16[2,128,2048]{2,1,0:T(8,128)(2,1)S(1)} %pad_maximum_fusion.5.refs_6_.refs_22_.refs_7_.refs_1_.refs_9_), channel_id=1, source_target_pairs={{0,16},{4,12},{8,24},{12,4},{16,0},{20,28},{24,8},{28,20},{1,17},{... | collective-permute-start | bytes 3145736 | tf_op jit(solution)/shard_map/ppermute | solution.py:828
  156.0 16.0 %collective-permute-start.32 = (bf16[2,160,896]{2,1,0:T(8,128)(2,1)S(1)}, bf16[2,160,896]{2,1,0:T(8,128)(2,1)S(1)}, u32[]{:S(2)}, u32[]{:S(2)}) collective-permute-start(bf16[2,160,896]{2,1,0:T(8,128)(2,1)S(1)} %bitcast.149), channel_id=1, source_target_pairs={{0,8},{4,20},{8,0},{12,28},{16,24},{20,4},{24,16},{28,12},{1,9},{5... | collective-permute-start | bytes 1720328 | tf_op jit(solution)/shard_map/ppermute | solution.py:828
  156.9 20.1 %collective-permute-start.36 = (bf16[2,128,2048]{2,1,0:T(8,128)(2,1)S(1)}, bf16[2,128,2048]{2,1,0:T(8,128)(2,1)S(1)}, u32[]{:S(2)}, u32[]{:S(2)}) collective-permute-start(bf16[2,128,2048]{2,1,0:T(8,128)(2,1)S(1)} %pad_maximum_fusion.5.refs_6_.refs_22_.refs_7_.refs_1_.refs_9_), channel_id=1, source_target_pairs={{0,4},{4,0},{8,12},{12,8},{16,20},{20,16},{24,28},{28,24},{1,5},{5... | collective-permute-start | bytes 3145736 | tf_op jit(solution)/shard_map/ppermute | solution.py:828
  196.8 110.8 %reduce-scatter.9.cloned.1.call-start = ((), (), s32[]{:S(2)}) async-start(), calls=%async_computation.9 | async-start | bytes 2867200 | tf_op jit(solution)/shard_map/reduce_scatter | solution.py:1093
  196.9 18.0 %collective-permute-start.54 = (bf16[160,896]{1,0:T(8,128)(2,1)S(1)}, bf16[160,896]{1,0:T(8,128)(2,1)S(1)}, u32[]{:S(2)}, u32[]{:S(2)}) collective-permute-start(bf16[160,896]{1,0:T(8,128)(2,1)S(1)} %bitcast.158), channel_id=1, source_target_pairs={{0,24},{4,28},{8,16},{12,20},{16,8},{20,12},{24,0},{28,4},{1,25},{... | collective-permute-start | bytes 860168 | tf_op jit(solution)/shard_map/ppermute | solution.py:828
  198.4 14.2 %collective-permute-start.53 = (bf16[160,896]{1,0:T(8,128)(2,1)S(1)}, bf16[160,896]{1,0:T(8,128)(2,1)S(1)}, u32[]{:S(2)}, u32[]{:S(2)}) collective-permute-start(bf16[160,896]{1,0:T(8,128)(2,1)S(1)} %bitcast.159), channel_id=1, source_target_pairs={{0,8},{4,20},{8,0},{12,28},{16,24},{20,4},{24,16},{28,12},{1,9},{5... | collective-permute-start | bytes 860168 | tf_op jit(solution)/shard_map/ppermute | solution.py:828
  199.6 13.4 %collective-permute-start.52 = (bf16[160,896]{1,0:T(8,128)(2,1)S(1)}, bf16[160,896]{1,0:T(8,128)(2,1)S(1)}, u32[]{:S(2)}, u32[]{:S(2)}) collective-permute-start(bf16[160,896]{1,0:T(8,128)(2,1)S(1)} %bitcast.160), channel_id=1, source_target_pairs={{0,16},{4,12},{8,24},{12,4},{16,0},{20,28},{24,8},{28,20},{1,17},{... | collective-permute-start | bytes 860168 | tf_op jit(solution)/shard_map/ppermute | solution.py:828
  213.5 10.8 %collective-permute-start.47 = (bf16[160,896]{1,0:T(8,128)(2,1)}, bf16[160,896]{1,0:T(8,128)(2,1)S(1)}, u32[]{:S(2)}, u32[]{:S(2)}) collective-permute-start(bf16[160,896]{1,0:T(8,128)(2,1)} %get-tuple-element.180.refs_0_), channel_id=1, source_target_pairs={{0,24},{4,28},{8,16},{12,20},{16,8},{20,12},{24,0},{28,4},{1,25},{... | collective-permute-start | bytes 860168 | tf_op jit(solution)/shard_map/ppermute | solution.py:828
  214.9 14.5 %collective-permute-start.46 = (bf16[160,896]{1,0:T(8,128)(2,1)}, bf16[160,896]{1,0:T(8,128)(2,1)S(1)}, u32[]{:S(2)}, u32[]{:S(2)}) collective-permute-start(bf16[160,896]{1,0:T(8,128)(2,1)} %get-tuple-element.180.refs_0_), channel_id=1, source_target_pairs={{0,8},{4,20},{8,0},{12,28},{16,24},{20,4},{24,16},{28,12},{1,9},{5... | collective-permute-start | bytes 860168 | tf_op jit(solution)/shard_map/ppermute | solution.py:828
  216.1 13.7 %collective-permute-start.45 = (bf16[160,896]{1,0:T(8,128)(2,1)}, bf16[160,896]{1,0:T(8,128)(2,1)S(1)}, u32[]{:S(2)}, u32[]{:S(2)}) collective-permute-start(bf16[160,896]{1,0:T(8,128)(2,1)} %get-tuple-element.180.refs_0_), channel_id=1, source_target_pairs={{0,16},{4,12},{8,24},{12,4},{16,0},{20,28},{24,8},{28,20},{1,17},{... | collective-permute-start | bytes 860168 | tf_op jit(solution)/shard_map/ppermute | solution.py:828
  217.0 12.9 %collective-permute-start.48 = (bf16[160,896]{1,0:T(8,128)(2,1)}, bf16[160,896]{1,0:T(8,128)(2,1)S(1)}, u32[]{:S(2)}, u32[]{:S(2)}) collective-permute-start(bf16[160,896]{1,0:T(8,128)(2,1)} %get-tuple-element.180.refs_0_), channel_id=1, source_target_pairs={{0,4},{4,0},{8,12},{12,8},{16,20},{20,16},{24,28},{28,24},{1,5},{5... | collective-permute-start | bytes 860168 | tf_op jit(solution)/shard_map/ppermute | solution.py:828
  217.0 12.9 %collective-permute-start.58 = (bf16[160,896]{1,0:T(8,128)(2,1)S(1)}, bf16[160,896]{1,0:T(8,128)(2,1)S(1)}, u32[]{:S(2)}, u32[]{:S(2)}) collective-permute-start(bf16[160,896]{1,0:T(8,128)(2,1)S(1)} %collective-permute-done.54.refs_11_), channel_id=1, source_target_pairs={{0,4},{4,0},{8,12},{12,8},{16,20},{20,16},{24,28},{28,24},{1,5},{5... | collective-permute-start | bytes 860168 | tf_op jit(solution)/shard_map/ppermute | solution.py:828
  258.6 75.9 %reduce-scatter.13.cloned.1.call-start = ((), (), s32[]{:S(2)}) async-start(), calls=%async_computation.11 | async-start | bytes 1361920
  259.0 9.8 %collective-permute-start.60 = (bf16[2,160,896]{2,1,0:T(8,128)(2,1)S(1)}, bf16[2,160,896]{2,1,0:T(8,128)(2,1)S(1)}, u32[]{:S(2)}, u32[]{:S(2)}) collective-permute-start(bf16[2,160,896]{2,1,0:T(8,128)(2,1)S(1)} %bitcast.148), channel_id=1, source_target_pairs={{0,8},{4,20},{8,0},{12,28},{16,24},{20,4},{24,16},{28,12},{1,9},{5... | collective-permute-start | bytes 1720328 | tf_op jit(solution)/shard_map/ppermute | solution.py:828
  298.9 123.3 %reduce-scatter.11.cloned.1.call-start = ((), (), s32[]{:S(2)}) async-start(), calls=%async_computation.10 | async-start | bytes 2867200 | tf_op jit(solution)/shard_map/reduce_scatter | solution.py:1093
  314.4 8.3 %collective-permute-start.74 = (bf16[512,896]{1,0:T(8,128)(2,1)S(1)}, bf16[512,896]{1,0:T(8,128)(2,1)S(1)}, u32[]{:S(2)}, u32[]{:S(2)}) collective-permute-start(bf16[512,896]{1,0:T(8,128)(2,1)S(1)} %convolution_convert_fusion.6), channel_id=1, source_target_pairs={{0,4},{4,0},{8,12},{12,8},{16,20},{20,16},{24,28},{28,24},{1,5},{5... | collective-permute-start | bytes 2752520 | tf_op jit(solution)/shard_map/ppermute | solution.py:828
  317.5 10.8 %collective-permute-start.69 = (bf16[160,896]{1,0:T(8,128)(2,1)}, bf16[160,896]{1,0:T(8,128)(2,1)S(1)}, u32[]{:S(2)}, u32[]{:S(2)}) collective-permute-start(bf16[160,896]{1,0:T(8,128)(2,1)} %get-tuple-element.212.refs_1_), channel_id=1, source_target_pairs={{0,24},{4,28},{8,16},{12,20},{16,8},{20,12},{24,0},{28,4},{1,25},{... | collective-permute-start | bytes 860168 | tf_op jit(solution)/shard_map/ppermute | solution.py:828
  318.9 15.6 %collective-permute-start.68 = (bf16[160,896]{1,0:T(8,128)(2,1)}, bf16[160,896]{1,0:T(8,128)(2,1)}, u32[]{:S(2)}, u32[]{:S(2)}) collective-permute-start(bf16[160,896]{1,0:T(8,128)(2,1)} %get-tuple-element.212.refs_1_), channel_id=1, source_target_pairs={{0,8},{4,20},{8,0},{12,28},{16,24},{20,4},{24,16},{28,12},{1,9},{5... | collective-permute-start | bytes 860168 | tf_op jit(solution)/shard_map/ppermute | solution.py:828
  322.2 12.8 %collective-permute-start.65 = (bf16[640,896]{1,0:T(8,128)(2,1)}, bf16[640,896]{1,0:T(8,128)(2,1)}, u32[]{:S(2)}, u32[]{:S(2)}) collective-permute-start(bf16[640,896]{1,0:T(8,128)(2,1)} %convolution_convert_fusion.2), channel_id=1, source_target_pairs={{0,4},{4,0},{8,12},{12,8},{16,20},{20,16},{24,28},{28,24},{1,5},{5... | collective-permute-start | bytes 3440648 | tf_op jit(solution)/shard_map/ppermute | solution.py:828
  322.7 11.8 %collective-permute-start.67 = (bf16[160,896]{1,0:T(8,128)(2,1)}, bf16[160,896]{1,0:T(8,128)(2,1)}, u32[]{:S(2)}, u32[]{:S(2)}) collective-permute-start(bf16[160,896]{1,0:T(8,128)(2,1)} %get-tuple-element.212.refs_1_), channel_id=1, source_target_pairs={{0,16},{4,12},{8,24},{12,4},{16,0},{20,28},{24,8},{28,20},{1,17},{... | collective-permute-start | bytes 860168 | tf_op jit(solution)/shard_map/ppermute | solution.py:828
  326.5 26.9 %collective-permute-start.76 = (bf16[2,128,2048]{2,1,0:T(8,128)(2,1)}, bf16[2,128,2048]{2,1,0:T(8,128)(2,1)S(1)}, u32[]{:S(2)}, u32[]{:S(2)}) collective-permute-start(bf16[2,128,2048]{2,1,0:T(8,128)(2,1)} %fusion.10), channel_id=1, source_target_pairs={{0,8},{4,20},{8,0},{12,28},{16,24},{20,4},{24,16},{28,12},{1,9},{5... | collective-permute-start | bytes 3145736 | tf_op jit(solution)/shard_map/ppermute | solution.py:828
  328.3 12.8 %collective-permute-start.70 = (bf16[160,896]{1,0:T(8,128)(2,1)}, bf16[160,896]{1,0:T(8,128)(2,1)}, u32[]{:S(2)}, u32[]{:S(2)}) collective-permute-start(bf16[160,896]{1,0:T(8,128)(2,1)} %get-tuple-element.212.refs_1_), channel_id=1, source_target_pairs={{0,4},{4,0},{8,12},{12,8},{16,20},{20,16},{24,28},{28,24},{1,5},{5... | collective-permute-start | bytes 860168 | tf_op jit(solution)/shard_map/ppermute | solution.py:828
  339.5 13.9 %collective-permute-start.66 = (bf16[2,160,896]{2,1,0:T(8,128)(2,1)S(1)}, bf16[2,160,896]{2,1,0:T(8,128)(2,1)S(1)}, u32[]{:S(2)}, u32[]{:S(2)}) collective-permute-start(bf16[2,160,896]{2,1,0:T(8,128)(2,1)S(1)} %bitcast.146), channel_id=1, source_target_pairs={{0,8},{4,20},{8,0},{12,28},{16,24},{20,4},{24,16},{28,12},{1,9},{5... | collective-permute-start | bytes 1720328 | tf_op jit(solution)/shard_map/ppermute | solution.py:828
  364.9 90.8 %reduce-scatter.15.cloned.1.call-start = ((), (), s32[]{:S(2)}) async-start(), calls=%async_computation.12 | async-start | bytes 1361920
  364.9 9.8 %collective-permute-start.78 = (bf16[2,160,896]{2,1,0:T(8,128)(2,1)S(1)}, bf16[2,160,896]{2,1,0:T(8,128)(2,1)S(1)}, u32[]{:S(2)}, u32[]{:S(2)}) collective-permute-start(bf16[2,160,896]{2,1,0:T(8,128)(2,1)S(1)} %bitcast.147), channel_id=1, source_target_pairs={{0,8},{4,20},{8,0},{12,28},{16,24},{20,4},{24,16},{28,12},{1,9},{5... | collective-permute-start | bytes 1720328 | tf_op jit(solution)/shard_map/ppermute | solution.py:828
  391.5 15.8 %collective-permute-start.81 = (bf16[1,128,2048]{2,1,0:T(8,128)(2,1)S(1)}, bf16[1,128,2048]{2,1,0:T(8,128)(2,1)S(1)}, u32[]{:S(2)}, u32[]{:S(2)}) collective-permute-start(bf16[1,128,2048]{2,1,0:T(8,128)(2,1)S(1)} %slice.584), channel_id=1, source_target_pairs={{0,16},{4,12},{8,24},{12,4},{16,0},{20,28},{24,8},{28,20},{1,17},{... | collective-permute-start | bytes 1572872 | tf_op jit(solution)/shard_map/ppermute | solution.py:828
  394.1 13.1 %collective-permute-start.80 = (bf16[1,160,896]{2,1,0:T(8,128)(2,1)S(1)}, bf16[1,160,896]{2,1,0:T(8,128)(2,1)S(1)}, u32[]{:S(2)}, u32[]{:S(2)}) collective-permute-start(bf16[1,160,896]{2,1,0:T(8,128)(2,1)S(1)} %slice.585), channel_id=1, source_target_pairs={{0,16},{4,12},{8,24},{12,4},{16,0},{20,28},{24,8},{28,20},{1,17},{... | collective-permute-start | bytes 860168 | tf_op jit(solution)/shard_map/ppermute | solution.py:828
  410.0 7.5 %collective-permute-start.83 = (bf16[2,160,256]{2,1,0:T(8,128)(2,1)S(1)}, bf16[2,160,256]{2,1,0:T(8,128)(2,1)S(1)}, u32[]{:S(2)}, u32[]{:S(2)}) collective-permute-start(bf16[2,160,256]{2,1,0:T(8,128)(2,1)S(1)} %bitcast.170), channel_id=1, source_target_pairs={{0,8},{4,20},{8,0},{12,28},{16,24},{20,4},{24,16},{28,12},{1,9},{5... | collective-permute-start | bytes 491528 | tf_op jit(solution)/shard_map/ppermute | solution.py:828
  412.3 19.3 %collective-permute-start.85 = (bf16[512,896]{1,0:T(8,128)(2,1)}, bf16[512,896]{1,0:T(8,128)(2,1)}, u32[]{:S(2)}, u32[]{:S(2)}) collective-permute-start(bf16[512,896]{1,0:T(8,128)(2,1)} %select_convert_fusion.1), channel_id=1, source_target_pairs={{0,4},{4,0},{8,12},{12,8},{16,20},{20,16},{24,28},{28,24},{1,5},{5... | collective-permute-start | bytes 2752520 | tf_op jit(solution)/shard_map/ppermute | solution.py:828
  420.3 9.9 %collective-permute-start.86 = (bf16[512,896]{1,0:T(8,128)(2,1)S(1)}, bf16[512,896]{1,0:T(8,128)(2,1)}, u32[]{:S(2)}, u32[]{:S(2)}) collective-permute-start(bf16[512,896]{1,0:T(8,128)(2,1)S(1)} %convolution_convert_fusion.5), channel_id=1, source_target_pairs={{0,4},{4,0},{8,12},{12,8},{16,20},{20,16},{24,28},{28,24},{1,5},{5... | collective-permute-start | bytes 2752520 | tf_op jit(solution)/shard_map/ppermute | solution.py:828
  434.5 17.4 %collective-permute-start.87 = (bf16[2,128,1792]{2,1,0:T(8,128)(2,1)}, bf16[2,128,1792]{2,1,0:T(8,128)(2,1)}, u32[]{:S(2)}, u32[]{:S(2)}) collective-permute-start(bf16[2,128,1792]{2,1,0:T(8,128)(2,1)} %fusion.14), channel_id=1, source_target_pairs={{0,8},{4,20},{8,0},{12,28},{16,24},{20,4},{24,16},{28,12},{1,9},{5... | collective-permute-start | bytes 2752520 | tf_op jit(solution)/shard_map/ppermute | solution.py:828
  436.6 13.6 %collective-permute-start.89 = (bf16[2,128,384]{2,1,0:T(8,128)(2,1)}, bf16[2,128,384]{2,1,0:T(8,128)(2,1)S(1)}, u32[]{:S(2)}, u32[]{:S(2)}) collective-permute-start(bf16[2,128,384]{2,1,0:T(8,128)(2,1)} %bitcast.168), channel_id=1, source_target_pairs={{0,8},{4,20},{8,0},{12,28},{16,24},{20,4},{24,16},{28,12},{1,9},{5... | collective-permute-start | bytes 589832 | tf_op jit(solution)/shard_map/ppermute | solution.py:828
  438.5 57.5 %collective-permute-start.94 = (bf16[32,2048]{1,0:T(8,128)(2,1)}, bf16[32,2048]{1,0:T(8,128)(2,1)}, u32[]{:S(2)}, u32[]{:S(2)}) collective-permute-start(bf16[32,2048]{1,0:T(8,128)(2,1)} %get-tuple-element.310), channel_id=1, source_target_pairs={{0,1},{1,0},{2,3},{3,2},{4,5},{5,4},{6,7},{7,6},{8,9},{9,8},{10,11... | collective-permute-start | bytes 393224 | tf_op jit(solution)/shard_map/ppermute | solution.py:833
  439.1 52.4 %collective-permute-start.96 = (bf16[32,2048]{1,0:T(8,128)(2,1)}, bf16[32,2048]{1,0:T(8,128)(2,1)}, u32[]{:S(2)}, u32[]{:S(2)}) collective-permute-start(bf16[32,2048]{1,0:T(8,128)(2,1)} %get-tuple-element.311), channel_id=1, source_target_pairs={{0,3},{1,2},{2,1},{3,0},{4,7},{5,6},{6,5},{7,4},{8,11},{9,10},{10,... | collective-permute-start | bytes 393224 | tf_op jit(solution)/shard_map/ppermute | solution.py:833
  455.6 11.2 %collective-permute-start.90 = (bf16[1,128,2176]{2,1,0:T(8,128)(2,1)}, bf16[1,128,2176]{2,1,0:T(8,128)(2,1)}, u32[]{:S(2)}, u32[]{:S(2)}) collective-permute-start(bf16[1,128,2176]{2,1,0:T(8,128)(2,1)} %fusion.20), channel_id=1, source_target_pairs={{0,16},{4,12},{8,24},{12,4},{16,0},{20,28},{24,8},{28,20},{1,17},{... | collective-permute-start | bytes 1671176 | tf_op jit(solution)/shard_map/ppermute | solution.py:828
  463.0 20.2 %all-to-all-start = ((bf16[8,2,28,1280]{3,1,2,0:T(2,128)(2,1)}), bf16[8,2,28,1280]{3,1,2,0:T(2,128)(2,1)S(1)}, u32[]{:S(2)}, u32[]{:S(2)}) async-start(bf16[8,2,28,1280]{3,1,2,0:T(2,128)(2,1)} %copy.102), calls=%async_computation.2 | async-start | bytes 2293760 | tf_op jit(solution)/shard_map/all_to_all | solution.py:962
  468.8 19.9 %collective-permute-start.91 = (bf16[32,2176]{1,0:T(8,128)(2,1)}, bf16[32,2176]{1,0:T(8,128)(2,1)S(1)}, u32[]{:S(2)}, u32[]{:S(2)}) collective-permute-start(bf16[32,2176]{1,0:T(8,128)(2,1)} %get-tuple-element.305), channel_id=1, source_target_pairs={{0,1},{1,0},{2,3},{3,2},{4,5},{5,4},{6,7},{7,6},{8,9},{9,8},{10,11... | collective-permute-start | bytes 417800 | tf_op jit(solution)/shard_map/ppermute | solution.py:833
  469.3 21.1 %collective-permute-start.93 = (bf16[32,2176]{1,0:T(8,128)(2,1)S(1)}, bf16[32,2176]{1,0:T(8,128)(2,1)S(1)}, u32[]{:S(2)}, u32[]{:S(2)}) collective-permute-start(bf16[32,2176]{1,0:T(8,128)(2,1)S(1)} %get-tuple-element.306), channel_id=1, source_target_pairs={{0,3},{1,2},{2,1},{3,0},{4,7},{5,6},{6,5},{7,4},{8,11},{9,10},{10,... | collective-permute-start | bytes 417800 | tf_op jit(solution)/shard_map/ppermute | solution.py:833
  472.0 18.4 %collective-permute-start.92 = (bf16[32,2176]{1,0:T(8,128)(2,1)S(1)}, bf16[32,2176]{1,0:T(8,128)(2,1)}, u32[]{:S(2)}, u32[]{:S(2)}) collective-permute-start(bf16[32,2176]{1,0:T(8,128)(2,1)S(1)} %get-tuple-element.307), channel_id=1, source_target_pairs={{0,2},{1,3},{2,0},{3,1},{4,6},{5,7},{6,4},{7,5},{8,10},{9,11},{10,... | collective-permute-start | bytes 417800 | tf_op jit(solution)/shard_map/ppermute | solution.py:833
  488.6 7.3 %collective-permute-start.95 = (bf16[32,2048]{1,0:T(8,128)(2,1)S(1)}, bf16[32,2048]{1,0:T(8,128)(2,1)S(1)}, u32[]{:S(2)}, u32[]{:S(2)}) collective-permute-start(bf16[32,2048]{1,0:T(8,128)(2,1)S(1)} %copy-done.66), channel_id=1, source_target_pairs={{0,2},{1,3},{2,0},{3,1},{4,6},{5,7},{6,4},{7,5},{8,10},{9,11},{10,... | collective-permute-start | bytes 393224 | tf_op jit(solution)/shard_map/ppermute | solution.py:833
  (175 other events, 920.4 us)
Sparse Core Ops, SparseCore 0:
  32.6 28.7 all-gather.4
  63.6 49.7 all-gather.6
  144.9 48.3 all-gather.8
  197.0 27.4 all-gather.10
  258.7 45.8 reduce-scatter.8
  307.5 26.9 reduce-scatter.12
  365.0 45.6 reduce-scatter.10
  413.6 26.9 reduce-scatter.14
